TPU v7x, 32 devices: a whole 2x2x4 slice. The times are simulated.
32 devices in a mesh: ctx: 16 (over z, y, core), head: 2 (over x).
Axes of the slice: x: 2, y: 2, z: 4, core: 2. Of those that a mesh axis runs over, the one named last changes fastest.
Arguments:
- key_rows: bfloat16 [16384, 2560], P('ctx', 'head'), may hold values from -6 to 6
- value_rows: bfloat16 [16384, 2560], P('ctx', 'head'), may hold values from -6 to 6
- query_rows: bfloat16 [16384, 2560], P('ctx', 'head'), may hold values from -6 to 6
- learn_rates: float32 [4, 16384], P('head', 'ctx'), may hold values from 5e-05 to 0.0005
- fast_in: bfloat16 [4, 640, 640], P('head'), may hold values from -0.25 to 0.25
- fast_gate: bfloat16 [4, 640, 640], P('head'), may hold values from -0.25 to 0.25
- fast_out: bfloat16 [4, 640, 640], P('head'), may hold values from -0.25 to 0.25
- head_gain: float32 [2560], P('head'), may hold values from 0.1 to 1.9
- out_proj: bfloat16 [2560, 2560], P('head', 'ctx'), may hold values from -0.15625 to 0.15625
Outputs:
- output: bfloat16 [16384, 2560], P('ctx', 'head')
- new_in: bfloat16 [4, 640, 640], P('head')
- new_gate: bfloat16 [4, 640, 640], P('head')
- new_out: bfloat16 [4, 640, 640], P('head')
All inputs are finite; a program needn't handle non-finite values.
Results may differ from a plain program's by a relative error of at most 0.012.
Values may be sent and summed in bfloat16 or wider, within the bound.
No kernel may reach another device: no remote copies, remote signals or barrier semaphores. Data moves between devices by JAX's collectives and lax.ppermute only.
A program may use at most 128 MiB of HBM per device.

v0:
```python
import jax
import jax.numpy as jnp
from jax import lax
from jax.sharding import PartitionSpec as P


def renorm(weight, grad):
    wide = weight.astype(jnp.float32)
    moved = wide - grad
    scale = jnp.sqrt(jnp.sum(wide * wide, axis=1, keepdims=True) + 1e-06) / jnp.sqrt(
        jnp.sum(moved * moved, axis=1, keepdims=True) + 1e-06
    )
    return (moved * scale).astype(jnp.bfloat16)


def on_device(
    key_rows, value_rows, query_rows, learn_rates, fast_in, fast_gate, fast_out, head_gain, out_proj
):
    tok_count = key_rows.shape[0]
    local_heads = fast_in.shape[0]
    head_width = fast_in.shape[1]
    keyed = key_rows.reshape(tok_count, local_heads, head_width)
    valued = value_rows.reshape(tok_count, local_heads, head_width)
    queried = query_rows.reshape(tok_count, local_heads, head_width)
    pre_in = jnp.einsum("thd,hdf->thf", keyed, fast_in, preferred_element_type=jnp.float32)
    pre_gate = jnp.einsum("thd,hdf->thf", keyed, fast_gate, preferred_element_type=jnp.float32)
    sig = jax.nn.sigmoid(pre_in)
    act = pre_in * sig
    hidden = (act * pre_gate).astype(jnp.bfloat16)
    rate_cols = learn_rates.T[:, :, None]
    err = (-rate_cols * valued.astype(jnp.float32)).astype(jnp.bfloat16)
    grad_out = jnp.einsum("thf,thd->hfd", hidden, err, preferred_element_type=jnp.float32)
    back = jnp.einsum("thd,hfd->thf", err, fast_out, preferred_element_type=jnp.float32)
    back_in = (back * pre_gate * sig * (1.0 + pre_in * (1.0 - sig))).astype(jnp.bfloat16)
    back_gate = (back * act).astype(jnp.bfloat16)
    grad_in = jnp.einsum("thd,thf->hdf", keyed, back_in, preferred_element_type=jnp.float32)
    grad_gate = jnp.einsum("thd,thf->hdf", keyed, back_gate, preferred_element_type=jnp.float32)
    sum_in, sum_gate, sum_out = lax.psum((grad_in, grad_gate, grad_out), "ctx")
    upd_in = renorm(fast_in, sum_in)
    upd_gate = renorm(fast_gate, sum_gate)
    upd_out = renorm(fast_out, sum_out)
    q_in = jnp.einsum("thd,hdf->thf", queried, upd_in, preferred_element_type=jnp.float32)
    q_gate = jnp.einsum("thd,hdf->thf", queried, upd_gate, preferred_element_type=jnp.float32)
    q_hidden = (jax.nn.silu(q_in) * q_gate).astype(jnp.bfloat16)
    head_out = jnp.einsum("thf,hfd->thd", q_hidden, upd_out, preferred_element_type=jnp.float32)
    inverse = lax.rsqrt(jnp.mean(head_out * head_out, axis=-1, keepdims=True) + 1e-06)
    gains = head_gain.reshape(local_heads, head_width)
    normed = (
        (head_out * inverse * gains)
        .astype(jnp.bfloat16)
        .reshape(tok_count, local_heads * head_width)
    )
    partial_out = jnp.dot(
        normed,
        lax.all_gather(out_proj, "ctx", axis=1, tiled=True),
        preferred_element_type=jnp.float32,
    )
    output = lax.psum_scatter(
        partial_out.astype(jnp.bfloat16), "head", scatter_dimension=1, tiled=True
    )
    return (output, upd_in, upd_gate, upd_out)


def solution(mesh):
    return jax.shard_map(
        on_device,
        mesh=mesh,
        in_specs=(
            P("ctx", "head"),
            P("ctx", "head"),
            P("ctx", "head"),
            P("head", "ctx"),
            P("head", None, None),
            P("head", None, None),
            P("head", None, None),
            P("head"),
            P("head", "ctx"),
        ),
        out_specs=(
            P("ctx", "head"),
            P("head", None, None),
            P("head", None, None),
            P("head", None, None),
        ),
        check_vma=False,
    )
```

profile of v0, /device:TPU:0, one launch (start us, length us, event | category | flops | bytes accessed | tf_op | source)
XLA Modules:
  0.0 389.8 jit_solution(14458042487574289752)
XLA Ops:
  7.2 7.1 %fusion.27 = f32[2,640,1024]{2,1,0:T(8,128)} fusion(bf16[2,640,640]{2,1,0:T(8,128)(2,1)} %param.14, bf16[128,2,8,640]{3,2,1,0:T(8,128)(2,1)} %bitcast.129), kind=kOutput, calls=%fused_computation.50 | convolution fusion | flops 1677721600 | bytes 9502720 | tf_op jit(solution)/shard_map/thd,hdf->thf/dot_general | solution.py:26
  14.3 4.8 %fusion.29 = f32[2,640,1024]{2,1,0:T(8,128)} fusion(bf16[2,640,640]{2,1,0:T(8,128)(2,1)S(1)} %copy-done.8, bf16[128,2,8,640]{3,2,1,0:T(8,128)(2,1)S(1)} %bitcast.130), kind=kOutput, calls=%fused_computation.52 | convolution fusion | flops 1677721600 | bytes 9502720 | tf_op jit(solution)/shard_map/thd,hdf->thf/dot_general | solution.py:25
  19.8 0.7 copy-done
  20.6 2.3 fusion.50
  22.9 8.3 %fusion.20 = f32[2,640,640]{2,1,0:T(8,128)} fusion(f32[2,640,1024]{2,1,0:T(8,128)} %fusion.27, f32[2,640,1024]{2,1,0:T(8,128)} %fusion.29, f32[128,2,8,640]{3,2,1,0:T(8,128)S(1)} %bitcast.125, f32[1024,2]{0,1:T(2,128)S(1)} %negate_bitcast_fusion), kind=kOutput, calls=%fused_computation.45 | convolution fusion | flops 1688207360 | bytes 19013632 | tf_op jit(solution)/shard_map/thf,thd->hfd/dot_general | solution.py:32
  31.2 9.0 %fusion.34 = f32[2,640,640]{1,2,0:T(8,128)} fusion(f32[2,1024,640]{1,2,0:T(8,128)S(1)} %fusion.50, f32[2,640,1024]{2,1,0:T(8,128)} %fusion.27, f32[2,640,1024]{2,1,0:T(8,128)} %fusion.29, bf16[128,2,8,640]{3,2,1,0:T(8,128)(2,1)S(1)} %bitcast.131), kind=kOutput, calls=%fused_computation.55 | convolution fusion | flops 1690828800 | bytes 21626880 | tf_op jit(solution)/shard_map/thd,thf->hdf/dot_general | solution.py:36
  40.2 6.6 %fusion.39 = f32[2,640,640]{1,2,0:T(8,128)} fusion(f32[2,1024,640]{1,2,0:T(8,128)S(1)} %fusion.50, bf16[128,2,8,640]{3,2,1,0:T(8,128)(2,1)S(1)} %bitcast.132, f32[2,640,1024]{2,1,0:T(8,128)} %fusion.29), kind=kOutput, calls=%fused_computation.56 | convolution fusion | flops 1685585920 | bytes 16384000 | tf_op jit(solution)/shard_map/thd,thf->hdf/dot_general | solution.py:37
  47.6 2.2 copy.18
  49.8 2.8 copy.22
  52.6 4.6 %copy.34 = bf16[1024,1280]{0,1:T(8,128)(2,1)} copy(bf16[1024,1280]{1,0:T(8,128)(2,1)} %param.11) | data formatting | bytes 5242880 | tf_op jit(solution)/shard_map/reshape | solution.py:24
  57.2 183.8 %all-reduce.3.cloned.1.call-done = (f32[2,640,640]{2,1,0:T(8,128)}, f32[2,640,640]{1,2,0:T(8,128)}, f32[2,640,640]{1,2,0:T(8,128)}) async-done(((f32[2,640,640]{2,1,0:T(8,128)}, f32[2,640,640]{1,2,0:T(8,128)}, f32[2,640,640]{1,2,0:T(8,128)}), (f32[2,640,640]{2,1,0:T(8,128)}, f32[2,640,640]{1,2,0:T(8,128)}, f32[2,640,640]{1,2,0:T(8,128)})) %all-reduce.3.cloned.1.call-update) | async-done | bytes 9830416 | tf_op jit(solution)/shard_map/psum | solution.py:38
  241.1 2.7 fusion.17
  244.5 3.5 fusion.18
  248.1 1.7 multiply_convert_fusion.2
  249.7 0.9 copy-done.3
  251.1 1.6 multiply_convert_fusion
  253.5 4.6 %fusion.57 = f32[2,640,1024]{2,1,0:T(8,128)} fusion(bf16[2,640,640]{1,2,0:T(8,128)(2,1)S(1)} %multiply_convert_fusion.1, bf16[1024,2,640]{0,2,1:T(8,128)(2,1)S(1)} %bitcast.127), kind=kOutput, calls=%fused_computation.72 | convolution fusion | flops 1677721600 | bytes 9502720 | tf_op jit(solution)/shard_map/thd,hdf->thf/dot_general | solution.py:42
  258.1 10.7 %fusion.1 = (f32[1024,2]{0,1:T(2,128)S(1)}, f32[2,640,1024]{2,1,0:T(8,128)}) fusion(bf16[2,640,640]{2,1,0:T(8,128)(2,1)} %multiply_convert_fusion.2, f32[2,640,1024]{2,1,0:T(8,128)} %fusion.57, bf16[2,640,640]{1,2,0:T(8,128)(2,1)S(1)} %copy-done.5, bf16[1024,2,640]{0,2,1:T(8,128)(2,1)} %bitcast.126), kind=kOutput, calls=%fused_computation.5 | convolution fusion | flops 3365926912 | bytes 16392192 | tf_op jit(solution)/shard_map/thf,hfd->thd/dot_general | solution.py:45
  268.8 4.5 %fusion.3 = bf16[1024,2,640]{0,2,1:T(8,128)(2,1)} fusion(f32[2,640,1024]{2,1,0:T(8,128)} %get-tuple-element.18, f32[2,640]{1,0:T(2,128)S(1)} %mul.125, f32[1024,2]{0,1:T(2,128)S(1)} %add_rsqrt_fusion), kind=kLoop, calls=%fused_computation.7 | loop fusion | flops 3932160 | bytes 7877632 | tf_op jit(solution)/shard_map/convert_element_type | solution.py:50
  273.3 33.6 %all-gather.2.cloned.1.call-done = bf16[1280,2560]{0,1:T(8,128)(2,1)} async-done(((bf16[1280,160]{0,1:T(8,128)(2,1)}), bf16[1280,2560]{0,1:T(8,128)(2,1)}) %all-gather.2.cloned.1.call-update) | async-done | bytes 6553616 | tf_op jit(solution)/shard_map/all_gather | solution.py:55
  306.8 12.0 %convolution_convert_fusion = bf16[1024,2560]{1,0:T(8,128)(2,1)} fusion(bf16[1024,1280]{0,1:T(8,128)(2,1)} %bitcast.128, bf16[1280,2560]{0,1:T(8,128)(2,1)} %all-gather.2.cloned.1.call-done), kind=kOutput, calls=%fused_computation | convolution fusion | flops 6713507840 | bytes 14417920 | tf_op jit(solution)/shard_map/dot_general | solution.py:53
  318.9 2.2 copy.26
  321.1 2.2 copy.27
  323.2 60.0 %reduce-scatter.2.cloned.1.call-done = bf16[1024,1280]{1,0:T(8,128)(2,1)} async-done(((bf16[1024,2560]{1,0:T(8,128)(2,1)}), bf16[1024,1280]{1,0:T(8,128)(2,1)}) %reduce-scatter.2.cloned.1.call-update) | async-done | bytes 2621456 | tf_op jit(solution)/shard_map/reduce_scatter | solution.py:58
  (36 shorter events, 3.5 us)
Async XLA Ops:
  7.2 233.9 %all-reduce.3.cloned.1.call-start = ((), (), s32[]{:S(2)}) async-start(), calls=%async_computation.3 | async-start | bytes 19660800 | tf_op jit(solution)/shard_map/psum | solution.py:38
  7.2 7.1 %copy-start.8 = (bf16[2,640,640]{2,1,0:T(8,128)(2,1)S(1)}, bf16[2,640,640]{2,1,0:T(8,128)(2,1)}, u32[]{:S(2)}) copy-start(bf16[2,640,640]{2,1,0:T(8,128)(2,1)} %param.13) | copy-start | bytes 4915204
  7.2 7.1 %copy-start.11 = (bf16[1024,1280]{1,0:T(8,128)(2,1)S(1)}, bf16[1024,1280]{1,0:T(8,128)(2,1)}, u32[]{:S(2)}) copy-start(bf16[1024,1280]{1,0:T(8,128)(2,1)} %param.9) | copy-start | bytes 7864324
  14.3 4.8 %copy-start.7 = (bf16[1024,1280]{1,0:T(8,128)(2,1)S(1)}, bf16[1024,1280]{1,0:T(8,128)(2,1)}, u32[]{:S(2)}) copy-start(bf16[1024,1280]{1,0:T(8,128)(2,1)} %param.10) | copy-start | bytes 7864324
  19.1 0.7 copy-start.9
  19.1 1.4 copy-start
  46.8 260.0 %all-gather.2.cloned.1.call-start = ((), (), s32[]{:S(2)}) async-start(), calls=%async_computation.1 | async-start | bytes 6963200 | tf_op jit(solution)/shard_map/all_gather | solution.py:55
  47.6 335.7 %reduce-scatter.2.cloned.1.call-start = ((), (), s32[]{:S(2)}) async-start(), calls=%async_computation.2 | async-start | bytes 7864320 | tf_op jit(solution)/shard_map/reduce_scatter | solution.py:58
  52.6 4.6 %copy-start.10 = (f32[1280]{0:T(1024)S(1)}, f32[1280]{0:T(1024)}, u32[]{:S(2)}) copy-start(f32[1280]{0:T(1024)} %param.16) | copy-start | bytes 15364
  241.1 2.8 copy-start.1
  241.1 3.4 copy-start.2
  244.5 3.6 copy-start.4
  248.1 2.6 copy-start.3
  251.1 2.4 copy-start.6
  253.5 4.6 %copy-start.5 = (bf16[2,640,640]{1,2,0:T(8,128)(2,1)S(1)}, bf16[2,640,640]{1,2,0:T(8,128)(2,1)}, u32[]{:S(2)}) copy-start(bf16[2,640,640]{1,2,0:T(8,128)(2,1)} %multiply_convert_fusion) | copy-start | bytes 4915204
Sparse Core Ops, SparseCore 0:
  46.9 194.0 all-reduce.2
  243.3 63.4 all-gather.1
  319.0 64.2 reduce-scatter.1
where the time goes:
time: 390 us
  waiting for transfers between devices  278 us (71%)
  matrix products  65.3 us (17%)
  local copies, waits for them, and re-layouts  17.3 us (4%)
  other arithmetic  15 us (4%)
  between operations  13.9 us (4%)
    psum x1, waiting for transfers between devices, on_device(): sum_in, sum_gate, sum_out = lax.psum((grad_in, grad_gate, grad_out), 'ctx')  184 us
    reduce_scatter x1, waiting for transfers between devices, on_device(): lax.psum_scatter(partial_out.astype(jnp.bfloat16), 'head', scatter_dimens...  60 us
    all_gather x1, waiting for transfers between devices, on_device(): lax.all_gather(out_proj, 'ctx', axis=1, tiled=True)  33.6 us
    unnamed x28, local copies, waits for them, and re-layouts  12.7 us
    dot_general x1, matrix products, on_device(): jnp.dot(normed, lax.all_gather(out_proj, 'ctx', axis=1, tiled=True), pref...  12 us
    dot_general x1, matrix products, on_device(): jnp.einsum('thf,hfd->thd', q_hidden, upd_out, preferred_element_type=jnp....  10.7 us
    dot_general x1, matrix products, on_device(): jnp.einsum('thd,thf->hdf', keyed, back_in, preferred_element_type=jnp.flo...  9.04 us
    dot_general x1, matrix products, on_device(): jnp.einsum('thf,thd->hfd', hidden, err, preferred_element_type=jnp.float32)  8.26 us
  transfers between devices with their start and end apart: 3, of which 3 were waited for; matrix products, arithmetic and copies ran while one was open for 11% of the time, Pallas kernels for 0%

commit v1 on v0

v1 whole, which is shorter than its diff:
```python
import functools

import jax
import jax.numpy as jnp
from jax import lax
from jax.experimental import pallas as pl
from jax.experimental.pallas import tpu as pltpu
from jax.sharding import PartitionSpec as P

F32 = jnp.float32
BF16 = jnp.bfloat16
NT = (((1,), (1,)), ((), ()))
EPS = 1e-06
VMEM_BYTES = 56 * 1024 * 1024
PARAMS = pltpu.CompilerParams(vmem_limit_bytes=VMEM_BYTES, dimension_semantics=("arbitrary",))


def dot(a, b):
    return jnp.dot(a, b, preferred_element_type=F32)


def dot_nt(a, b):
    return lax.dot_general(a, b, NT, preferred_element_type=F32)


def sigmoid(x):
    return 0.5 * jnp.tanh(0.5 * x) + 0.5


def grad_kernel(head_ref, k_ref, v_ref, lr_ref, win_ref, wgate_ref, wout_ref, pair_ref, out_ref, *refs):
    w_t, backs = refs[-2:]
    units = wout_ref.shape[1]
    w_t[0:units] = win_ref[0].T
    w_t[units:] = wgate_ref[0].T
    if len(refs) > 2:
        refs[0][...] = w_t[...].reshape(refs[0].shape)
        refs[1][...] = wout_ref[0].T
    k = k_ref[...]
    v = v_ref[...]
    rate = -lr_ref[pl.ds(head_ref[0], 1), :]
    count = units // 2
    for lo in range(0, units, count):
        pre_in = dot_nt(w_t[lo : lo + count], k)
        pre_gate = dot_nt(w_t[units + lo : units + lo + count], k)
        back = dot_nt(wout_ref[0, lo : lo + count], v) * rate
        sig = sigmoid(pre_in)
        act = pre_in * sig
        backs[lo : lo + count] = (back * pre_gate * (sig + act * (1.0 - sig))).astype(BF16)
        backs[units + lo : units + lo + count] = (back * act).astype(BF16)
        backs[2 * units + lo : 2 * units + lo + count] = (act * pre_gate * rate).astype(BF16)
    pair_ref[...] = dot(backs[0 : 2 * units], k).astype(BF16).reshape(pair_ref.shape)
    out_ref[...] = dot(backs[2 * units :], v).T.astype(BF16)


def grads_of(head, with_weights, key_rows, value_rows, learn_rates, fast_in, fast_gate, fast_out):
    tokens = key_rows.shape[0]
    heads, width, units = fast_in.shape
    weight = pl.BlockSpec((1, width, units), lambda t, h: (h[0], 0, 0))
    rows = pl.BlockSpec((tokens, width), lambda t, h: (0, h[0]))
    copies = 1 + with_weights
    return pl.pallas_call(
        grad_kernel,
        out_shape=[jax.ShapeDtypeStruct((2, units, width), BF16), jax.ShapeDtypeStruct((width, units), BF16)] * copies,
        grid_spec=pltpu.PrefetchScalarGridSpec(
            num_scalar_prefetch=1,
            grid=(1,),
            in_specs=[rows, rows, pl.BlockSpec((heads, tokens), lambda t, h: (0, 0)), weight, weight, weight],
            out_specs=[
                pl.BlockSpec((2, units, width), lambda t, h: (0, 0, 0)),
                pl.BlockSpec((width, units), lambda t, h: (0, 0)),
            ]
            * copies,
            scratch_shapes=[pltpu.VMEM((2 * units, width), BF16), pltpu.VMEM((3 * units, tokens), BF16)],
        ),
        compiler_params=PARAMS,
        cost_estimate=pl.CostEstimate(
            flops=tokens * width * units, bytes_accessed=4 * tokens * width, transcendentals=0
        ),
        name="grads",
    )(head, key_rows, value_rows, learn_rates, fast_in, fast_gate, fast_out)


def settle(spot_ref, pairs, outs, pair_scratch, out_scratch):
    sides, ranks, two, piece, _ = pairs.shape
    upper, rank = spot_ref[1], spot_ref[2]
    half = ranks * piece
    units = sides * half
    for s in range(sides):
        for r in range(ranks):
            start = (upper ^ s) * half + (rank ^ r) * piece
            for m in range(two):
                pair_scratch[pl.ds(pl.multiple_of(m * units + start, piece), piece), :] = pairs[s, r, m]
            start = (rank ^ r) * (sides * piece) + (upper ^ s) * piece
            out_scratch[pl.ds(pl.multiple_of(start, piece), piece), :] = outs[r, s]


def query_kernel(final, spot_ref, *refs):
    q_refs, gain_ref = refs[0:2], refs[2]
    earlier_ref = refs[7] if final else None
    proj_ref, out_ref, normed_ref, pair_scratch, out_scratch = refs[-5:]
    width = q_refs[0].shape[1]

    @pl.when(pl.program_id(0) == 0)
    def _():
        for j in range(2):
            settle(spot_ref, refs[3 + 2 * j], refs[4 + 2 * j], pair_scratch.at[j], out_scratch.at[j])

    for j in range(2):
        head = spot_ref[0] if j == 0 else 1 - spot_ref[0]
        both = dot_nt(q_refs[j][...], pair_scratch[j])
        units = both.shape[1] // 2
        q_in, q_gate = both[:, :units], both[:, units:]
        hidden = (q_in * sigmoid(q_in) * q_gate).astype(BF16)
        head_out = dot_nt(hidden, out_scratch[j])
        inverse = lax.rsqrt(jnp.mean(head_out * head_out, axis=-1, keepdims=True) + EPS)
        normed = (head_out * inverse * gain_ref[head]).astype(BF16)
        normed_ref[:, pl.ds(pl.multiple_of(head * width, 128), width)] = normed
    total = dot_nt(normed_ref[...], proj_ref[0])
    if final:
        total = total + earlier_ref[...]
    out_ref[...] = total.astype(out_ref.dtype)


def query_heads(spot, queries, gains, proj, mine, theirs, earlier):
    tokens = queries.shape[0]
    _, outs, lanes = proj.shape
    width = units = lanes // 2
    block = tokens // 2
    final = earlier is not None

    def whole(array):
        return pl.BlockSpec(array.shape, lambda t, s: (0,) * array.ndim)

    in_specs = [
        pl.BlockSpec((block, width), lambda t, s: (t, s[0])),
        pl.BlockSpec((block, width), lambda t, s: (t, 1 - s[0])),
        whole(gains),
    ] + [whole(a) for a in (*mine, *theirs)]
    operands = [queries, queries, gains, *mine, *theirs]
    if final:
        in_specs.append(pl.BlockSpec((block, outs), lambda t, s: (t, 0)))
        operands.append(earlier)
    in_specs.append(pl.BlockSpec((1, outs, lanes), lambda t, s: (s[3], 0, 0)))
    operands.append(proj)
    return pl.pallas_call(
        functools.partial(query_kernel, final),
        out_shape=jax.ShapeDtypeStruct((tokens, outs), BF16 if final else F32),
        grid_spec=pltpu.PrefetchScalarGridSpec(
            num_scalar_prefetch=1,
            grid=(tokens // block,),
            in_specs=in_specs,
            out_specs=pl.BlockSpec((block, outs), lambda t, s: (t, 0)),
            scratch_shapes=[
                pltpu.VMEM((block, lanes), BF16),
                pltpu.VMEM((2, 2 * units, width), BF16),
                pltpu.VMEM((2, width, units), BF16),
            ],
        ),
        compiler_params=PARAMS,
        cost_estimate=pl.CostEstimate(
            flops=12 * tokens * width * width + 4 * tokens * width * outs,
            bytes_accessed=4 * tokens * width + 12 * width * width + 4 * tokens * outs,
            transcendentals=0,
        ),
        name="queries",
    )(spot, *operands)


def untranspose_kernel(spot_ref, *refs):
    outs, pair_scratch, out_scratch = refs[4:7], refs[7], refs[8]
    units = out_scratch.shape[1]
    for j in range(2):

        @pl.when(pl.program_id(0) == j)
        def _():
            settle(spot_ref, refs[2 * j], refs[2 * j + 1], pair_scratch, out_scratch)

    outs[0][0] = pair_scratch[0:units].T
    outs[1][0] = pair_scratch[units:].T
    outs[2][0] = out_scratch[...].T


def untransposed(spot, mine, theirs):
    width = mine[0].shape[-1]
    units = width

    def whole(array):
        return pl.BlockSpec(array.shape, lambda j, s: (0,) * array.ndim)

    return pl.pallas_call(
        untranspose_kernel,
        out_shape=[jax.ShapeDtypeStruct((2, width, units), BF16)] * 3,
        grid_spec=pltpu.PrefetchScalarGridSpec(
            num_scalar_prefetch=1,
            grid=(2,),
            in_specs=[whole(a) for a in (*mine, *theirs)],
            out_specs=[pl.BlockSpec((1, width, units), lambda j, s: (j + s[0] - 2 * j * s[0], 0, 0))] * 3,
            scratch_shapes=[pltpu.VMEM((2 * units, width), BF16), pltpu.VMEM((width, units), BF16)],
        ),
        compiler_params=PARAMS,
        cost_estimate=pl.CostEstimate(flops=0, bytes_accessed=24 * units * width, transcendentals=0),
        name="untranspose",
    )(spot, *mine, *theirs)


def renorm(wide, grad):
    moved = wide - grad
    scale = jnp.sqrt(jnp.sum(wide * wide, axis=-1, keepdims=True) + EPS) / jnp.sqrt(
        jnp.sum(moved * moved, axis=-1, keepdims=True) + EPS
    )
    return (moved * scale).astype(BF16)


def on_device(n_ctx, n_head, key_rows, value_rows, query_rows, learn_rates, fast_in, fast_gate, fast_out, head_gain, out_proj):
    heads, width, units = fast_in.shape
    place = lax.axis_index("ctx")
    group = lax.axis_index("head")
    core, upper, rank = place % 2, (place // 2) % 2, place // 4
    ranks = n_ctx // 4
    half = units // 2
    piece = half // ranks

    def across(array, mask):
        return lax.ppermute(array, "ctx", [(j, j ^ mask) for j in range(n_ctx)])

    def over(array):
        return lax.ppermute(array, "head", [(j, j ^ 1) for j in range(n_head)])

    def part(array, start, count, axis=0):
        return lax.dynamic_slice_in_dim(array, start, count, axis)

    def to_upper(array_for):
        return across(array_for(1 - upper), 2)

    def to_ranks(array_for):
        return [across(array_for(rank ^ d), 4 * d) for d in range(1, ranks)]

    tie = lax.optimization_barrier

    core_arg = core.astype(jnp.int32).reshape(1)
    inputs = (key_rows, value_rows, learn_rates, fast_in, fast_gate, fast_out)

    tokens = query_rows.shape[0]
    third = tokens // 3 // 16 * 16
    cuts = (0, tokens - 2 * third, tokens - third, tokens)
    query_parts = [query_rows[a:b] for a, b in zip(cuts, cuts[1:])]
    far_parts = [over(query_parts[0])]
    far_gain = over(head_gain)

    half_ctx = n_ctx // 2
    here = (place // half_ctx) == group
    block = out_proj.T
    pairs = []
    for j in range(half_ctx):
        low, high = (j * n_head) + 1, (j + half_ctx) * n_head
        pairs += [(low, high), (high, low)]
    swapped = lax.ppermute(block, ("ctx", "head"), pairs)

    other = grads_of(1 - core_arg, 0, *inputs)
    other, inputs, far_gain = tie((other, inputs, far_gain))
    got_pair, got_out = (across(a, 1) for a in other)
    own_pair, own_out, pair_old, out_old = grads_of(core_arg, 1, *inputs)
    own_pair, own_out, swapped = tie((own_pair, own_out, swapped))
    proj = lax.all_gather(jnp.where(here, block, swapped), "ctx", axis=0, tiled=True)
    proj = proj.reshape(2, -1, proj.shape[1])

    def pair_sum(start, count):
        return part(own_pair, start, count, 1).astype(F32) + part(got_pair, start, count, 1).astype(F32)

    def out_sum(start, count):
        return part(own_out, start, count).astype(F32) + part(got_out, start, count).astype(F32)

    pair_got = to_upper(lambda u: pair_sum(u * half, half).astype(BF16))
    out_got = to_ranks(lambda r: out_sum(r * 2 * piece, 2 * piece).astype(BF16))
    pair_total = pair_sum(upper * half, half) + pair_got.astype(F32)
    out_total = out_sum(rank * 2 * piece, 2 * piece)
    for a in out_got:
        out_total = out_total + a.astype(F32)
    pair_sent, out_sent = pair_total.astype(BF16), out_total.astype(BF16)
    pair_sent, out_sent, far_parts[0], query_parts = tie((pair_sent, out_sent, far_parts[0], query_parts))
    pair_got = to_ranks(lambda r: part(pair_sent, r * piece, piece, 1))
    out_got = to_upper(lambda u: part(out_sent, u * piece, piece))
    far_parts.append(over(query_parts[1]))
    pair_grad = part(pair_total, rank * piece, piece, 1)
    for a in pair_got:
        pair_grad = pair_grad + a.astype(F32)
    out_grad = part(out_total, upper * piece, piece) + out_got.astype(F32)

    pair_wide = part(pair_old, upper * half + rank * piece, piece, 1).astype(F32)
    out_wide = part(out_old, rank * 2 * piece + upper * piece, piece).astype(F32)
    pair_new, out_new = renorm(pair_wide, pair_grad), renorm(out_wide, out_grad)
    pair_new, out_new, far_parts[1], query_parts = tie((pair_new, out_new, far_parts[1], query_parts))

    pair_held = jnp.stack([pair_new] + to_ranks(lambda r: pair_new))
    out_held = jnp.stack([out_new, to_upper(lambda u: out_new)])
    far_parts.append(over(query_parts[2]))
    pair_held, out_held, far_parts = tie((pair_held, out_held, far_parts))

    def finish(pair, out, beside):
        pair_got, out_got = across(pair, 2), to_ranks(lambda r: out)
        pair_got, out_got, done = tie((pair_got, out_got, beside()))
        return (jnp.stack([pair, pair_got]), jnp.stack([out] + out_got)), done

    if piece % 16:
        spot = jnp.stack([core, 0, 0, 0]).astype(jnp.int32)
    else:
        spot = jnp.stack([core, upper, rank, 0]).astype(jnp.int32)
    spot, far_spot = spot.at[3].set(group), spot.at[3].set(1 - group)

    def settled(pair, out):
        if piece % 16:
            side, order = jnp.arange(2) ^ upper, jnp.arange(ranks) ^ rank
            pair = jnp.take(jnp.take(pair, side, 0), order, 1).transpose(2, 0, 1, 3, 4).reshape(1, 1, 2, units, width)
            out = jnp.take(jnp.take(out, order, 0), side, 1).reshape(1, 1, units, width)
        return pair, out

    shards = pair_held.size // pair_new[0].size
    both = jnp.concatenate([pair_held.reshape(shards, piece, width), out_held])
    mine, both = finish(pair_held, out_held, lambda: over(both))
    far_pair, far_out = both[:shards].reshape(pair_held.shape), both[shards:]
    theirs = tuple(across(a, 1) for a in mine)
    mine, theirs, far_pair, far_out = tie((mine, theirs, far_pair, far_out))

    gains = head_gain.reshape(heads, 1, width)
    far_gains = far_gain.reshape(heads, 1, width)
    far_mine, partial = finish(
        far_pair,
        far_out,
        lambda: query_heads(spot, query_rows, gains, proj, settled(*mine), settled(*theirs), None),
    )
    mine, theirs, far_mine = tie((mine, theirs, far_mine))
    far_theirs = tuple(across(a, 1) for a in far_mine)
    news = untransposed(spot, settled(*mine), settled(*theirs))
    far_rows = jnp.concatenate(far_parts)
    output = query_heads(far_spot, far_rows, far_gains, proj, settled(*far_mine), settled(*far_theirs), partial)
    return (output, *news)


def solution(mesh):
    return jax.shard_map(
        functools.partial(on_device, mesh.shape["ctx"], mesh.shape["head"]),
        mesh=mesh,
        in_specs=(
            P("ctx", "head"),
            P("ctx", "head"),
            P("ctx", "head"),
            P("head", "ctx"),
            P("head", None, None),
            P("head", None, None),
            P("head", None, None),
            P("head"),
            P("head", "ctx"),
        ),
        out_specs=(
            P("ctx", "head"),
            P("head", None, None),
            P("head", None, None),
            P("head", None, None),
        ),
        check_vma=False,
    )
```

time: 390 us -> 243 us (0.62)
  waiting for transfers between devices: 278 us -> 97.4 us
  Pallas kernels: 0 us -> 65.8 us
  matrix products: 65.3 us -> 0 us
  starting transfers between devices: 0.12 us -> 39.8 us
  local copies, waits for them, and re-layouts: 17.3 us -> 5.01 us
  other arithmetic: 15 us -> 20.1 us
    psum x1 -> x0, waiting for transfers between devices: 184 us -> none  [on_device(): sum_in, sum_gate, sum_out = lax.psum((grad_in, grad_gate, grad_out), 'ctx')]
    ppermute x0 -> x32, waiting for transfers between devices: none -> 97.4 us  [the longest x26 92.7 us: across(): return lax.ppermute(array, 'ctx', [(j, j ^ mask) for j in range(n_ctx)])]
    pallas_call x0 -> x5, Pallas kernels: none -> 65.8 us  [the longest x2 38.8 us: query_heads(): pl.pallas_call(functools.partial(query_kernel, final), out_shape=jax.Shap...]
    dot_general x9 -> x0, matrix products: 65.3 us -> none  [the longest x1 12 us: on_device(): jnp.dot(normed, lax.all_gather(out_proj, 'ctx', axis=1, tiled=True), pref...]
    reduce_scatter x1 -> x0, waiting for transfers between devices: 60 us -> none  [on_device(): lax.psum_scatter(partial_out.astype(jnp.bfloat16), 'head', scatter_dimens...]
    ppermute x0 -> x32, starting transfers between devices: none -> 39.7 us  [the longest x26 27.4 us: across(): return lax.ppermute(array, 'ctx', [(j, j ^ mask) for j in range(n_ctx)])]
    all_gather x1, waiting for transfers between devices: 33.6 us -> 0.01 us  [on_device(): lax.all_gather(jnp.where(here, block, swapped), 'ctx', axis=0, tiled=True)]
    unnamed x28 -> x41, local copies, waits for them, and re-layouts: 12.7 us -> 1.27 us
  transfers between devices with their start and end apart: 3 -> 33, of which waited for: 3 -> 14; matrix products, arithmetic and copies ran while one was open for 11% -> 8% of each run, Pallas kernels for 0% -> 19%
where the time goes in v1:
time: 243 us; the launch traced here: 242 us
  waiting for transfers between devices  97.4 us (40%)
  Pallas kernels  65.8 us (27%)
  starting transfers between devices  39.8 us (16%)
  other arithmetic  20.1 us (8%)
  between operations  14.4 us (6%)
  local copies, waits for them, and re-layouts  5.01 us (2%)
    ppermute x26, waiting for transfers between devices, across(): return lax.ppermute(array, 'ctx', [(j, j ^ mask) for j in range(n_ctx)])  92.7 us
    pallas_call x2, Pallas kernels, query_heads(): pl.pallas_call(functools.partial(query_kernel, final), out_shape=jax.Shap...  38.8 us
    ppermute x26, starting transfers between devices, across(): return lax.ppermute(array, 'ctx', [(j, j ^ mask) for j in range(n_ctx)])  27.4 us
    pallas_call x2, Pallas kernels, grads_of(): pl.pallas_call(grad_kernel, out_shape=[jax.ShapeDtypeStruct((2, units, wi...  20.8 us
    ppermute x5, starting transfers between devices, over(): return lax.ppermute(array, 'head', [(j, j ^ 1) for j in range(n_head)])  11.6 us
    pallas_call x1, Pallas kernels, untransposed(): pl.pallas_call(untranspose_kernel, out_shape=[jax.ShapeDtypeStruct((2, wi...  6.15 us
  transfers between devices with their start and end apart: 33, of which 14 were waited for; matrix products, arithmetic and copies ran while one was open for 8% of the time, Pallas kernels for 19%

profile of v1, /device:TPU:0, one launch (start us, length us, event | category | flops | bytes accessed | tf_op | source)
XLA Modules:
  0.0 242.4 jit_solution(1278554541849949645)
XLA Ops:
  7.9 6.8 %collective-permute-start = (f32[1280]{0:T(1024)}, f32[1280]{0:T(1024)S(1)}, u32[]{:S(2)}, u32[]{:S(2)}) collective-permute-start(f32[1280]{0:T(1024)} %param.20), channel_id=1, source_target_pairs={{0,1},{1,0},{2,3},{3,2},{4,5},{5,4},{6,7},{7,6},{8,9},{9,8},{10,11... | collective-permute-start | bytes 15368 | tf_op jit(solution)/shard_map/ppermute | solution.py:227
  14.7 10.1 %grads.2 = (bf16[2,640,640]{2,1,0:T(8,128)(2,1)}, bf16[640,640]{1,0:T(8,128)(2,1)}) custom-call(s32[1]{0:T(128)S(6)} %sub.29.head_ref, bf16[1024,1280]{1,0:T(8,128)(2,1)} %k_ref.2, bf16[1024,1280]{1,0:T(8,128)(2,1)} %v_ref.2, f32[2,1024]{1,0:T(2,128)} %lr_ref.2, bf16[2,640,640]{2,1,0:T(8,128)(2,1)} %win_ref.2, bf16[2,640,640]{2,1,0:T(8,128)(2,1)} %wgate_ref.2, ...), custom_call_target="tpu_custom_call" | custom-call | flops 419430400 | bytes 2621440 | tf_op jit(solution)/shard_map/grads/pallas_call | solution.py:61
  24.8 10.8 %grads.3 = (bf16[2,640,640]{2,1,0:T(8,128)(2,1)}, bf16[640,640]{1,0:T(8,128)(2,1)}, bf16[2,640,640]{2,1,0:T(8,128)(2,1)}, bf16[640,640]{1,0:T(8,128)(2,1)}) custom-call(s32[1]{0:T(128)} %bitcast.head_ref, bf16[1024,1280]{1,0:T(8,128)(2,1)} %k_ref.2, bf16[1024,1280]{1,0:T(8,128)(2,1)} %v_ref.2, f32[2,1024]{1,0:T(2,128)} %lr_ref.2, ...), custom_call_target="tpu_custom_call" | custom-call | flops 419430400 | bytes 2621440 | tf_op jit(solution)/shard_map/grads/pallas_call | solution.py:61
  38.0 2.3 collective-permute-done.2
  40.3 2.5 %add_convert_fusion = bf16[2,320,640]{2,1,0:T(8,128)(2,1)} fusion(bf16[2,640,640]{2,1,0:T(8,128)(2,1)} %collective-permute-done.2, s32[]{:T(128)S(6)} %select_n.83, bf16[2,640,640]{2,1,0:T(8,128)(2,1)} %get-tuple-element.96), kind=kLoop, calls=%fused_computation.4 | loop fusion | flops 1638400 | bytes 2457604 | tf_op jit(solution)/shard_map/convert_element_type | solution.py:273
  51.2 11.3 %collective-permute-done.5 = bf16[160,640]{1,0:T(8,128)(2,1)} collective-permute-done((bf16[160,640]{1,0:T(8,128)(2,1)}, bf16[160,640]{1,0:T(8,128)(2,1)}, u32[]{:S(2)}, u32[]{:S(2)}) %collective-permute-start.5) | collective-permute-done | bytes 204832 | tf_op jit(solution)/shard_map/ppermute | solution.py:224
  62.5 4.2 %collective-permute-done.7 = bf16[160,640]{1,0:T(8,128)(2,1)} collective-permute-done((bf16[160,640]{1,0:T(8,128)(2,1)}, bf16[160,640]{1,0:T(8,128)(2,1)}, u32[]{:S(2)}, u32[]{:S(2)}) %collective-permute-start.7) | collective-permute-done | bytes 204832 | tf_op jit(solution)/shard_map/ppermute | solution.py:224
  66.7 11.7 %collective-permute-done.6 = bf16[160,640]{1,0:T(8,128)(2,1)} collective-permute-done((bf16[160,640]{1,0:T(8,128)(2,1)}, bf16[160,640]{1,0:T(8,128)(2,1)}, u32[]{:S(2)}, u32[]{:S(2)}) %collective-permute-start.6) | collective-permute-done | bytes 204832 | tf_op jit(solution)/shard_map/ppermute | solution.py:224
  91.5 12.5 %collective-permute-done.9 = bf16[2,80,640]{2,1,0:T(8,128)(2,1)S(1)} collective-permute-done((bf16[2,80,640]{2,1,0:T(8,128)(2,1)S(1)}, bf16[2,80,640]{2,1,0:T(8,128)(2,1)S(1)}, u32[]{:S(2)}, u32[]{:S(2)}) %collective-permute-start.9) | collective-permute-done | bytes 204832 | tf_op jit(solution)/shard_map/ppermute | solution.py:224
  104.0 22.2 %collective-permute-done.10 = bf16[2,80,640]{2,1,0:T(8,128)(2,1)S(1)} collective-permute-done((bf16[2,80,640]{2,1,0:T(8,128)(2,1)S(1)}, bf16[2,80,640]{2,1,0:T(8,128)(2,1)S(1)}, u32[]{:S(2)}, u32[]{:S(2)}) %collective-permute-start.10) | collective-permute-done | bytes 204832 | tf_op jit(solution)/shard_map/ppermute | solution.py:224
  130.5 3.8 %collective-permute-start.14 = (bf16[2,80,640]{2,1,0:T(8,128)(2,1)S(1)}, bf16[2,80,640]{2,1,0:T(8,128)(2,1)S(1)}, u32[]{:S(2)}, u32[]{:S(2)}) collective-permute-start(bf16[2,80,640]{2,1,0:T(8,128)(2,1)S(1)} %multiply_convert_fusion), channel_id=1, source_target_pairs={{0,8},{2,10},{4,12},{6,14},{8,0},{10,2},{12,4},{14,6},{16,24},{18,... | collective-permute-start | bytes 614408 | tf_op jit(solution)/shard_map/ppermute | solution.py:224
  134.3 5.4 %collective-permute-done.16 = bf16[2,80,640]{2,1,0:T(8,128)(2,1)S(1)} collective-permute-done((bf16[2,80,640]{2,1,0:T(8,128)(2,1)S(1)}, bf16[2,80,640]{2,1,0:T(8,128)(2,1)S(1)}, u32[]{:S(2)}, u32[]{:S(2)}) %collective-permute-start.16) | collective-permute-done | bytes 204832 | tf_op jit(solution)/shard_map/ppermute | solution.py:224
  139.8 6.6 %collective-permute-done.15 = bf16[2,80,640]{2,1,0:T(8,128)(2,1)S(1)} collective-permute-done((bf16[2,80,640]{2,1,0:T(8,128)(2,1)S(1)}, bf16[2,80,640]{2,1,0:T(8,128)(2,1)S(1)}, u32[]{:S(2)}, u32[]{:S(2)}) %collective-permute-start.15) | collective-permute-done | bytes 204832 | tf_op jit(solution)/shard_map/ppermute | solution.py:224
  150.9 3.5 %collective-permute-start.20 = (bf16[2,80,640]{2,1,0:T(8,128)(2,1)S(1)}, bf16[2,80,640]{2,1,0:T(8,128)(2,1)S(1)}, u32[]{:S(2)}, u32[]{:S(2)}) collective-permute-start(bf16[2,80,640]{2,1,0:T(8,128)(2,1)S(1)} %pad_maximum_fusion.7), channel_id=1, source_target_pairs={{0,8},{2,10},{4,12},{6,14},{8,0},{10,2},{12,4},{14,6},{16,24},{18,... | collective-permute-start | bytes 614408 | tf_op jit(solution)/shard_map/ppermute | solution.py:224
  154.4 5.4 %collective-permute-done.22 = bf16[2,80,640]{2,1,0:T(8,128)(2,1)S(1)} collective-permute-done((bf16[2,80,640]{2,1,0:T(8,128)(2,1)S(1)}, bf16[2,80,640]{2,1,0:T(8,128)(2,1)S(1)}, u32[]{:S(2)}, u32[]{:S(2)}) %collective-permute-start.22) | collective-permute-done | bytes 204832 | tf_op jit(solution)/shard_map/ppermute | solution.py:224
  159.9 6.6 %collective-permute-done.21 = bf16[2,80,640]{2,1,0:T(8,128)(2,1)S(1)} collective-permute-done((bf16[2,80,640]{2,1,0:T(8,128)(2,1)S(1)}, bf16[2,80,640]{2,1,0:T(8,128)(2,1)S(1)}, u32[]{:S(2)}, u32[]{:S(2)}) %collective-permute-start.21) | collective-permute-done | bytes 204832 | tf_op jit(solution)/shard_map/ppermute | solution.py:224
  166.4 4.1 %collective-permute-done.23 = bf16[10,80,640]{2,1,0:T(8,128)(2,1)S(1)} collective-permute-done((bf16[10,80,640]{2,1,0:T(8,128)(2,1)S(1)}, bf16[10,80,640]{2,1,0:T(8,128)(2,1)S(1)}, u32[]{:S(2)}, u32[]{:S(2)}) %collective-permute-start.23) | collective-permute-done | bytes 1024032 | tf_op jit(solution)/shard_map/ppermute | solution.py:227
  171.8 3.6 %collective-permute-done.25.refs_6_.refs_3_ = bf16[4,2,80,640]{3,2,1,0:T(8,128)(2,1)S(1)} collective-permute-done((bf16[4,2,80,640]{3,2,1,0:T(8,128)(2,1)S(1)}, bf16[4,2,80,640]{3,2,1,0:T(8,128)(2,1)S(1)}, u32[]{:S(2)}, u32[]{:S(2)}) %collective-permute-start.25) | collective-permute-done | bytes 819232 | tf_op jit(solution)/shard_map/ppermute | solution.py:224
  179.2 3.1 %collective-permute-start.27 = (bf16[2,80,640]{2,1,0:T(8,128)(2,1)S(1)}, bf16[2,80,640]{2,1,0:T(8,128)(2,1)}, u32[]{:S(2)}, u32[]{:S(2)}) collective-permute-start(bf16[2,80,640]{2,1,0:T(8,128)(2,1)S(1)} %slice.38), channel_id=1, source_target_pairs={{0,8},{2,10},{4,12},{6,14},{8,0},{10,2},{12,4},{14,6},{16,24},{18,... | collective-permute-start | bytes 614408 | tf_op jit(solution)/shard_map/ppermute | solution.py:224
  182.4 19.2 %queries.2.refs_7_ = f32[1024,1280]{1,0:T(8,128)} custom-call(s32[4]{0:T(128)} %copy-done.18, bf16[1024,1280]{1,0:T(8,128)(2,1)} %refs_1_.1, bf16[1024,1280]{1,0:T(8,128)(2,1)} %refs_1_.1, f32[2,1,640]{2,1,0:T(1,128)} %reshape.101.refs_2_, bf16[2,4,2,80,640]{4,3,2,1,0:T(8,128)(2,1)} %copy-done, bf16[4,2,80,640]{3,2,1,0:T(8,128)(2,1)} %copy-done.1, ...), custom_call_target="tpu_custom_call" | custom-call | flops 8388608000 | bytes 12779520 | tf_op jit(solution)/shard_map/queries/pallas_call | solution.py:145
  203.0 2.8 %pad_maximum_fusion.6.refs_4_ = bf16[4,2,80,640]{3,2,1,0:T(8,128)(2,1)} fusion(bf16[1,2,80,640]{3,2,1,0:T(8,128)(2,1)} %bitcast.26, bf16[1,2,80,640]{3,2,1,0:T(8,128)(2,1)} %bitcast.25, bf16[1,2,80,640]{3,2,1,0:T(8,128)(2,1)} %bitcast.24, bf16[1,2,80,640]{3,2,1,0:T(8,128)(2,1)S(1)} %bitcast.33), kind=kLoop, calls=%fused_computation.8 | loop fusion | flops 1228800 | bytes 1638400 | tf_op jit(solution)/shard_map/stack | solution.py:302
  206.9 2.8 %pad_maximum_fusion.refs_0_.refs_1_ = bf16[1024,1280]{1,0:T(8,128)(2,1)} fusion(bf16[336,1280]{1,0:T(8,128)(2,1)} %collective-permute-done.18, bf16[336,1280]{1,0:T(8,128)(2,1)S(1)} %copy-done.9, bf16[352,1280]{1,0:T(8,128)(2,1)S(1)} %copy-done.7), kind=kLoop, calls=%fused_computation | loop fusion | flops 7864320 | bytes 5242880 | tf_op jit(solution)/shard_map/concatenate | solution.py:334
  209.7 6.1 %untranspose.1 = (bf16[2,640,640]{2,1,0:T(8,128)(2,1)}, bf16[2,640,640]{2,1,0:T(8,128)(2,1)}, bf16[2,640,640]{2,1,0:T(8,128)(2,1)}) custom-call(s32[4]{0:T(128)} %copy-done.18, bf16[2,4,2,80,640]{4,3,2,1,0:T(8,128)(2,1)} %copy-done, bf16[4,2,80,640]{3,2,1,0:T(8,128)(2,1)} %copy-done.1, bf16[2,4,2,80,640]{4,3,2,1,0:T(8,128)(2,1)} %copy-done.4, ...), custom_call_target="tpu_custom_call" | custom-call | bytes 9830400 | tf_op jit(solution)/shard_map/untranspose/pallas_call | solution.py:190
  215.9 19.7 %queries.3 = bf16[1024,1280]{1,0:T(8,128)(2,1)} custom-call(s32[4]{0:T(128)} %copy-done.19, bf16[1024,1280]{1,0:T(8,128)(2,1)} %pad_maximum_fusion.refs_0_.refs_1_, bf16[1024,1280]{1,0:T(8,128)(2,1)} %pad_maximum_fusion.refs_0_.refs_1_, f32[2,1,640]{2,1,0:T(1,128)} %reshape.97.refs_2_, bf16[2,4,2,80,640]{4,3,2,1,0:T(8,128)(2,1)} %copy-done.5, ...), custom_call_target="tpu_custom_call" | custom-call | flops 8388608000 | bytes 12779520 | tf_op jit(solution)/shard_map/queries/pallas_call | solution.py:145
  (119 shorter events, 41.0 us)
Async XLA Ops:
  7.2 175.2 %all-gather.2.cloned.1.call-start = ((), (), s32[]{:S(2)}) async-start(), calls=%async_computation | async-start | bytes 6963200 | tf_op jit(solution)/shard_map/all_gather | solution.py:264
  7.2 28.3 %collective-permute-start.1 = (bf16[160,1280]{1,0:T(8,128)(2,1)}, bf16[160,1280]{1,0:T(8,128)(2,1)S(1)}, u32[]{:S(2)}, u32[]{:S(2)}) collective-permute-start(bf16[160,1280]{1,0:T(8,128)(2,1)} %bitcast.36), channel_id=1, source_target_pairs={{1,16},{16,1},{3,18},{18,3},{5,20},{20,5},{7,22},{22,7},{9,24},{24... | collective-permute-start | bytes 1228808 | tf_op jit(solution)/shard_map/ppermute | solution.py:257
  7.9 16.9 %collective-permute-start = (f32[1280]{0:T(1024)}, f32[1280]{0:T(1024)S(1)}, u32[]{:S(2)}, u32[]{:S(2)}) collective-permute-start(f32[1280]{0:T(1024)} %param.20), channel_id=1, source_target_pairs={{0,1},{1,0},{2,3},{3,2},{4,5},{5,4},{6,7},{7,6},{8,9},{9,8},{10,11... | collective-permute-start | bytes 15368 | tf_op jit(solution)/shard_map/ppermute | solution.py:227
  37.9 44.2 %collective-permute-start.8 = (bf16[352,1280]{1,0:T(8,128)(2,1)}, bf16[352,1280]{1,0:T(8,128)(2,1)S(1)}, u32[]{:S(2)}, u32[]{:S(2)}) collective-permute-start(bf16[352,1280]{1,0:T(8,128)(2,1)} %slice.34), channel_id=1, source_target_pairs={{0,1},{1,0},{2,3},{3,2},{4,5},{5,4},{6,7},{7,6},{8,9},{9,8},{10,11... | collective-permute-start | bytes 2703368 | tf_op jit(solution)/shard_map/ppermute | solution.py:227
  42.8 37.0 %collective-permute-start.3 = (bf16[2,320,640]{2,1,0:T(8,128)(2,1)}, bf16[2,320,640]{2,1,0:T(8,128)(2,1)}, u32[]{:S(2)}, u32[]{:S(2)}) collective-permute-start(bf16[2,320,640]{2,1,0:T(8,128)(2,1)} %add_convert_fusion), channel_id=1, source_target_pairs={{0,4},{2,6},{4,0},{6,2},{8,12},{10,14},{12,8},{14,10},{16,20},{18,... | collective-permute-start | bytes 2457608 | tf_op jit(solution)/shard_map/ppermute | solution.py:224
  46.4 16.1 %collective-permute-start.5 = (bf16[160,640]{1,0:T(8,128)(2,1)}, bf16[160,640]{1,0:T(8,128)(2,1)}, u32[]{:S(2)}, u32[]{:S(2)}) collective-permute-start(bf16[160,640]{1,0:T(8,128)(2,1)} %get-tuple-element.153), channel_id=1, source_target_pairs={{0,8},{2,10},{4,12},{6,14},{8,0},{10,2},{12,4},{14,6},{16,24},{18,... | collective-permute-start | bytes 614408 | tf_op jit(solution)/shard_map/ppermute | solution.py:224
  48.0 18.7 %collective-permute-start.7 = (bf16[160,640]{1,0:T(8,128)(2,1)}, bf16[160,640]{1,0:T(8,128)(2,1)}, u32[]{:S(2)}, u32[]{:S(2)}) collective-permute-start(bf16[160,640]{1,0:T(8,128)(2,1)} %get-tuple-element.154), channel_id=1, source_target_pairs={{0,24},{2,26},{4,28},{6,30},{8,16},{10,18},{12,20},{14,22},{16,8},... | collective-permute-start | bytes 614408 | tf_op jit(solution)/shard_map/ppermute | solution.py:224
  48.0 30.4 %collective-permute-start.6 = (bf16[160,640]{1,0:T(8,128)(2,1)}, bf16[160,640]{1,0:T(8,128)(2,1)}, u32[]{:S(2)}, u32[]{:S(2)}) collective-permute-start(bf16[160,640]{1,0:T(8,128)(2,1)} %get-tuple-element.155), channel_id=1, source_target_pairs={{0,16},{2,18},{4,20},{6,22},{8,24},{10,26},{12,28},{14,30},{16,0},... | collective-permute-start | bytes 614408 | tf_op jit(solution)/shard_map/ppermute | solution.py:224
  83.5 20.5 %collective-permute-start.9 = (bf16[2,80,640]{2,1,0:T(8,128)(2,1)S(1)}, bf16[2,80,640]{2,1,0:T(8,128)(2,1)S(1)}, u32[]{:S(2)}, u32[]{:S(2)}) collective-permute-start(bf16[2,80,640]{2,1,0:T(8,128)(2,1)S(1)} %get-tuple-element.156), channel_id=1, source_target_pairs={{0,8},{2,10},{4,12},{6,14},{8,0},{10,2},{12,4},{14,6},{16,24},{18,... | collective-permute-start | bytes 614408 | tf_op jit(solution)/shard_map/ppermute | solution.py:224
  83.6 20.4 %collective-permute-start.11 = (bf16[2,80,640]{2,1,0:T(8,128)(2,1)S(1)}, bf16[2,80,640]{2,1,0:T(8,128)(2,1)S(1)}, u32[]{:S(2)}, u32[]{:S(2)}) collective-permute-start(bf16[2,80,640]{2,1,0:T(8,128)(2,1)S(1)} %get-tuple-element.157), channel_id=1, source_target_pairs={{0,24},{2,26},{4,28},{6,30},{8,16},{10,18},{12,20},{14,22},{16,8},... | collective-permute-start | bytes 614408 | tf_op jit(solution)/shard_map/ppermute | solution.py:224
  84.8 41.4 %collective-permute-start.10 = (bf16[2,80,640]{2,1,0:T(8,128)(2,1)S(1)}, bf16[2,80,640]{2,1,0:T(8,128)(2,1)S(1)}, u32[]{:S(2)}, u32[]{:S(2)}) collective-permute-start(bf16[2,80,640]{2,1,0:T(8,128)(2,1)S(1)} %get-tuple-element.158), channel_id=1, source_target_pairs={{0,16},{2,18},{4,20},{6,22},{8,24},{10,26},{12,28},{14,30},{16,0},... | collective-permute-start | bytes 614408 | tf_op jit(solution)/shard_map/ppermute | solution.py:224
  87.0 40.4 %collective-permute-start.13 = (bf16[336,1280]{1,0:T(8,128)(2,1)S(1)}, bf16[336,1280]{1,0:T(8,128)(2,1)S(1)}, u32[]{:S(2)}, u32[]{:S(2)}) collective-permute-start(bf16[336,1280]{1,0:T(8,128)(2,1)S(1)} %copy-done.11), channel_id=1, source_target_pairs={{0,1},{1,0},{2,3},{3,2},{4,5},{5,4},{6,7},{7,6},{8,9},{9,8},{10,11... | collective-permute-start | bytes 2580488 | tf_op jit(solution)/shard_map/ppermute | solution.py:227
  127.5 19.6 %collective-permute-start.18 = (bf16[336,1280]{1,0:T(8,128)(2,1)S(1)}, bf16[336,1280]{1,0:T(8,128)(2,1)}, u32[]{:S(2)}, u32[]{:S(2)}) collective-permute-start(bf16[336,1280]{1,0:T(8,128)(2,1)S(1)} %copy-done.10), channel_id=1, source_target_pairs={{0,1},{1,0},{2,3},{3,2},{4,5},{5,4},{6,7},{7,6},{8,9},{9,8},{10,11... | collective-permute-start | bytes 2580488 | tf_op jit(solution)/shard_map/ppermute | solution.py:227
  130.5 15.9 %collective-permute-start.15 = (bf16[2,80,640]{2,1,0:T(8,128)(2,1)S(1)}, bf16[2,80,640]{2,1,0:T(8,128)(2,1)S(1)}, u32[]{:S(2)}, u32[]{:S(2)}) collective-permute-start(bf16[2,80,640]{2,1,0:T(8,128)(2,1)S(1)} %multiply_convert_fusion), channel_id=1, source_target_pairs={{0,16},{2,18},{4,20},{6,22},{8,24},{10,26},{12,28},{14,30},{16,0},... | collective-permute-start | bytes 614408 | tf_op jit(solution)/shard_map/ppermute | solution.py:224
  130.5 15.9 %collective-permute-start.14 = (bf16[2,80,640]{2,1,0:T(8,128)(2,1)S(1)}, bf16[2,80,640]{2,1,0:T(8,128)(2,1)S(1)}, u32[]{:S(2)}, u32[]{:S(2)}) collective-permute-start(bf16[2,80,640]{2,1,0:T(8,128)(2,1)S(1)} %multiply_convert_fusion), channel_id=1, source_target_pairs={{0,8},{2,10},{4,12},{6,14},{8,0},{10,2},{12,4},{14,6},{16,24},{18,... | collective-permute-start | bytes 614408 | tf_op jit(solution)/shard_map/ppermute | solution.py:224
  147.2 23.3 %collective-permute-start.23 = (bf16[10,80,640]{2,1,0:T(8,128)(2,1)S(1)}, bf16[10,80,640]{2,1,0:T(8,128)(2,1)S(1)}, u32[]{:S(2)}, u32[]{:S(2)}) collective-permute-start(bf16[10,80,640]{2,1,0:T(8,128)(2,1)S(1)} %pad_maximum_fusion.3), channel_id=1, source_target_pairs={{0,1},{1,0},{2,3},{3,2},{4,5},{5,4},{6,7},{7,6},{8,9},{9,8},{10,11... | collective-permute-start | bytes 3072008 | tf_op jit(solution)/shard_map/ppermute | solution.py:227
  148.9 17.5 %collective-permute-start.19 = (bf16[4,2,80,640]{3,2,1,0:T(8,128)(2,1)S(1)}, bf16[4,2,80,640]{3,2,1,0:T(8,128)(2,1)S(1)}, u32[]{:S(2)}, u32[]{:S(2)}) collective-permute-start(bf16[4,2,80,640]{3,2,1,0:T(8,128)(2,1)S(1)} %pad_maximum_fusion.4), channel_id=1, source_target_pairs={{0,4},{2,6},{4,0},{6,2},{8,12},{10,14},{12,8},{14,10},{16,20},{18,... | collective-permute-start | bytes 2457608 | tf_op jit(solution)/shard_map/ppermute | solution.py:224
  150.9 15.5 %collective-permute-start.21 = (bf16[2,80,640]{2,1,0:T(8,128)(2,1)S(1)}, bf16[2,80,640]{2,1,0:T(8,128)(2,1)S(1)}, u32[]{:S(2)}, u32[]{:S(2)}) collective-permute-start(bf16[2,80,640]{2,1,0:T(8,128)(2,1)S(1)} %pad_maximum_fusion.7), channel_id=1, source_target_pairs={{0,16},{2,18},{4,20},{6,22},{8,24},{10,26},{12,28},{14,30},{16,0},... | collective-permute-start | bytes 614408 | tf_op jit(solution)/shard_map/ppermute | solution.py:224
  150.9 15.5 %collective-permute-start.20 = (bf16[2,80,640]{2,1,0:T(8,128)(2,1)S(1)}, bf16[2,80,640]{2,1,0:T(8,128)(2,1)S(1)}, u32[]{:S(2)}, u32[]{:S(2)}) collective-permute-start(bf16[2,80,640]{2,1,0:T(8,128)(2,1)S(1)} %pad_maximum_fusion.7), channel_id=1, source_target_pairs={{0,8},{2,10},{4,12},{6,14},{8,0},{10,2},{12,4},{14,6},{16,24},{18,... | collective-permute-start | bytes 614408 | tf_op jit(solution)/shard_map/ppermute | solution.py:224
  176.4 25.2 %collective-permute-start.26 = (bf16[4,2,80,640]{3,2,1,0:T(8,128)(2,1)S(1)}, bf16[4,2,80,640]{3,2,1,0:T(8,128)(2,1)}, u32[]{:S(2)}, u32[]{:S(2)}) collective-permute-start(bf16[4,2,80,640]{3,2,1,0:T(8,128)(2,1)S(1)} %bitcast.30), channel_id=1, source_target_pairs={{0,4},{2,6},{4,0},{6,2},{8,12},{10,14},{12,8},{14,10},{16,20},{18,... | collective-permute-start | bytes 2457608 | tf_op jit(solution)/shard_map/ppermute | solution.py:224
  177.9 23.6 %collective-permute-start.29 = (bf16[2,80,640]{2,1,0:T(8,128)(2,1)S(1)}, bf16[2,80,640]{2,1,0:T(8,128)(2,1)}, u32[]{:S(2)}, u32[]{:S(2)}) collective-permute-start(bf16[2,80,640]{2,1,0:T(8,128)(2,1)S(1)} %slice.38), channel_id=1, source_target_pairs={{0,24},{2,26},{4,28},{6,30},{8,16},{10,18},{12,20},{14,22},{16,8},... | collective-permute-start | bytes 614408 | tf_op jit(solution)/shard_map/ppermute | solution.py:224
  179.2 22.3 %collective-permute-start.28 = (bf16[2,80,640]{2,1,0:T(8,128)(2,1)S(1)}, bf16[2,80,640]{2,1,0:T(8,128)(2,1)}, u32[]{:S(2)}, u32[]{:S(2)}) collective-permute-start(bf16[2,80,640]{2,1,0:T(8,128)(2,1)S(1)} %slice.38), channel_id=1, source_target_pairs={{0,16},{2,18},{4,20},{6,22},{8,24},{10,26},{12,28},{14,30},{16,0},... | collective-permute-start | bytes 614408 | tf_op jit(solution)/shard_map/ppermute | solution.py:224
  179.2 22.3 %collective-permute-start.27 = (bf16[2,80,640]{2,1,0:T(8,128)(2,1)S(1)}, bf16[2,80,640]{2,1,0:T(8,128)(2,1)}, u32[]{:S(2)}, u32[]{:S(2)}) collective-permute-start(bf16[2,80,640]{2,1,0:T(8,128)(2,1)S(1)} %slice.38), channel_id=1, source_target_pairs={{0,8},{2,10},{4,12},{6,14},{8,0},{10,2},{12,4},{14,6},{16,24},{18,... | collective-permute-start | bytes 614408 | tf_op jit(solution)/shard_map/ppermute | solution.py:224
  205.8 10.1 %collective-permute-start.30 = (bf16[2,4,2,80,640]{4,3,2,1,0:T(8,128)(2,1)S(1)}, bf16[2,4,2,80,640]{4,3,2,1,0:T(8,128)(2,1)}, u32[]{:S(2)}, u32[]{:S(2)}) collective-permute-start(bf16[2,4,2,80,640]{4,3,2,1,0:T(8,128)(2,1)S(1)} %pad_maximum_fusion.2.refs_3_), channel_id=1, source_target_pairs={{0,2},{2,0},{4,6},{6,4},{8,10},{10,8},{12,14},{14,12},{16,18},{18,... | collective-permute-start | bytes 4915208 | tf_op jit(solution)/shard_map/ppermute | solution.py:224
  (29 other events, 317.9 us)
Sparse Core Ops, SparseCore 0:
  36.5 92.8 all-gather.1

commit v2 on v1

v2 whole, which is shorter than its diff:
```python
import functools

import jax
import jax.numpy as jnp
from jax import lax
from jax.experimental import pallas as pl
from jax.experimental.pallas import tpu as pltpu
from jax.sharding import PartitionSpec as P

F32 = jnp.float32
BF16 = jnp.bfloat16
NT = (((1,), (1,)), ((), ()))
EPS = 1e-06
VMEM_BYTES = 56 * 1024 * 1024
PARAMS = pltpu.CompilerParams(vmem_limit_bytes=VMEM_BYTES, dimension_semantics=("arbitrary",))


def dot(a, b):
    return jnp.dot(a, b, preferred_element_type=F32)


def dot_nt(a, b):
    return lax.dot_general(a, b, NT, preferred_element_type=F32)


def sigmoid(x):
    return 0.5 * jnp.tanh(0.5 * x) + 0.5


def grad_kernel(head_ref, k_ref, v_ref, lr_ref, win_ref, wgate_ref, wout_ref, pair_ref, out_ref, *refs):
    w_t, backs = refs[-2:]
    units = wout_ref.shape[1]
    w_t[0:units] = win_ref[0].T
    w_t[units:] = wgate_ref[0].T
    if len(refs) > 2:
        refs[0][...] = w_t[...].reshape(refs[0].shape)
        refs[1][...] = wout_ref[0].T
    k = k_ref[...]
    v = v_ref[...]
    rate = -lr_ref[pl.ds(head_ref[0], 1), :]
    count = units // 2
    for lo in range(0, units, count):
        pre_in = dot_nt(w_t[lo : lo + count], k)
        pre_gate = dot_nt(w_t[units + lo : units + lo + count], k)
        back = dot_nt(wout_ref[0, lo : lo + count], v) * rate
        sig = sigmoid(pre_in)
        act = pre_in * sig
        backs[lo : lo + count] = (back * pre_gate * (sig + act * (1.0 - sig))).astype(BF16)
        backs[units + lo : units + lo + count] = (back * act).astype(BF16)
        backs[2 * units + lo : 2 * units + lo + count] = (act * pre_gate * rate).astype(BF16)
    pair_ref[...] = dot(backs[0 : 2 * units], k).astype(BF16).reshape(pair_ref.shape)
    out_ref[...] = dot(backs[2 * units :], v).T.astype(BF16)


def grads_of(head, with_weights, key_rows, value_rows, learn_rates, fast_in, fast_gate, fast_out):
    tokens = key_rows.shape[0]
    heads, width, units = fast_in.shape
    weight = pl.BlockSpec((1, width, units), lambda t, h: (h[0], 0, 0))
    rows = pl.BlockSpec((tokens, width), lambda t, h: (0, h[0]))
    copies = 1 + with_weights
    return pl.pallas_call(
        grad_kernel,
        out_shape=[jax.ShapeDtypeStruct((2, units, width), BF16), jax.ShapeDtypeStruct((width, units), BF16)] * copies,
        grid_spec=pltpu.PrefetchScalarGridSpec(
            num_scalar_prefetch=1,
            grid=(1,),
            in_specs=[rows, rows, pl.BlockSpec((heads, tokens), lambda t, h: (0, 0)), weight, weight, weight],
            out_specs=[
                pl.BlockSpec((2, units, width), lambda t, h: (0, 0, 0)),
                pl.BlockSpec((width, units), lambda t, h: (0, 0)),
            ]
            * copies,
            scratch_shapes=[pltpu.VMEM((2 * units, width), BF16), pltpu.VMEM((3 * units, tokens), BF16)],
        ),
        compiler_params=PARAMS,
        cost_estimate=pl.CostEstimate(
            flops=tokens * width * units, bytes_accessed=4 * tokens * width, transcendentals=0
        ),
        name="grads",
    )(head, key_rows, value_rows, learn_rates, fast_in, fast_gate, fast_out)


def settle(spot_ref, pair_refs, out_refs, pair_scratch, out_scratch):
    upper, rank = spot_ref[1], spot_ref[2]
    pairs = [r.at[s] for r in pair_refs for s in range(r.shape[0])]
    outs = [r.at[s] for r in out_refs for s in range(r.shape[0])]
    sides, (ranks, two, piece, _) = len(pairs), pairs[0].shape
    half = ranks * piece
    units = sides * half
    for s in range(sides):
        for r in range(ranks):
            start = (upper ^ s) * half + (rank ^ r) * piece
            for m in range(two):
                pair_scratch[pl.ds(pl.multiple_of(m * units + start, piece), piece), :] = pairs[s][r, m]
            start = (rank ^ r) * (sides * piece) + (upper ^ s) * piece
            out_scratch[pl.ds(pl.multiple_of(start, piece), piece), :] = outs[r][s]


def taken(refs, counts):
    groups, at = [], 0
    for c in counts:
        groups.append(refs[at : at + c])
        at += c
    return groups


def query_kernel(counts, masks, final, spot_ref, *refs):
    *groups, rest = taken(refs, (*counts, len(refs) - sum(counts)))
    q_refs, proj_refs, weight_refs = groups[0], groups[1], groups[2:6]
    gain_ref = rest[0]
    earlier_ref = rest[1] if final else None
    out_ref, normed_ref, pair_scratch, out_scratch, proj_scratch, q_scratch = rest[-6:]
    block, lanes = normed_ref.shape
    width = lanes // 2

    @pl.when(pl.program_id(0) == 0)
    def _():
        for j in range(2):
            settle(spot_ref, weight_refs[2 * j], weight_refs[2 * j + 1], pair_scratch.at[j], out_scratch.at[j])
        rows = proj_refs[0].shape[2]
        for ref, mask in zip(proj_refs, masks):
            for k, m in enumerate(mask):
                start = pl.multiple_of((spot_ref[3] ^ m) * rows, rows)
                for j in range(2):
                    proj_scratch[pl.ds(start, rows), j * width : (j + 1) * width] = ref[k, j]
        at = 0
        for ref in q_refs:
            q_scratch[at : at + ref.shape[0]] = ref[...]
            at += ref.shape[0]

    here = pl.ds(pl.multiple_of(pl.program_id(0) * block, block), block)
    for j in range(2):
        head = spot_ref[0] if j == 0 else 1 - spot_ref[0]
        columns = pl.ds(pl.multiple_of(head * width, 128), width)
        both = dot_nt(q_scratch[here, columns], pair_scratch[j])
        units = both.shape[1] // 2
        q_in, q_gate = both[:, :units], both[:, units:]
        hidden = (q_in * sigmoid(q_in) * q_gate).astype(BF16)
        head_out = dot_nt(hidden, out_scratch[j])
        inverse = lax.rsqrt(jnp.mean(head_out * head_out, axis=-1, keepdims=True) + EPS)
        normed_ref[:, columns] = (head_out * inverse * gain_ref[head]).astype(BF16)
    total = dot_nt(normed_ref[...], proj_scratch[...])
    if final:
        total = total + earlier_ref[...]
    out_ref[...] = total.astype(out_ref.dtype)


def whole(array):
    return pl.BlockSpec(array.shape, lambda t, s: (0,) * array.ndim, pipeline_mode=pl.Buffered(1))


def query_heads(spot, queries, gains, proj, masks, mine, theirs, earlier):
    tokens = sum(q.shape[0] for q in queries)
    lanes = queries[0].shape[1]
    width = units = lanes // 2
    outs = sum(len(m) for m in masks) * proj[0].shape[2]
    block = tokens // 2
    final = earlier is not None
    groups = (queries, proj, *mine, *theirs)
    counts = tuple(len(g) for g in groups)
    operands = [a for g in groups for a in g] + [gains]
    in_specs = [whole(a) for a in operands]
    if final:
        in_specs.append(pl.BlockSpec((block, outs), lambda t, s: (t, 0)))
        operands.append(earlier)
    return pl.pallas_call(
        functools.partial(query_kernel, counts, masks, final),
        out_shape=jax.ShapeDtypeStruct((tokens, outs), BF16 if final else F32),
        grid_spec=pltpu.PrefetchScalarGridSpec(
            num_scalar_prefetch=1,
            grid=(tokens // block,),
            in_specs=in_specs,
            out_specs=pl.BlockSpec((block, outs), lambda t, s: (t, 0)),
            scratch_shapes=[
                pltpu.VMEM((block, lanes), BF16),
                pltpu.VMEM((2, 2 * units, width), BF16),
                pltpu.VMEM((2, width, units), BF16),
                pltpu.VMEM((outs, lanes), BF16),
                pltpu.VMEM((tokens, lanes), BF16),
            ],
        ),
        compiler_params=PARAMS,
        cost_estimate=pl.CostEstimate(
            flops=12 * tokens * width * width + 4 * tokens * width * outs,
            bytes_accessed=4 * tokens * width + 12 * width * width + 4 * tokens * outs,
            transcendentals=0,
        ),
        name="queries",
    )(spot, *operands)


def untranspose_kernel(counts, spot_ref, *refs):
    *groups, rest = taken(refs, (*counts, len(refs) - sum(counts)))
    outs, pair_scratch, out_scratch = rest[0:3], rest[3], rest[4]
    units = out_scratch.shape[1]
    for j in range(2):

        @pl.when(pl.program_id(0) == j)
        def _():
            settle(spot_ref, groups[2 * j], groups[2 * j + 1], pair_scratch, out_scratch)

    outs[0][0] = pair_scratch[0:units].T
    outs[1][0] = pair_scratch[units:].T
    outs[2][0] = out_scratch[...].T


def untransposed(spot, mine, theirs):
    groups = (*mine, *theirs)
    operands = [a for g in groups for a in g]
    width = units = operands[0].shape[-1]
    return pl.pallas_call(
        functools.partial(untranspose_kernel, tuple(len(g) for g in groups)),
        out_shape=[jax.ShapeDtypeStruct((2, width, units), BF16)] * 3,
        grid_spec=pltpu.PrefetchScalarGridSpec(
            num_scalar_prefetch=1,
            grid=(2,),
            in_specs=[whole(a) for a in operands],
            out_specs=[pl.BlockSpec((1, width, units), lambda j, s: (j + s[0] - 2 * j * s[0], 0, 0))] * 3,
            scratch_shapes=[pltpu.VMEM((2 * units, width), BF16), pltpu.VMEM((width, units), BF16)],
        ),
        compiler_params=PARAMS,
        cost_estimate=pl.CostEstimate(flops=0, bytes_accessed=24 * units * width, transcendentals=0),
        name="untranspose",
    )(spot, *operands)


def renorm(wide, grad):
    moved = wide - grad
    scale = jnp.sqrt(jnp.sum(wide * wide, axis=-1, keepdims=True) + EPS) / jnp.sqrt(
        jnp.sum(moved * moved, axis=-1, keepdims=True) + EPS
    )
    return (moved * scale).astype(BF16)


def on_device(n_ctx, n_head, key_rows, value_rows, query_rows, learn_rates, fast_in, fast_gate, fast_out, head_gain, out_proj):
    heads, width, units = fast_in.shape
    place = lax.axis_index("ctx")
    group = lax.axis_index("head")
    core, upper, rank = place % 2, (place // 2) % 2, place // 4
    ranks = n_ctx // 4
    half = units // 2
    piece = half // ranks

    def across(array, mask):
        return lax.ppermute(array, "ctx", [(j, j ^ mask) for j in range(n_ctx)])

    def over(array):
        return lax.ppermute(array, "head", [(j, j ^ 1) for j in range(n_head)])

    def part(array, start, count, axis=0):
        return lax.dynamic_slice_in_dim(array, start, count, axis)

    def joined(array, rider):
        flat = array.reshape(-1, width)
        return flat if rider is None else jnp.concatenate([flat, rider])

    def parted(array, like, rider):
        count = like.size // width
        return array[:count].reshape(like.shape), None if rider is None else array[count:]

    def to_upper(array_for, rider=None):
        array = array_for(1 - upper)
        return parted(across(joined(array, rider), 2), array, rider)

    def to_ranks(array_for, rider=None):
        sent = [array_for(rank ^ d) for d in range(1, ranks)]
        first, rider = parted(across(joined(sent[0], rider), 4), sent[0], rider)
        return [first] + [across(a, 4 * d) for d, a in enumerate(sent[1:], 2)], rider

    tie = lax.optimization_barrier
    core_arg = core.astype(jnp.int32).reshape(1)
    inputs = (key_rows, value_rows, learn_rates, fast_in, fast_gate, fast_out)

    tokens = query_rows.shape[0]
    third = tokens // 3 // 16 * 16
    cuts = (0, tokens - 2 * third, tokens - third, tokens)
    query_parts = [query_rows[a:b] for a, b in zip(cuts, cuts[1:])]
    far_parts = [over(query_parts[0])]

    half_ctx = n_ctx // 2
    here = (place // half_ctx) == group
    rows = out_proj.shape[1]
    stepwise = ranks == 4 and rows % 16 == 0
    block = out_proj.T.reshape(rows, 2, width).transpose(1, 0, 2).reshape(2 * rows, width)
    if stepwise:
        blocks = [block, across(block, 4), across(block, 8)]
    else:
        pairs = []
        for j in range(half_ctx):
            low, high = (j * n_head) + 1, (j + half_ctx) * n_head
            pairs += [(low, high), (high, low)]
        swapped = lax.ppermute(out_proj.T, ("ctx", "head"), pairs)
        proj = lax.all_gather(jnp.where(here, out_proj.T, swapped), "ctx", axis=0, tiled=True)
        proj = proj.reshape(2, -1, 2, width).transpose(0, 2, 1, 3)
        blocks = []

    other = grads_of(1 - core_arg, 0, *inputs)
    other, inputs = tie((other, inputs))
    got_pair, got_out = (across(a, 1) for a in other)
    own_pair, own_out, pair_old, out_old = grads_of(core_arg, 1, *inputs)
    own_pair, own_out, blocks, far_parts, query_parts = tie((own_pair, own_out, blocks, far_parts, query_parts))
    far_parts.append(over(query_parts[1]))

    def pair_sum(start, count):
        return part(own_pair, start, count, 1).astype(F32) + part(got_pair, start, count, 1).astype(F32)

    def out_sum(start, count):
        return part(own_out, start, count).astype(F32) + part(got_out, start, count).astype(F32)

    pair_got, _ = to_upper(lambda u: pair_sum(u * half, half).astype(BF16))
    out_got, rider = to_ranks(
        lambda r: out_sum(r * 2 * piece, 2 * piece).astype(BF16), blocks[2] if stepwise else None
    )
    pair_total = pair_sum(upper * half, half) + pair_got.astype(F32)
    out_total = out_sum(rank * 2 * piece, 2 * piece)
    for a in out_got:
        out_total = out_total + a.astype(F32)
    pair_sent, out_sent = pair_total.astype(BF16), out_total.astype(BF16)
    kept = given = None
    if stepwise:
        near, away = jnp.concatenate(blocks[:2]), jnp.concatenate([blocks[2], rider])
        kept, given = jnp.where(here, near, away), jnp.where(here, away, near)
    pair_sent, out_sent, kept, given, far_parts = tie((pair_sent, out_sent, kept, given, far_parts))
    pair_got, _ = to_ranks(lambda r: part(pair_sent, r * piece, piece, 1))
    out_got, kept_upper = to_upper(lambda u: part(out_sent, u * piece, piece), kept)
    come = over(given) if stepwise else None
    pair_grad = part(pair_total, rank * piece, piece, 1)
    for a in pair_got:
        pair_grad = pair_grad + a.astype(F32)
    out_grad = part(out_total, upper * piece, piece) + out_got.astype(F32)
    pair_wide = part(pair_old, upper * half + rank * piece, piece, 1).astype(F32)
    out_wide = part(out_old, rank * 2 * piece + upper * piece, piece).astype(F32)
    pair_new, out_new = renorm(pair_wide, pair_grad), renorm(out_wide, out_grad)
    pair_new, out_new, come, query_parts = tie((pair_new, out_new, come, query_parts))

    pair_got, _ = to_ranks(lambda r: pair_new)
    out_got, come_upper = to_upper(lambda u: out_new, come)
    far_parts.append(over(query_parts[2]))
    pair_held, out_held = jnp.stack([pair_new] + pair_got), jnp.stack([out_new, out_got])
    if stepwise:
        masks = [[0, 4], [2, 6], [1, 5], [3, 7]]
        own_proj = [kept, kept_upper, across(kept, 1), across(kept_upper, 1)]
        come_core = across(come, 1)
    else:
        masks = [[0]]
        own_proj, far_proj = [part(proj, group, 1)], [part(proj, 1 - group, 1)]
        come_core = None
    pair_held, out_held, far_parts, own_proj, come_core = tie((pair_held, out_held, far_parts, own_proj, come_core))

    def finish(pair, out, beside):
        (pair_got, _), (out_got, _) = to_upper(lambda u: pair), to_ranks(lambda r: out)
        pair_got, out_got, done = tie((pair_got, out_got, beside()))
        return ([pair[None], pair_got[None]], [a[None] for a in (out, *out_got)]), done

    mine, far_pair = finish(pair_held, out_held, lambda: over(pair_held))
    mine = tuple([jnp.concatenate(g)] for g in mine)

    tiled = piece % 16 == 0
    spot = [core, upper, rank] if tiled else [core, 0, 0]
    spot = jnp.stack(spot + [place % half_ctx if stepwise else 0]).astype(jnp.int32)

    def settled(pair, out):
        if not tiled:
            side, order = jnp.arange(2) ^ upper, jnp.arange(ranks) ^ rank
            pair, out = jnp.concatenate(pair), jnp.concatenate(out)
            pair = jnp.take(jnp.take(pair, side, 0), order, 1).transpose(2, 0, 1, 3, 4).reshape(1, 1, 2, units, width)
            out = jnp.take(jnp.take(out, order, 0), side, 1).reshape(1, 1, units, width)
            pair, out = [pair], [out]
        return pair, out

    def swapped_cores(arrays):
        return [across(a, 1) for a in arrays]

    theirs = tuple(swapped_cores(g) for g in mine)
    if stepwise:
        far_proj = [come, come_upper, come_core, across(come_upper, 1)]
    mine, theirs, far_pair, far_out, far_proj = tie((mine, theirs, far_pair, over(out_held), far_proj))

    def blocks_of(arrays):
        return [a.reshape(-1, 2, rows, width) for a in arrays] if stepwise else arrays

    gains = head_gain.reshape(heads, 1, width)
    far_mine, (partial, far_gain, first_pair, first_out) = finish(
        far_pair,
        far_out,
        lambda: (
            query_heads(spot, [query_rows], gains, blocks_of(own_proj), masks, settled(*mine), settled(*theirs), None),
            over(head_gain),
            across(far_pair, 1),
            across(far_out, 1),
        ),
    )
    mine, theirs, far_mine = tie((mine, theirs, far_mine))
    far_theirs = [first_pair[None]] + swapped_cores(far_mine[0][1:]), [first_out[None]] + swapped_cores(far_mine[1][1:])
    far_gains = far_gain.reshape(heads, 1, width)
    news = untransposed(spot, settled(*mine), settled(*theirs))
    output = query_heads(
        spot, far_parts, far_gains, blocks_of(far_proj), masks, settled(*far_mine), settled(*far_theirs), partial
    )
    return (output, *news)


def solution(mesh):
    return jax.shard_map(
        functools.partial(on_device, mesh.shape["ctx"], mesh.shape["head"]),
        mesh=mesh,
        in_specs=(
            P("ctx", "head"),
            P("ctx", "head"),
            P("ctx", "head"),
            P("head", "ctx"),
            P("head", None, None),
            P("head", None, None),
            P("head", None, None),
            P("head"),
            P("head", "ctx"),
        ),
        out_specs=(
            P("ctx", "head"),
            P("head", None, None),
            P("head", None, None),
            P("head", None, None),
        ),
        check_vma=False,
    )
```

time: 243 us -> 215 us (0.88)
  waiting for transfers between devices: 97.4 us -> 77.8 us
  between operations: 14.4 us -> 1.14 us
  local copies, waits for them, and re-layouts: 5.01 us -> 14 us
  other arithmetic: 20.1 us -> 14.3 us
    ppermute x26 -> x36, waiting for transfers between devices: 92.7 us -> 71.6 us  [across(): return lax.ppermute(array, 'ctx', [(j, j ^ mask) for j in range(n_ctx)])]
    unnamed x41 -> x61, local copies, waits for them, and re-layouts: 1.27 us -> 6.23 us
    ppermute x26 -> x36, starting transfers between devices: 27.4 us -> 31.8 us  [across(): return lax.ppermute(array, 'ctx', [(j, j ^ mask) for j in range(n_ctx)])]
    another operation x7 -> x3, other arithmetic: 4.69 us -> 0.79 us  [the longest x1 0.64 us: on_device(): jnp.stack(spot + [place % half_ctx if stepwise else 0]).astype(jnp.int32)]
    ppermute x5 -> x7, starting transfers between devices: 11.6 us -> 8.47 us  [over(): return lax.ppermute(array, 'head', [(j, j ^ 1) for j in range(n_head)])]
    ppermute x5 -> x7, waiting for transfers between devices: 4.62 us -> 6.25 us  [over(): return lax.ppermute(array, 'head', [(j, j ^ 1) for j in range(n_head)])]
  transfers between devices with their start and end apart: 33 -> 43, of which waited for: 14 -> 17; matrix products, arithmetic and copies ran while one was open for 8% -> 10% of each run, Pallas kernels for 19% -> 17%
where the time goes in v2:
time: 215 us
  waiting for transfers between devices  77.8 us (36%)
  Pallas kernels  67.5 us (31%)
  starting transfers between devices  40.2 us (19%)
  other arithmetic  14.3 us (7%)
  local copies, waits for them, and re-layouts  14 us (7%)
    ppermute x36, waiting for transfers between devices, across(): return lax.ppermute(array, 'ctx', [(j, j ^ mask) for j in range(n_ctx)])  71.6 us
    pallas_call x2, Pallas kernels, query_heads(): pl.pallas_call(functools.partial(query_kernel, counts, masks, final), out...  40.5 us
    ppermute x36, starting transfers between devices, across(): return lax.ppermute(array, 'ctx', [(j, j ^ mask) for j in range(n_ctx)])  31.8 us
    pallas_call x2, Pallas kernels, grads_of(): pl.pallas_call(grad_kernel, out_shape=[jax.ShapeDtypeStruct((2, units, wi...  20.9 us
    ppermute x7, starting transfers between devices, over(): return lax.ppermute(array, 'head', [(j, j ^ 1) for j in range(n_head)])  8.47 us
    ppermute x7, waiting for transfers between devices, over(): return lax.ppermute(array, 'head', [(j, j ^ 1) for j in range(n_head)])  6.25 us
    unnamed x61, local copies, waits for them, and re-layouts  6.23 us
    pallas_call x1, Pallas kernels, untransposed(): pl.pallas_call(functools.partial(untranspose_kernel, tuple((len(g) for g...  6.15 us
  transfers between devices with their start and end apart: 43, of which 17 were waited for; matrix products, arithmetic and copies ran while one was open for 10% of the time, Pallas kernels for 17%

profile of v2, /device:TPU:0, one launch (start us, length us, event | category | flops | bytes accessed | tf_op | source)
XLA Modules:
  0.0 215.0 jit_solution(8289642671147532698)
XLA Ops:
  0.7 10.2 %grads.2 = (bf16[2,640,640]{2,1,0:T(8,128)(2,1)}, bf16[640,640]{1,0:T(8,128)(2,1)}) custom-call(s32[1]{0:T(128)S(6)} %sub.25.head_ref, bf16[1024,1280]{1,0:T(8,128)(2,1)} %k_ref.2, bf16[1024,1280]{1,0:T(8,128)(2,1)} %v_ref.2, f32[2,1024]{1,0:T(2,128)} %lr_ref.2, bf16[2,640,640]{2,1,0:T(8,128)(2,1)} %win_ref.2, bf16[2,640,640]{2,1,0:T(8,128)(2,1)} %wgate_ref.2, ...), custom_call_target="tpu_custom_call" | custom-call | flops 419430400 | bytes 2621440 | tf_op jit(solution)/shard_map/grads/pallas_call | solution.py:61
  12.3 2.5 %collective-permute-start.2 = (bf16[352,1280]{1,0:T(8,128)(2,1)}, bf16[352,1280]{1,0:T(8,128)(2,1)}, u32[]{:S(2)}, u32[]{:S(2)}) collective-permute-start(bf16[352,1280]{1,0:T(8,128)(2,1)} %slice.27), channel_id=1, source_target_pairs={{0,1},{1,0},{2,3},{3,2},{4,5},{5,4},{6,7},{7,6},{8,9},{9,8},{10,11... | collective-permute-start | bytes 2703368 | tf_op jit(solution)/shard_map/ppermute | solution.py:248
  15.0 2.6 %collective-permute-start.1 = (bf16[320,640]{1,0:T(8,128)(2,1)S(1)}, bf16[320,640]{1,0:T(8,128)(2,1)S(1)}, u32[]{:S(2)}, u32[]{:S(2)}) collective-permute-start(bf16[320,640]{1,0:T(8,128)(2,1)S(1)} %bitcast.59), channel_id=1, source_target_pairs={{0,16},{2,18},{4,20},{6,22},{8,24},{10,26},{12,28},{14,30},{16,0},... | collective-permute-start | bytes 1228808 | tf_op jit(solution)/shard_map/ppermute | solution.py:245
  19.3 10.7 %grads.3 = (bf16[2,640,640]{2,1,0:T(8,128)(2,1)}, bf16[640,640]{1,0:T(8,128)(2,1)}, bf16[2,640,640]{2,1,0:T(8,128)(2,1)}, bf16[640,640]{1,0:T(8,128)(2,1)}) custom-call(s32[1]{0:T(128)} %bitcast.head_ref, bf16[1024,1280]{1,0:T(8,128)(2,1)} %k_ref.2, bf16[1024,1280]{1,0:T(8,128)(2,1)} %v_ref.2, f32[2,1024]{1,0:T(2,128)} %lr_ref.2, ...), custom_call_target="tpu_custom_call" | custom-call | flops 419430400 | bytes 2621440 | tf_op jit(solution)/shard_map/grads/pallas_call | solution.py:61
  31.3 5.2 %collective-permute-done.1 = bf16[320,640]{1,0:T(8,128)(2,1)S(1)} collective-permute-done((bf16[320,640]{1,0:T(8,128)(2,1)S(1)}, bf16[320,640]{1,0:T(8,128)(2,1)S(1)}, u32[]{:S(2)}, u32[]{:S(2)}) %collective-permute-start.1) | collective-permute-done | bytes 409632 | tf_op jit(solution)/shard_map/ppermute | solution.py:245
  36.8 2.0 add_convert_fusion.3
  48.5 15.2 %collective-permute-done.6 = bf16[480,640]{1,0:T(8,128)(2,1)} collective-permute-done((bf16[480,640]{1,0:T(8,128)(2,1)}, bf16[480,640]{1,0:T(8,128)(2,1)}, u32[]{:S(2)}, u32[]{:S(2)}) %collective-permute-start.6) | collective-permute-done | bytes 614432 | tf_op jit(solution)/shard_map/ppermute | solution.py:245
  75.1 2.3 %collective-permute-start.12 = (bf16[2,80,640]{2,1,0:T(8,128)(2,1)}, bf16[2,80,640]{2,1,0:T(8,128)(2,1)S(1)}, u32[]{:S(2)}, u32[]{:S(2)}) collective-permute-start(bf16[2,80,640]{2,1,0:T(8,128)(2,1)} %get-tuple-element.177), channel_id=1, source_target_pairs={{0,24},{2,26},{4,28},{6,30},{8,16},{10,18},{12,20},{14,22},{16,8},... | collective-permute-start | bytes 614408 | tf_op jit(solution)/shard_map/ppermute | solution.py:245
  78.8 2.2 %collective-permute-done.10 = bf16[160,640]{1,0:T(8,128)(2,1)S(1)} collective-permute-done((bf16[160,640]{1,0:T(8,128)(2,1)}, bf16[160,640]{1,0:T(8,128)(2,1)S(1)}, u32[]{:S(2)}, u32[]{:S(2)}) %collective-permute-start.10) | collective-permute-done | bytes 204832 | tf_op jit(solution)/shard_map/ppermute | solution.py:245
  80.9 7.2 %collective-permute-done.12 = bf16[2,80,640]{2,1,0:T(8,128)(2,1)S(1)} collective-permute-done((bf16[2,80,640]{2,1,0:T(8,128)(2,1)}, bf16[2,80,640]{2,1,0:T(8,128)(2,1)S(1)}, u32[]{:S(2)}, u32[]{:S(2)}) %collective-permute-start.12) | collective-permute-done | bytes 204832 | tf_op jit(solution)/shard_map/ppermute | solution.py:245
  88.1 7.2 %collective-permute-done.11 = bf16[2,80,640]{2,1,0:T(8,128)(2,1)} collective-permute-done((bf16[2,80,640]{2,1,0:T(8,128)(2,1)S(1)}, bf16[2,80,640]{2,1,0:T(8,128)(2,1)}, u32[]{:S(2)}, u32[]{:S(2)}) %collective-permute-start.11) | collective-permute-done | bytes 204832 | tf_op jit(solution)/shard_map/ppermute | solution.py:245
  99.7 2.7 %collective-permute-start.17 = (bf16[2,80,640]{2,1,0:T(8,128)(2,1)S(1)}, bf16[2,80,640]{2,1,0:T(8,128)(2,1)S(1)}, u32[]{:S(2)}, u32[]{:S(2)}) collective-permute-start(bf16[2,80,640]{2,1,0:T(8,128)(2,1)S(1)} %multiply_convert_fusion), channel_id=1, source_target_pairs={{0,24},{2,26},{4,28},{6,30},{8,16},{10,18},{12,20},{14,22},{16,8},... | collective-permute-start | bytes 614408 | tf_op jit(solution)/shard_map/ppermute | solution.py:245
  104.8 4.1 %collective-permute-done.15 = bf16[160,640]{1,0:T(8,128)(2,1)S(1)} collective-permute-done((bf16[160,640]{1,0:T(8,128)(2,1)S(1)}, bf16[160,640]{1,0:T(8,128)(2,1)S(1)}, u32[]{:S(2)}, u32[]{:S(2)}) %collective-permute-start.15) | collective-permute-done | bytes 204832 | tf_op jit(solution)/shard_map/ppermute | solution.py:245
  109.0 3.3 %collective-permute-done.17 = bf16[2,80,640]{2,1,0:T(8,128)(2,1)S(1)} collective-permute-done((bf16[2,80,640]{2,1,0:T(8,128)(2,1)S(1)}, bf16[2,80,640]{2,1,0:T(8,128)(2,1)S(1)}, u32[]{:S(2)}, u32[]{:S(2)}) %collective-permute-start.17) | collective-permute-done | bytes 204832 | tf_op jit(solution)/shard_map/ppermute | solution.py:245
  112.3 6.9 %collective-permute-done.16 = bf16[2,80,640]{2,1,0:T(8,128)(2,1)S(1)} collective-permute-done((bf16[2,80,640]{2,1,0:T(8,128)(2,1)S(1)}, bf16[2,80,640]{2,1,0:T(8,128)(2,1)S(1)}, u32[]{:S(2)}, u32[]{:S(2)}) %collective-permute-start.16) | collective-permute-done | bytes 204832 | tf_op jit(solution)/shard_map/ppermute | solution.py:245
  124.5 2.9 %collective-permute-start.26 = (bf16[2,80,640]{2,1,0:T(8,128)(2,1)S(1)}, bf16[2,80,640]{2,1,0:T(8,128)(2,1)S(1)}, u32[]{:S(2)}, u32[]{:S(2)}) collective-permute-start(bf16[2,80,640]{2,1,0:T(8,128)(2,1)S(1)} %pad_maximum_fusion.7), channel_id=1, source_target_pairs={{0,24},{2,26},{4,28},{6,30},{8,16},{10,18},{12,20},{14,22},{16,8},... | collective-permute-start | bytes 614408 | tf_op jit(solution)/shard_map/ppermute | solution.py:245
  128.0 4.7 %collective-permute-done.24 = bf16[160,640]{1,0:T(8,128)(2,1)S(1)} collective-permute-done((bf16[160,640]{1,0:T(8,128)(2,1)S(1)}, bf16[160,640]{1,0:T(8,128)(2,1)S(1)}, u32[]{:S(2)}, u32[]{:S(2)}) %collective-permute-start.24) | collective-permute-done | bytes 204832 | tf_op jit(solution)/shard_map/ppermute | solution.py:245
  132.7 5.2 %collective-permute-done.26 = bf16[2,80,640]{2,1,0:T(8,128)(2,1)S(1)} collective-permute-done((bf16[2,80,640]{2,1,0:T(8,128)(2,1)S(1)}, bf16[2,80,640]{2,1,0:T(8,128)(2,1)S(1)}, u32[]{:S(2)}, u32[]{:S(2)}) %collective-permute-start.26) | collective-permute-done | bytes 204832 | tf_op jit(solution)/shard_map/ppermute | solution.py:245
  137.9 7.5 %collective-permute-done.25 = bf16[2,80,640]{2,1,0:T(8,128)(2,1)S(1)} collective-permute-done((bf16[2,80,640]{2,1,0:T(8,128)(2,1)S(1)}, bf16[2,80,640]{2,1,0:T(8,128)(2,1)S(1)}, u32[]{:S(2)}, u32[]{:S(2)}) %collective-permute-start.25) | collective-permute-done | bytes 204832 | tf_op jit(solution)/shard_map/ppermute | solution.py:245
  149.1 6.0 %collective-permute-done.30 = bf16[2,80,640]{2,1,0:T(8,128)(2,1)S(1)} collective-permute-done((bf16[2,80,640]{2,1,0:T(8,128)(2,1)S(1)}, bf16[2,80,640]{2,1,0:T(8,128)(2,1)S(1)}, u32[]{:S(2)}, u32[]{:S(2)}) %collective-permute-start.30) | collective-permute-done | bytes 204832 | tf_op jit(solution)/shard_map/ppermute | solution.py:248
  160.4 2.6 %collective-permute-start.35 = (bf16[2,80,640]{2,1,0:T(8,128)(2,1)S(1)}, bf16[2,80,640]{2,1,0:T(8,128)(2,1)}, u32[]{:S(2)}, u32[]{:S(2)}) collective-permute-start(bf16[2,80,640]{2,1,0:T(8,128)(2,1)S(1)} %collective-permute-done.30), channel_id=1, source_target_pairs={{0,24},{2,26},{4,28},{6,30},{8,16},{10,18},{12,20},{14,22},{16,8},... | collective-permute-start | bytes 614408 | tf_op jit(solution)/shard_map/ppermute | solution.py:245
  164.9 20.1 %queries.2.refs_20_ = f32[1024,1280]{1,0:T(8,128)} custom-call(s32[4]{0:T(128)} %pad_add_fusion.spot_ref, bf16[1024,1280]{1,0:T(8,128)(2,1)} %refs_0_.1, bf16[2,2,160,640]{3,2,1,0:T(8,128)(2,1)} %bitcast.56, bf16[2,2,160,640]{3,2,1,0:T(8,128)(2,1)} %bitcast.69, bf16[2,2,160,640]{3,2,1,0:T(8,128)(2,1)} %bitcast.84, bf16[2,2,160,640]{3,2,1,0:T(8,128)(2,1)} %bitcast.85, ...), custom_call_target="tpu_custom_call" | custom-call | flops 8388608000 | bytes 12779520 | tf_op jit(solution)/shard_map/queries/pallas_call | solution.py:166
  187.3 6.1 %untranspose.1 = (bf16[2,640,640]{2,1,0:T(8,128)(2,1)}, bf16[2,640,640]{2,1,0:T(8,128)(2,1)}, bf16[2,640,640]{2,1,0:T(8,128)(2,1)}) custom-call(s32[4]{0:T(128)} %pad_add_fusion.spot_ref, bf16[2,4,2,80,640]{4,3,2,1,0:T(8,128)(2,1)} %copy-done, bf16[4,2,80,640]{3,2,1,0:T(8,128)(2,1)} %copy-done.1, bf16[2,4,2,80,640]{4,3,2,1,0:T(8,128)(2,1)} %copy-done.6, ...), custom_call_target="tpu_custom_call" | custom-call | bytes 9830400 | tf_op jit(solution)/shard_map/untranspose/pallas_call | solution.py:211
  194.6 20.4 %queries.3 = bf16[1024,1280]{1,0:T(8,128)(2,1)} custom-call(s32[4]{0:T(128)} %pad_add_fusion.spot_ref, bf16[352,1280]{1,0:T(8,128)(2,1)} %collective-permute-done.2.refs_0_, bf16[336,1280]{1,0:T(8,128)(2,1)} %copy-done.16, bf16[336,1280]{1,0:T(8,128)(2,1)} %copy-done.17, bf16[2,2,160,640]{3,2,1,0:T(8,128)(2,1)} %bitcast.64, ...), custom_call_target="tpu_custom_call" | custom-call | flops 8388608000 | bytes 12779520 | tf_op jit(solution)/shard_map/queries/pallas_call | solution.py:166
  (159 shorter events, 54.0 us)
Async XLA Ops:
  10.8 30.3 %collective-permute-start.3 = (bf16[2,640,640]{2,1,0:T(8,128)(2,1)}, bf16[2,640,640]{2,1,0:T(8,128)(2,1)}, u32[]{:S(2)}, u32[]{:S(2)}) collective-permute-start(bf16[2,640,640]{2,1,0:T(8,128)(2,1)} %get-tuple-element.94), channel_id=1, source_target_pairs={{0,2},{2,0},{4,6},{6,4},{8,10},{10,8},{12,14},{14,12},{16,18},{18,... | collective-permute-start | bytes 4915208 | tf_op jit(solution)/shard_map/ppermute | solution.py:245
  12.3 24.6 %collective-permute-start.2 = (bf16[352,1280]{1,0:T(8,128)(2,1)}, bf16[352,1280]{1,0:T(8,128)(2,1)}, u32[]{:S(2)}, u32[]{:S(2)}) collective-permute-start(bf16[352,1280]{1,0:T(8,128)(2,1)} %slice.27), channel_id=1, source_target_pairs={{0,1},{1,0},{2,3},{3,2},{4,5},{5,4},{6,7},{7,6},{8,9},{9,8},{10,11... | collective-permute-start | bytes 2703368 | tf_op jit(solution)/shard_map/ppermute | solution.py:248
  14.8 22.1 %collective-permute-start.5 = (bf16[640,640]{1,0:T(8,128)(2,1)}, bf16[640,640]{1,0:T(8,128)(2,1)}, u32[]{:S(2)}, u32[]{:S(2)}) collective-permute-start(bf16[640,640]{1,0:T(8,128)(2,1)} %get-tuple-element.96), channel_id=1, source_target_pairs={{0,2},{2,0},{4,6},{6,4},{8,10},{10,8},{12,14},{14,12},{16,18},{18,... | collective-permute-start | bytes 2457608 | tf_op jit(solution)/shard_map/ppermute | solution.py:245
  15.0 21.5 %collective-permute-start.1 = (bf16[320,640]{1,0:T(8,128)(2,1)S(1)}, bf16[320,640]{1,0:T(8,128)(2,1)S(1)}, u32[]{:S(2)}, u32[]{:S(2)}) collective-permute-start(bf16[320,640]{1,0:T(8,128)(2,1)S(1)} %bitcast.59), channel_id=1, source_target_pairs={{0,16},{2,18},{4,20},{6,22},{8,24},{10,26},{12,28},{14,30},{16,0},... | collective-permute-start | bytes 1228808 | tf_op jit(solution)/shard_map/ppermute | solution.py:245
  17.7 19.2 %collective-permute-start = (bf16[320,640]{1,0:T(8,128)(2,1)S(1)}, bf16[320,640]{1,0:T(8,128)(2,1)}, u32[]{:S(2)}, u32[]{:S(2)}) collective-permute-start(bf16[320,640]{1,0:T(8,128)(2,1)S(1)} %bitcast.60), channel_id=1, source_target_pairs={{0,8},{2,10},{4,12},{6,14},{8,0},{10,2},{12,4},{14,6},{16,24},{18,... | collective-permute-start | bytes 1228808 | tf_op jit(solution)/shard_map/ppermute | solution.py:245
  39.7 24.0 %collective-permute-start.6 = (bf16[480,640]{1,0:T(8,128)(2,1)}, bf16[480,640]{1,0:T(8,128)(2,1)}, u32[]{:S(2)}, u32[]{:S(2)}) collective-permute-start(bf16[480,640]{1,0:T(8,128)(2,1)} %pad_maximum_fusion.6), channel_id=1, source_target_pairs={{0,8},{2,10},{4,12},{6,14},{8,0},{10,2},{12,4},{14,6},{16,24},{18,... | collective-permute-start | bytes 1843208 | tf_op jit(solution)/shard_map/ppermute | solution.py:245
  42.5 24.8 %collective-permute-start.4 = (bf16[640,640]{1,0:T(8,128)(2,1)S(1)}, bf16[640,640]{1,0:T(8,128)(2,1)S(1)}, u32[]{:S(2)}, u32[]{:S(2)}) collective-permute-start(bf16[640,640]{1,0:T(8,128)(2,1)S(1)} %bitcast.72), channel_id=1, source_target_pairs={{0,4},{2,6},{4,0},{6,2},{8,12},{10,14},{12,8},{14,10},{16,20},{18,... | collective-permute-start | bytes 2457608 | tf_op jit(solution)/shard_map/ppermute | solution.py:245
  44.1 20.7 %collective-permute-start.8 = (bf16[160,640]{1,0:T(8,128)(2,1)}, bf16[160,640]{1,0:T(8,128)(2,1)S(1)}, u32[]{:S(2)}, u32[]{:S(2)}) collective-permute-start(bf16[160,640]{1,0:T(8,128)(2,1)} %get-tuple-element.174), channel_id=1, source_target_pairs={{0,24},{2,26},{4,28},{6,30},{8,16},{10,18},{12,20},{14,22},{16,8},... | collective-permute-start | bytes 614408 | tf_op jit(solution)/shard_map/ppermute | solution.py:245
  45.8 18.9 %collective-permute-start.7 = (bf16[160,640]{1,0:T(8,128)(2,1)S(1)}, bf16[160,640]{1,0:T(8,128)(2,1)S(1)}, u32[]{:S(2)}, u32[]{:S(2)}) collective-permute-start(bf16[160,640]{1,0:T(8,128)(2,1)S(1)} %get-tuple-element.175), channel_id=1, source_target_pairs={{0,16},{2,18},{4,20},{6,22},{8,24},{10,26},{12,28},{14,30},{16,0},... | collective-permute-start | bytes 614408 | tf_op jit(solution)/shard_map/ppermute | solution.py:245
  46.3 23.6 %collective-permute-start.9 = (bf16[336,1280]{1,0:T(8,128)(2,1)}, bf16[336,1280]{1,0:T(8,128)(2,1)S(1)}, u32[]{:S(2)}, u32[]{:S(2)}) collective-permute-start(bf16[336,1280]{1,0:T(8,128)(2,1)} %get-tuple-element.101), channel_id=1, source_target_pairs={{0,1},{1,0},{2,3},{3,2},{4,5},{5,4},{6,7},{7,6},{8,9},{9,8},{10,11... | collective-permute-start | bytes 2580488 | tf_op jit(solution)/shard_map/ppermute | solution.py:248
  71.1 25.7 %collective-permute-start.13 = (bf16[720,640]{1,0:T(8,128)(2,1)}, bf16[720,640]{1,0:T(8,128)(2,1)}, u32[]{:S(2)}, u32[]{:S(2)}) collective-permute-start(bf16[720,640]{1,0:T(8,128)(2,1)} %pad_maximum_fusion.1), channel_id=1, source_target_pairs={{0,4},{2,6},{4,0},{6,2},{8,12},{10,14},{12,8},{14,10},{16,20},{18,... | collective-permute-start | bytes 2764808 | tf_op jit(solution)/shard_map/ppermute | solution.py:245
  77.4 17.9 %collective-permute-start.11 = (bf16[2,80,640]{2,1,0:T(8,128)(2,1)S(1)}, bf16[2,80,640]{2,1,0:T(8,128)(2,1)}, u32[]{:S(2)}, u32[]{:S(2)}) collective-permute-start(bf16[2,80,640]{2,1,0:T(8,128)(2,1)S(1)} %get-tuple-element.178), channel_id=1, source_target_pairs={{0,16},{2,18},{4,20},{6,22},{8,24},{10,26},{12,28},{14,30},{16,0},... | collective-permute-start | bytes 614408 | tf_op jit(solution)/shard_map/ppermute | solution.py:245
  78.0 21.0 %collective-permute-start.14 = (bf16[640,640]{1,0:T(8,128)(2,1)}, bf16[640,640]{1,0:T(8,128)(2,1)S(1)}, u32[]{:S(2)}, u32[]{:S(2)}) collective-permute-start(bf16[640,640]{1,0:T(8,128)(2,1)} %get-tuple-element.106), channel_id=1, source_target_pairs={{0,1},{1,0},{2,3},{3,2},{4,5},{5,4},{6,7},{7,6},{8,9},{9,8},{10,11... | collective-permute-start | bytes 2457608 | tf_op jit(solution)/shard_map/ppermute | solution.py:248
  99.1 20.4 %collective-permute-start.18 = (bf16[720,640]{1,0:T(8,128)(2,1)S(1)}, bf16[720,640]{1,0:T(8,128)(2,1)S(1)}, u32[]{:S(2)}, u32[]{:S(2)}) collective-permute-start(bf16[720,640]{1,0:T(8,128)(2,1)S(1)} %pad_maximum_fusion.2), channel_id=1, source_target_pairs={{0,4},{2,6},{4,0},{6,2},{8,12},{10,14},{12,8},{14,10},{16,20},{18,... | collective-permute-start | bytes 2764808 | tf_op jit(solution)/shard_map/ppermute | solution.py:245
  102.3 16.8 %collective-permute-start.16 = (bf16[2,80,640]{2,1,0:T(8,128)(2,1)S(1)}, bf16[2,80,640]{2,1,0:T(8,128)(2,1)S(1)}, u32[]{:S(2)}, u32[]{:S(2)}) collective-permute-start(bf16[2,80,640]{2,1,0:T(8,128)(2,1)S(1)} %multiply_convert_fusion), channel_id=1, source_target_pairs={{0,16},{2,18},{4,20},{6,22},{8,24},{10,26},{12,28},{14,30},{16,0},... | collective-permute-start | bytes 614408 | tf_op jit(solution)/shard_map/ppermute | solution.py:245
  103.1 18.4 %collective-permute-start.19 = (bf16[336,1280]{1,0:T(8,128)(2,1)S(1)}, bf16[336,1280]{1,0:T(8,128)(2,1)S(1)}, u32[]{:S(2)}, u32[]{:S(2)}) collective-permute-start(bf16[336,1280]{1,0:T(8,128)(2,1)S(1)} %copy-done.7), channel_id=1, source_target_pairs={{0,1},{1,0},{2,3},{3,2},{4,5},{5,4},{6,7},{7,6},{8,9},{9,8},{10,11... | collective-permute-start | bytes 2580488 | tf_op jit(solution)/shard_map/ppermute | solution.py:248
  122.4 23.0 %collective-permute-start.23 = (bf16[640,640]{1,0:T(8,128)(2,1)S(1)}, bf16[640,640]{1,0:T(8,128)(2,1)S(1)}, u32[]{:S(2)}, u32[]{:S(2)}) collective-permute-start(bf16[640,640]{1,0:T(8,128)(2,1)S(1)} %bitcast.57), channel_id=1, source_target_pairs={{0,4},{2,6},{4,0},{6,2},{8,12},{10,14},{12,8},{14,10},{16,20},{18,... | collective-permute-start | bytes 2457608 | tf_op jit(solution)/shard_map/ppermute | solution.py:245
  123.9 21.5 %collective-permute-start.27 = (bf16[4,2,80,640]{3,2,1,0:T(8,128)(2,1)S(1)}, bf16[4,2,80,640]{3,2,1,0:T(8,128)(2,1)S(1)}, u32[]{:S(2)}, u32[]{:S(2)}) collective-permute-start(bf16[4,2,80,640]{3,2,1,0:T(8,128)(2,1)S(1)} %pad_maximum_fusion.4), channel_id=1, source_target_pairs={{0,1},{1,0},{2,3},{3,2},{4,5},{5,4},{6,7},{7,6},{8,9},{9,8},{10,11... | collective-permute-start | bytes 2457608 | tf_op jit(solution)/shard_map/ppermute | solution.py:248
  127.4 18.0 %collective-permute-start.25 = (bf16[2,80,640]{2,1,0:T(8,128)(2,1)S(1)}, bf16[2,80,640]{2,1,0:T(8,128)(2,1)S(1)}, u32[]{:S(2)}, u32[]{:S(2)}) collective-permute-start(bf16[2,80,640]{2,1,0:T(8,128)(2,1)S(1)} %pad_maximum_fusion.7), channel_id=1, source_target_pairs={{0,16},{2,18},{4,20},{6,22},{8,24},{10,26},{12,28},{14,30},{16,0},... | collective-permute-start | bytes 614408 | tf_op jit(solution)/shard_map/ppermute | solution.py:245
  158.2 26.9 %collective-permute-start.37 = (bf16[4,2,80,640]{3,2,1,0:T(8,128)(2,1)S(1)}, bf16[4,2,80,640]{3,2,1,0:T(8,128)(2,1)}, u32[]{:S(2)}, u32[]{:S(2)}) collective-permute-start(bf16[4,2,80,640]{3,2,1,0:T(8,128)(2,1)S(1)} %copy-done.20), channel_id=1, source_target_pairs={{0,2},{2,0},{4,6},{6,4},{8,10},{10,8},{12,14},{14,12},{16,18},{18,... | collective-permute-start | bytes 2457608 | tf_op jit(solution)/shard_map/ppermute | solution.py:245
  158.2 26.8 %collective-permute-start.32 = (bf16[640,640]{1,0:T(8,128)(2,1)S(1)}, bf16[640,640]{1,0:T(8,128)(2,1)}, u32[]{:S(2)}, u32[]{:S(2)}) collective-permute-start(bf16[640,640]{1,0:T(8,128)(2,1)S(1)} %bitcast.83), channel_id=1, source_target_pairs={{0,4},{2,6},{4,0},{6,2},{8,12},{10,14},{12,8},{14,10},{16,20},{18,... | collective-permute-start | bytes 2457608 | tf_op jit(solution)/shard_map/ppermute | solution.py:245
  159.9 25.0 %collective-permute-start.38 = (bf16[2,80,640]{2,1,0:T(8,128)(2,1)S(1)}, bf16[2,80,640]{2,1,0:T(8,128)(2,1)S(1)}, u32[]{:S(2)}, u32[]{:S(2)}) collective-permute-start(bf16[2,80,640]{2,1,0:T(8,128)(2,1)S(1)} %collective-permute-done.30), channel_id=1, source_target_pairs={{0,2},{2,0},{4,6},{6,4},{8,10},{10,8},{12,14},{14,12},{16,18},{18,... | collective-permute-start | bytes 614408 | tf_op jit(solution)/shard_map/ppermute | solution.py:245
  160.4 24.6 %collective-permute-start.35 = (bf16[2,80,640]{2,1,0:T(8,128)(2,1)S(1)}, bf16[2,80,640]{2,1,0:T(8,128)(2,1)}, u32[]{:S(2)}, u32[]{:S(2)}) collective-permute-start(bf16[2,80,640]{2,1,0:T(8,128)(2,1)S(1)} %collective-permute-done.30), channel_id=1, source_target_pairs={{0,24},{2,26},{4,28},{6,30},{8,16},{10,18},{12,20},{14,22},{16,8},... | collective-permute-start | bytes 614408 | tf_op jit(solution)/shard_map/ppermute | solution.py:245
  163.4 21.6 %collective-permute-start.34 = (bf16[2,80,640]{2,1,0:T(8,128)(2,1)S(1)}, bf16[2,80,640]{2,1,0:T(8,128)(2,1)}, u32[]{:S(2)}, u32[]{:S(2)}) collective-permute-start(bf16[2,80,640]{2,1,0:T(8,128)(2,1)S(1)} %collective-permute-done.30), channel_id=1, source_target_pairs={{0,16},{2,18},{4,20},{6,22},{8,24},{10,26},{12,28},{14,30},{16,0},... | collective-permute-start | bytes 614408 | tf_op jit(solution)/shard_map/ppermute | solution.py:245
  (49 other events, 502.9 us)

commit v3 on v2

v3 whole, which is shorter than its diff:
```python
import functools

import jax
import jax.numpy as jnp
from jax import lax
from jax.experimental import pallas as pl
from jax.experimental.pallas import tpu as pltpu
from jax.sharding import PartitionSpec as P

F32 = jnp.float32
BF16 = jnp.bfloat16
NT = (((1,), (1,)), ((), ()))
EPS = 1e-06
VMEM_BYTES = 56 * 1024 * 1024
PARAMS = pltpu.CompilerParams(vmem_limit_bytes=VMEM_BYTES, dimension_semantics=("arbitrary",))


def dot(a, b):
    return jnp.dot(a, b, preferred_element_type=F32)


def dot_nt(a, b):
    return lax.dot_general(a, b, NT, preferred_element_type=F32)


def sigmoid(x):
    return 0.5 * jnp.tanh(0.5 * x) + 0.5


def grad_kernel(far, spot_ref, k_ref, v_ref, lr_ref, win_ref, wgate_ref, wout_ref, pair_ref, out_ref, *refs):
    w_t, backs = refs[-2:]
    units = wout_ref.shape[1]
    w_t[0:units] = win_ref[0].T
    w_t[units:] = wgate_ref[0].T
    if len(refs) > 2:
        refs[0][...] = w_t[...].reshape(refs[0].shape)
        refs[1][...] = wout_ref[0].T
    k = k_ref[...]
    v = v_ref[...]
    rate = -lr_ref[pl.ds(1 - spot_ref[0] if far else spot_ref[0], 1), :]
    count = units // 2
    for lo in range(0, units, count):
        pre_in = dot_nt(w_t[lo : lo + count], k)
        pre_gate = dot_nt(w_t[units + lo : units + lo + count], k)
        back = dot_nt(wout_ref[0, lo : lo + count], v) * rate
        sig = sigmoid(pre_in)
        act = pre_in * sig
        backs[lo : lo + count] = (back * pre_gate * (sig + act * (1.0 - sig))).astype(BF16)
        backs[units + lo : units + lo + count] = (back * act).astype(BF16)
        backs[2 * units + lo : 2 * units + lo + count] = (act * pre_gate * rate).astype(BF16)
    pair_ref[...] = dot(backs[0 : 2 * units], k).astype(BF16).reshape(pair_ref.shape)
    out_ref[...] = dot(backs[2 * units :], v).T.astype(BF16)


def grads_of(spot, far, key_rows, value_rows, learn_rates, fast_in, fast_gate, fast_out):
    tokens = key_rows.shape[0]
    heads, width, units = fast_in.shape
    weight = pl.BlockSpec((1, width, units), lambda t, s: (1 - s[0] if far else s[0], 0, 0))
    rows = pl.BlockSpec((tokens, width), lambda t, s: (0, 1 - s[0] if far else s[0]))
    copies = 1 if far else 2
    return pl.pallas_call(
        functools.partial(grad_kernel, far),
        out_shape=[jax.ShapeDtypeStruct((2, units, width), BF16), jax.ShapeDtypeStruct((width, units), BF16)] * copies,
        grid_spec=pltpu.PrefetchScalarGridSpec(
            num_scalar_prefetch=1,
            grid=(1,),
            in_specs=[rows, rows, pl.BlockSpec((heads, tokens), lambda t, h: (0, 0)), weight, weight, weight],
            out_specs=[
                pl.BlockSpec((2, units, width), lambda t, h: (0, 0, 0)),
                pl.BlockSpec((width, units), lambda t, h: (0, 0)),
            ]
            * copies,
            scratch_shapes=[pltpu.VMEM((2 * units, width), BF16), pltpu.VMEM((3 * units, tokens), BF16)],
        ),
        compiler_params=PARAMS,
        cost_estimate=pl.CostEstimate(
            flops=tokens * width * units, bytes_accessed=4 * tokens * width, transcendentals=0
        ),
        name="grads",
    )(spot, key_rows, value_rows, learn_rates, fast_in, fast_gate, fast_out)


def taken(refs, counts):
    groups, at = [], 0
    for c in counts:
        groups.append(refs[at : at + c])
        at += c
    return groups


def query_kernel(counts, masks, final, spot_ref, *refs):
    *groups, rest = taken(refs, (*counts, len(refs) - sum(counts)))
    q_refs, proj_refs, weight_refs = groups[0], groups[1], groups[2:6]
    extra_ref, *outs, normed_ref, pair_scratch, out_scratch, proj_scratch, q_scratch, tail_scratch, sems = rest
    block, lanes = normed_ref.shape
    width = lanes // 2
    step = pl.program_id(0)
    upper, rank = spot_ref[1], spot_ref[2]

    def lined(start, count):
        return pl.ds(pl.multiple_of(start, count), count)

    copies = {}

    def plan(name, source, target):
        number = sum(len(c) for c in copies.values())
        copies.setdefault(name, []).append(pltpu.make_async_copy(source, target, sems.at[number]))

    at = 0
    for ref in q_refs:
        count = min(ref.shape[0], q_scratch.shape[0] - at)
        plan("q", ref.at[pl.ds(0, count)], q_scratch.at[pl.ds(at, count)])
        at += count
    if final:
        plan("q", q_refs[-1].at[pl.ds(q_refs[-1].shape[0] - 16, 16)], tail_scratch)
    for j in range(2):
        pairs = [r.at[s] for r in weight_refs[2 * j] for s in range(r.shape[0])]
        results = [r.at[s] for r in weight_refs[2 * j + 1] for s in range(r.shape[0])]
        sides, (ranks, _, piece, _) = len(pairs), pairs[0].shape
        for s in range(sides):
            for r in range(ranks):
                start = (upper ^ s) * (ranks * piece) + (rank ^ r) * piece
                plan(j, pairs[s].at[r], pair_scratch.at[j, :, lined(start, piece), :])
                start = (rank ^ r) * (sides * piece) + (upper ^ s) * piece
                plan(j, results[r].at[s], out_scratch.at[j, lined(start, piece), :])
    rows = proj_refs[0].shape[2]
    for ref, mask in zip(proj_refs, masks):
        for k, m in enumerate(mask):
            for j in range(2):
                target = proj_scratch.at[lined((spot_ref[3] ^ m) * rows, rows), pl.ds(j * width, width)]
                plan("proj", ref.at[k, j], target)

    @pl.when(step == 0)
    def _():
        for name in ("q", 0, 1, "proj"):
            for copy in copies[name]:
                copy.start()

    def arrived(*names):
        @pl.when(step == 0)
        def _():
            for name in names:
                for copy in copies[name]:
                    copy.wait()

    arrived("q", 0)
    if final:
        tail = tail_scratch[...].astype(F32)
        gains = tail[0:1] + tail[1:2] + tail[2:3]
    else:
        gains = extra_ref[...].reshape(1, lanes)
    for j in range(2):
        if j == 1:
            arrived(1)
        head = spot_ref[0] if j == 0 else 1 - spot_ref[0]
        columns = pl.ds(pl.multiple_of(head * width, 128), width)
        weights = pair_scratch[j]
        both = dot_nt(q_scratch[lined(step * block, block), columns], weights.reshape(-1, width))
        units = both.shape[1] // 2
        q_in, q_gate = both[:, :units], both[:, units:]
        hidden = (q_in * sigmoid(q_in) * q_gate).astype(BF16)
        head_out = dot_nt(hidden, out_scratch[j])
        inverse = lax.rsqrt(jnp.mean(head_out * head_out, axis=-1, keepdims=True) + EPS)
        gain = jnp.where(head == 0, gains[:, :width], gains[:, width:])
        normed_ref[:, columns] = (head_out * inverse * gain).astype(BF16)
    arrived("proj")
    total = dot_nt(normed_ref[...], proj_scratch[...])
    if final:
        total = total + extra_ref[...]
    else:
        outs[1][0] = pair_scratch[step, 0].T
        outs[2][0] = pair_scratch[step, 1].T
        outs[3][0] = out_scratch[step].T
    outs[0][...] = total.astype(outs[0].dtype)


def query_heads(spot, queries, gain, proj, masks, mine, theirs, earlier):
    final = earlier is not None
    tokens = sum(q.shape[0] for q in queries) - 16 * final
    lanes = queries[0].shape[1]
    width = units = lanes // 2
    outs = sum(len(m) for m in masks) * proj[0].shape[2]
    block = tokens // 2
    groups = (queries, proj, *mine, *theirs)
    counts = tuple(len(g) for g in groups)
    operands = [a for g in groups for a in g]
    in_specs = [pl.BlockSpec(memory_space=pl.ANY)] * len(operands)
    rows_spec = pl.BlockSpec((block, outs), lambda t, s: (t, 0))
    out_shape, out_specs = [jax.ShapeDtypeStruct((tokens, outs), BF16 if final else F32)], [rows_spec]
    if final:
        in_specs.append(rows_spec)
    else:
        in_specs.append(pl.BlockSpec(gain.shape, lambda t, s: (0,)))
        out_shape += [jax.ShapeDtypeStruct((2, width, units), BF16)] * 3
        out_specs += [pl.BlockSpec((1, width, units), lambda t, s: (t + s[0] - 2 * t * s[0], 0, 0))] * 3
    operands.append(earlier if final else gain)
    sides = sum(a.shape[0] for a in mine[0])
    ranks = sum(a.shape[0] for a in mine[1])
    copies = len(queries) + 1 + 4 * sides * ranks + 2 * sum(len(m) for m in masks)
    result = pl.pallas_call(
        functools.partial(query_kernel, counts, masks, final),
        out_shape=out_shape,
        grid_spec=pltpu.PrefetchScalarGridSpec(
            num_scalar_prefetch=1,
            grid=(tokens // block,),
            in_specs=in_specs,
            out_specs=out_specs,
            scratch_shapes=[
                pltpu.VMEM((block, lanes), BF16),
                pltpu.VMEM((2, 2, units, width), BF16),
                pltpu.VMEM((2, width, units), BF16),
                pltpu.VMEM((outs, lanes), BF16),
                pltpu.VMEM((tokens, lanes), BF16),
                pltpu.VMEM((16, lanes), BF16),
                pltpu.SemaphoreType.DMA((copies,)),
            ],
        ),
        compiler_params=PARAMS,
        cost_estimate=pl.CostEstimate(
            flops=12 * tokens * width * width + 4 * tokens * width * outs,
            bytes_accessed=4 * tokens * width + 12 * width * width + 4 * tokens * outs,
            transcendentals=0,
        ),
        name="queries",
    )(spot, *operands)
    return result[0] if final else result


def renorm(wide, grad):
    moved = wide - grad
    scale = jnp.sqrt(jnp.sum(wide * wide, axis=-1, keepdims=True) + EPS) / jnp.sqrt(
        jnp.sum(moved * moved, axis=-1, keepdims=True) + EPS
    )
    return (moved * scale).astype(BF16)


def on_device(n_ctx, n_head, key_rows, value_rows, query_rows, learn_rates, fast_in, fast_gate, fast_out, head_gain, out_proj):
    heads, width, units = fast_in.shape
    place = lax.axis_index("ctx")
    group = lax.axis_index("head")
    core, upper, rank = place % 2, (place // 2) % 2, place // 4
    ranks = n_ctx // 4
    half = units // 2
    piece = half // ranks

    def across(array, mask):
        return lax.ppermute(array, "ctx", [(j, j ^ mask) for j in range(n_ctx)])

    def over(array):
        return lax.ppermute(array, "head", [(j, j ^ 1) for j in range(n_head)])

    def part(array, start, count, axis=0):
        return lax.dynamic_slice_in_dim(array, start, count, axis)

    def joined(array, rider):
        flat = array.reshape(-1, width)
        return flat if rider is None else jnp.concatenate([flat, rider])

    def parted(array, like, rider):
        count = like.size // width
        return array[:count].reshape(like.shape), None if rider is None else array[count:]

    def to_upper(array_for, rider=None):
        array = array_for(1 - upper)
        return parted(across(joined(array, rider), 2), array, rider)

    def to_ranks(array_for, rider=None):
        sent = [array_for(rank ^ d) for d in range(1, ranks)]
        first, rider = parted(across(joined(sent[0], rider), 4), sent[0], rider)
        return [first] + [across(a, 4 * d) for d, a in enumerate(sent[1:], 2)], rider

    tie = lax.optimization_barrier
    inputs = (key_rows, value_rows, learn_rates, fast_in, fast_gate, fast_out)

    half_ctx = n_ctx // 2
    rows = out_proj.shape[1]
    stepwise = ranks == 4 and rows % 16 == 0
    tiled = piece % 16 == 0
    spot = [core, upper, rank] if tiled else [core, 0, 0]
    spot = jnp.stack(spot + [place % half_ctx if stepwise else 0]).astype(jnp.int32)

    tokens = query_rows.shape[0]
    third = tokens // 3 // 16 * 16
    cuts = (0, tokens - 2 * third, tokens - third, tokens)
    query_parts = [query_rows[a:b] for a, b in zip(cuts, cuts[1:])]
    far_parts = [over(query_parts[0])]
    high = lax.reduce_precision(head_gain, 8, 7)
    middle = lax.reduce_precision(head_gain - high, 8, 7)
    gain_rows = jnp.stack([high, middle, head_gain - high - middle]).astype(BF16)
    gain_rows = jnp.pad(gain_rows, ((0, 13), (0, 0)))

    here = (place // half_ctx) == group
    block = out_proj.T.reshape(rows, 2, width).transpose(1, 0, 2).reshape(2 * rows, width)
    if stepwise:
        blocks = [block, across(block, 4), across(block, 8)]
    else:
        pairs = []
        for j in range(half_ctx):
            low, high = (j * n_head) + 1, (j + half_ctx) * n_head
            pairs += [(low, high), (high, low)]
        swapped = lax.ppermute(out_proj.T, ("ctx", "head"), pairs)
        proj = lax.all_gather(jnp.where(here, out_proj.T, swapped), "ctx", axis=0, tiled=True)
        proj = proj.reshape(2, -1, 2, width).transpose(0, 2, 1, 3)
        blocks = []

    other = grads_of(spot, 1, *inputs)
    other, inputs, spot = tie((other, inputs, spot))
    got_pair, got_out = (across(a, 1) for a in other)
    own_pair, own_out, pair_old, out_old = grads_of(spot, 0, *inputs)
    own_pair, own_out, blocks, far_parts, query_parts = tie((own_pair, own_out, blocks, far_parts, query_parts))
    far_parts.append(over(query_parts[1]))

    def pair_sum(start, count):
        return part(own_pair, start, count, 1).astype(F32) + part(got_pair, start, count, 1).astype(F32)

    def out_sum(start, count):
        return part(own_out, start, count).astype(F32) + part(got_out, start, count).astype(F32)

    pair_got, _ = to_upper(lambda u: pair_sum(u * half, half).astype(BF16))
    out_got, rider = to_ranks(
        lambda r: out_sum(r * 2 * piece, 2 * piece).astype(BF16), blocks[2] if stepwise else None
    )
    pair_total = pair_sum(upper * half, half) + pair_got.astype(F32)
    out_total = out_sum(rank * 2 * piece, 2 * piece)
    for a in out_got:
        out_total = out_total + a.astype(F32)
    pair_sent, out_sent = pair_total.astype(BF16), out_total.astype(BF16)
    kept = given = None
    if stepwise:
        near, away = jnp.concatenate(blocks[:2]), jnp.concatenate([blocks[2], rider])
        kept, given = jnp.where(here, near, away), jnp.where(here, away, near)
    pair_sent, out_sent, kept, given, far_parts = tie((pair_sent, out_sent, kept, given, far_parts))
    pair_got, _ = to_ranks(lambda r: part(pair_sent, r * piece, piece, 1))
    out_got, kept_upper = to_upper(lambda u: part(out_sent, u * piece, piece), kept)
    come = over(given) if stepwise else None
    pair_grad = part(pair_total, rank * piece, piece, 1)
    for a in pair_got:
        pair_grad = pair_grad + a.astype(F32)
    out_grad = part(out_total, upper * piece, piece) + out_got.astype(F32)
    pair_wide = part(pair_old, upper * half + rank * piece, piece, 1).astype(F32)
    out_wide = part(out_old, rank * 2 * piece + upper * piece, piece).astype(F32)
    pair_new, out_new = renorm(pair_wide, pair_grad), renorm(out_wide, out_grad)
    pair_new, out_new, come, query_parts, kept, kept_upper = tie((pair_new, out_new, come, query_parts, kept, kept_upper))

    pair_got, _ = to_ranks(lambda r: pair_new)
    out_got, come_upper = to_upper(lambda u: out_new, come)
    far_parts.append(over(jnp.concatenate([query_parts[2], gain_rows])))
    far_new = over(out_new)
    pair_held, out_held = jnp.stack([pair_new] + pair_got), jnp.stack([out_new, out_got])
    pair_held, out_held, far_parts, far_new = tie((pair_held, out_held, far_parts, far_new))

    def finish(pair, out, beside, rider=None):
        (pair_got, rider), (out_got, _) = to_upper(lambda u: pair, rider), to_ranks(lambda r: out)
        pair_got, out_got, rider, done = tie((pair_got, out_got, rider, beside()))
        return ([pair[None], pair_got[None]], [a[None] for a in (out, *out_got)]), rider, done

    if stepwise:
        masks = [[0, 4, 2, 6], [1, 5, 3, 7]]
        own_proj = [jnp.concatenate([kept, kept_upper])]
        own_proj.append(across(own_proj[0], 1))
    else:
        masks = [[0]]
        own_proj, far_proj = [part(proj, group, 1)], [part(proj, 1 - group, 1)]
    mine, rider, far_pair = finish(pair_held, out_held, lambda: over(pair_held), far_new)
    far_out = jnp.stack([far_new, rider])
    mine = tuple([jnp.concatenate(g)] for g in mine)

    def settled(pair, out):
        if not tiled:
            side, order = jnp.arange(2) ^ upper, jnp.arange(ranks) ^ rank
            pair, out = jnp.concatenate(pair), jnp.concatenate(out)
            pair = jnp.take(jnp.take(pair, side, 0), order, 1).transpose(2, 0, 1, 3, 4).reshape(1, 1, 2, units, width)
            out = jnp.take(jnp.take(out, order, 0), side, 1).reshape(1, 1, units, width)
            pair, out = [pair], [out]
        return pair, out

    def swapped_cores(arrays):
        return [across(a, 1) for a in arrays]

    theirs = tuple(swapped_cores(g) for g in mine)
    if stepwise:
        far_proj = [jnp.concatenate([come, come_upper])]
        far_proj.append(across(far_proj[0], 1))
    mine, theirs = tie((mine, theirs))

    def blocks_of(arrays):
        return [a.reshape(-1, 2, rows, width) for a in arrays] if stepwise else arrays

    far_mine, _, ((partial, *news), far_proj) = finish(
        far_pair,
        far_out,
        lambda: (
            query_heads(
                spot, [query_rows], head_gain, blocks_of(own_proj), masks, settled(*mine), settled(*theirs), None
            ),
            far_proj,
        ),
    )
    far_theirs = tuple(swapped_cores(g) for g in far_mine)
    output = query_heads(
        spot, far_parts, None, blocks_of(far_proj), masks, settled(*far_mine), settled(*far_theirs), partial
    )
    return (output, *news)


def solution(mesh):
    return jax.shard_map(
        functools.partial(on_device, mesh.shape["ctx"], mesh.shape["head"]),
        mesh=mesh,
        in_specs=(
            P("ctx", "head"),
            P("ctx", "head"),
            P("ctx", "head"),
            P("head", "ctx"),
            P("head", None, None),
            P("head", None, None),
            P("head", None, None),
            P("head"),
            P("head", "ctx"),
        ),
        out_specs=(
            P("ctx", "head"),
            P("head", None, None),
            P("head", None, None),
            P("head", None, None),
        ),
        check_vma=False,
    )
```

time: 215 us -> 206 us (0.958)
  Pallas kernels: 67.5 us -> 61.6 us
  waiting for transfers between devices: 77.8 us -> 73.2 us
  local copies, waits for them, and re-layouts: 14 us -> 11.2 us
  other arithmetic: 14.3 us -> 16.5 us
    ppermute x7 -> x6, waiting for transfers between devices: 6.25 us -> 1.19 us  [over(): return lax.ppermute(array, 'head', [(j, j ^ 1) for j in range(n_head)])]
    pallas_call x3 -> x2, Pallas kernels: 27 us -> 22.1 us  [grads_of(): pl.pallas_call(functools.partial(grad_kernel, far), out_shape=[jax.ShapeD...]
    unnamed x61 -> x62, local copies, waits for them, and re-layouts: 6.23 us -> 4.05 us
    ppermute x36 -> x34, starting transfers between devices: 31.8 us -> 33.1 us  [across(): return lax.ppermute(array, 'ctx', [(j, j ^ mask) for j in range(n_ctx)])]
    ppermute x7 -> x6, starting transfers between devices: 8.47 us -> 7.88 us  [over(): return lax.ppermute(array, 'head', [(j, j ^ 1) for j in range(n_head)])]
    ppermute x36 -> x34, waiting for transfers between devices: 71.6 us -> 72 us  [across(): return lax.ppermute(array, 'ctx', [(j, j ^ mask) for j in range(n_ctx)])]
  transfers between devices with their start and end apart: 43 -> 40, of which waited for: 17 -> 15; matrix products, arithmetic and copies ran while one was open for 10% -> 10% of each run, Pallas kernels for 17% -> 15%
where the time goes in v3:
time: 206 us; the launch traced here: 205 us
  waiting for transfers between devices  73.2 us (36%)
  Pallas kernels  61.6 us (30%)
  starting transfers between devices  40.9 us (20%)
  other arithmetic  16.5 us (8%)
  local copies, waits for them, and re-layouts  11.2 us (5%)
    ppermute x34, waiting for transfers between devices, across(): return lax.ppermute(array, 'ctx', [(j, j ^ mask) for j in range(n_ctx)])  72 us
    pallas_call x2, Pallas kernels, query_heads(): pl.pallas_call(functools.partial(query_kernel, counts, masks, final), out...  39.5 us
    ppermute x34, starting transfers between devices, across(): return lax.ppermute(array, 'ctx', [(j, j ^ mask) for j in range(n_ctx)])  33.1 us
    pallas_call x2, Pallas kernels, grads_of(): pl.pallas_call(functools.partial(grad_kernel, far), out_shape=[jax.ShapeD...  22.1 us
    ppermute x6, starting transfers between devices, over(): return lax.ppermute(array, 'head', [(j, j ^ 1) for j in range(n_head)])  7.88 us
    convert_element_type x2, other arithmetic, on_device(): pair_sent, out_sent = (pair_total.astype(BF16), out_total.astype(BF16))  4.64 us
  transfers between devices with their start and end apart: 40, of which 15 were waited for; matrix products, arithmetic and copies ran while one was open for 10% of the time, Pallas kernels for 15%

profile of v3, /device:TPU:0, one launch (start us, length us, event | category | flops | bytes accessed | tf_op | source)
XLA Modules:
  0.0 204.9 jit_solution(4949729581324278878)
XLA Ops:
  1.3 10.6 %grads.2 = (bf16[2,640,640]{2,1,0:T(8,128)(2,1)}, bf16[640,640]{1,0:T(8,128)(2,1)}) custom-call(s32[4]{0:T(128)} %pad_add_fusion.spot_ref, bf16[1024,1280]{1,0:T(8,128)(2,1)} %k_ref.2, bf16[1024,1280]{1,0:T(8,128)(2,1)} %v_ref.2, f32[2,1024]{1,0:T(2,128)} %lr_ref.2, bf16[2,640,640]{2,1,0:T(8,128)(2,1)} %win_ref.2, bf16[2,640,640]{2,1,0:T(8,128)(2,1)} %wgate_ref.2, ...), custom_call_target="tpu_custom_call" | custom-call | flops 419430400 | bytes 2621440 | tf_op jit(solution)/shard_map/grads/pallas_call | solution.py:61
  12.3 2.1 %slice.33 = bf16[352,1280]{1,0:T(8,128)(2,1)} slice(bf16[1024,1280]{1,0:T(8,128)(2,1)} %refs_0_.1), slice={[0:352], [0:1280]} | slice | bytes 1802240 | tf_op jit(solution)/shard_map/slice | solution.py:285
  14.5 2.5 %collective-permute-start.2 = (bf16[352,1280]{1,0:T(8,128)(2,1)}, bf16[352,1280]{1,0:T(8,128)(2,1)}, u32[]{:S(2)}, u32[]{:S(2)}) collective-permute-start(bf16[352,1280]{1,0:T(8,128)(2,1)} %slice.33), channel_id=1, source_target_pairs={{0,1},{1,0},{2,3},{3,2},{4,5},{5,4},{6,7},{7,6},{8,9},{9,8},{10,11... | collective-permute-start | bytes 2703368 | tf_op jit(solution)/shard_map/ppermute | solution.py:250
  18.9 2.6 %collective-permute-start.1 = (bf16[320,640]{1,0:T(8,128)(2,1)S(1)}, bf16[320,640]{1,0:T(8,128)(2,1)S(1)}, u32[]{:S(2)}, u32[]{:S(2)}) collective-permute-start(bf16[320,640]{1,0:T(8,128)(2,1)S(1)} %bitcast.58), channel_id=1, source_target_pairs={{0,16},{2,18},{4,20},{6,22},{8,24},{10,26},{12,28},{14,30},{16,0},... | collective-permute-start | bytes 1228808 | tf_op jit(solution)/shard_map/ppermute | solution.py:247
  21.5 11.5 %grads.3 = (bf16[2,640,640]{2,1,0:T(8,128)(2,1)}, bf16[640,640]{1,0:T(8,128)(2,1)}, bf16[2,640,640]{2,1,0:T(8,128)(2,1)}, bf16[640,640]{1,0:T(8,128)(2,1)}) custom-call(s32[4]{0:T(128)} %pad_add_fusion.spot_ref, bf16[1024,1280]{1,0:T(8,128)(2,1)} %k_ref.2, bf16[1024,1280]{1,0:T(8,128)(2,1)} %v_ref.2, f32[2,1024]{1,0:T(2,128)} %lr_ref.2, ...), custom_call_target="tpu_custom_call" | custom-call | flops 419430400 | bytes 2621440 | tf_op jit(solution)/shard_map/grads/pallas_call | solution.py:61
  34.1 3.7 %collective-permute-done = bf16[320,640]{1,0:T(8,128)(2,1)} collective-permute-done((bf16[320,640]{1,0:T(8,128)(2,1)S(1)}, bf16[320,640]{1,0:T(8,128)(2,1)}, u32[]{:S(2)}, u32[]{:S(2)}) %collective-permute-start) | collective-permute-done | bytes 409632 | tf_op jit(solution)/shard_map/ppermute | solution.py:247
  37.8 2.3 %collective-permute-done.1 = bf16[320,640]{1,0:T(8,128)(2,1)S(1)} collective-permute-done((bf16[320,640]{1,0:T(8,128)(2,1)S(1)}, bf16[320,640]{1,0:T(8,128)(2,1)S(1)}, u32[]{:S(2)}, u32[]{:S(2)}) %collective-permute-start.1) | collective-permute-done | bytes 409632 | tf_op jit(solution)/shard_map/ppermute | solution.py:247
  43.5 2.2 %add_convert_fusion = bf16[2,320,640]{2,1,0:T(8,128)(2,1)} fusion(bf16[2,640,640]{2,1,0:T(8,128)(2,1)S(1)} %collective-permute-done.3, s32[]{:T(128)S(6)} %select_n.92, bf16[2,640,640]{2,1,0:T(8,128)(2,1)} %get-tuple-element.81), kind=kLoop, calls=%fused_computation.3 | loop fusion | flops 1638400 | bytes 2457604 | tf_op jit(solution)/shard_map/convert_element_type | solution.py:319
  52.0 14.1 %collective-permute-done.6 = bf16[480,640]{1,0:T(8,128)(2,1)} collective-permute-done((bf16[480,640]{1,0:T(8,128)(2,1)}, bf16[480,640]{1,0:T(8,128)(2,1)}, u32[]{:S(2)}, u32[]{:S(2)}) %collective-permute-start.6) | collective-permute-done | bytes 614432 | tf_op jit(solution)/shard_map/ppermute | solution.py:247
  70.9 2.6 %fusion.12 = (bf16[2,320,640]{2,1,0:T(8,128)(2,1)S(1)}, f32[2,320,640]{2,1,0:T(8,128)}) fusion(bf16[2,320,640]{2,1,0:T(8,128)(2,1)} %bitcast.45, bf16[2,640,640]{2,1,0:T(8,128)(2,1)S(1)} %collective-permute-done.3, s32[]{:T(128)S(6)} %select_n.91, bf16[2,640,640]{2,1,0:T(8,128)(2,1)S(1)} %copy-done.2), kind=kLoop, calls=%fused_computation.59 | loop fusion | flops 2457600 | bytes 4915204 | tf_op jit(solution)/shard_map/convert_element_type | solution.py:327
  74.4 3.4 %collective-permute-start.12 = (bf16[2,80,640]{2,1,0:T(8,128)(2,1)}, bf16[2,80,640]{2,1,0:T(8,128)(2,1)}, u32[]{:S(2)}, u32[]{:S(2)}) collective-permute-start(bf16[2,80,640]{2,1,0:T(8,128)(2,1)} %get-tuple-element.151), channel_id=1, source_target_pairs={{0,24},{2,26},{4,28},{6,30},{8,16},{10,18},{12,20},{14,22},{16,8},... | collective-permute-start | bytes 614408 | tf_op jit(solution)/shard_map/ppermute | solution.py:247
  81.7 2.9 %collective-permute-done.12 = bf16[2,80,640]{2,1,0:T(8,128)(2,1)} collective-permute-done((bf16[2,80,640]{2,1,0:T(8,128)(2,1)}, bf16[2,80,640]{2,1,0:T(8,128)(2,1)}, u32[]{:S(2)}, u32[]{:S(2)}) %collective-permute-start.12) | collective-permute-done | bytes 204832 | tf_op jit(solution)/shard_map/ppermute | solution.py:247
  84.6 9.5 %collective-permute-done.11 = bf16[2,80,640]{2,1,0:T(8,128)(2,1)} collective-permute-done((bf16[2,80,640]{2,1,0:T(8,128)(2,1)}, bf16[2,80,640]{2,1,0:T(8,128)(2,1)}, u32[]{:S(2)}, u32[]{:S(2)}) %collective-permute-start.11) | collective-permute-done | bytes 204832 | tf_op jit(solution)/shard_map/ppermute | solution.py:247
  95.9 2.8 %collective-permute-done.13 = bf16[720,640]{1,0:T(8,128)(2,1)S(1)} collective-permute-done((bf16[720,640]{1,0:T(8,128)(2,1)S(1)}, bf16[720,640]{1,0:T(8,128)(2,1)S(1)}, u32[]{:S(2)}, u32[]{:S(2)}) %collective-permute-start.13) | collective-permute-done | bytes 921632 | tf_op jit(solution)/shard_map/ppermute | solution.py:247
  104.4 3.5 %collective-permute-start.17 = (bf16[2,80,640]{2,1,0:T(8,128)(2,1)S(1)}, bf16[2,80,640]{2,1,0:T(8,128)(2,1)S(1)}, u32[]{:S(2)}, u32[]{:S(2)}) collective-permute-start(bf16[2,80,640]{2,1,0:T(8,128)(2,1)S(1)} %multiply_convert_fusion), channel_id=1, source_target_pairs={{0,24},{2,26},{4,28},{6,30},{8,16},{10,18},{12,20},{14,22},{16,8},... | collective-permute-start | bytes 614408 | tf_op jit(solution)/shard_map/ppermute | solution.py:247
  108.8 5.4 %collective-permute-done.17 = bf16[2,80,640]{2,1,0:T(8,128)(2,1)S(1)} collective-permute-done((bf16[2,80,640]{2,1,0:T(8,128)(2,1)S(1)}, bf16[2,80,640]{2,1,0:T(8,128)(2,1)S(1)}, u32[]{:S(2)}, u32[]{:S(2)}) %collective-permute-start.17) | collective-permute-done | bytes 204832 | tf_op jit(solution)/shard_map/ppermute | solution.py:247
  114.6 7.6 %collective-permute-done.16 = bf16[2,80,640]{2,1,0:T(8,128)(2,1)S(1)} collective-permute-done((bf16[2,80,640]{2,1,0:T(8,128)(2,1)S(1)}, bf16[2,80,640]{2,1,0:T(8,128)(2,1)S(1)}, u32[]{:S(2)}, u32[]{:S(2)}) %collective-permute-start.16) | collective-permute-done | bytes 204832 | tf_op jit(solution)/shard_map/ppermute | solution.py:247
  127.7 2.6 %collective-permute-start.23 = (bf16[2,80,640]{2,1,0:T(8,128)(2,1)S(1)}, bf16[2,80,640]{2,1,0:T(8,128)(2,1)S(1)}, u32[]{:S(2)}, u32[]{:S(2)}) collective-permute-start(bf16[2,80,640]{2,1,0:T(8,128)(2,1)S(1)} %pad_maximum_fusion.10), channel_id=1, source_target_pairs={{0,16},{2,18},{4,20},{6,22},{8,24},{10,26},{12,28},{14,30},{16,0},... | collective-permute-start | bytes 614408 | tf_op jit(solution)/shard_map/ppermute | solution.py:247
  130.4 13.7 %collective-permute-done.21 = bf16[720,640]{1,0:T(8,128)(2,1)S(1)} collective-permute-done((bf16[720,640]{1,0:T(8,128)(2,1)S(1)}, bf16[720,640]{1,0:T(8,128)(2,1)S(1)}, u32[]{:S(2)}, u32[]{:S(2)}) %collective-permute-start.21) | collective-permute-done | bytes 921632 | tf_op jit(solution)/shard_map/ppermute | solution.py:247
  148.3 6.1 %collective-permute-done.32.refs_6_ = bf16[4,2,80,640]{3,2,1,0:T(8,128)(2,1)S(1)} collective-permute-done((bf16[4,2,80,640]{3,2,1,0:T(8,128)(2,1)S(1)}, bf16[4,2,80,640]{3,2,1,0:T(8,128)(2,1)S(1)}, u32[]{:S(2)}, u32[]{:S(2)}) %collective-permute-start.32) | collective-permute-done | bytes 819232 | tf_op jit(solution)/shard_map/ppermute | solution.py:247
  155.4 2.3 %collective-permute-start.29 = (bf16[2,80,640]{2,1,0:T(8,128)(2,1)S(1)}, bf16[2,80,640]{2,1,0:T(8,128)(2,1)S(1)}, u32[]{:S(2)}, u32[]{:S(2)}) collective-permute-start(bf16[2,80,640]{2,1,0:T(8,128)(2,1)S(1)} %get-tuple-element.154), channel_id=1, source_target_pairs={{0,24},{2,26},{4,28},{6,30},{8,16},{10,18},{12,20},{14,22},{16,8},... | collective-permute-start | bytes 614408 | tf_op jit(solution)/shard_map/ppermute | solution.py:247
  158.9 19.6 %queries.2 = (f32[1024,1280]{1,0:T(8,128)}, bf16[2,640,640]{2,1,0:T(8,128)(2,1)}, bf16[2,640,640]{2,1,0:T(8,128)(2,1)}, bf16[2,640,640]{2,1,0:T(8,128)(2,1)}) custom-call(s32[4]{0:T(128)} %pad_add_fusion.spot_ref, bf16[1024,1280]{1,0:T(8,128)(2,1)} %refs_0_.1, bf16[4,2,160,640]{3,2,1,0:T(8,128)(2,1)} %bitcast.67, bf16[4,2,160,640]{3,2,1,0:T(8,128)(2,1)} %bitcast.76, ...), custom_call_target="tpu_custom_call" | custom-call | flops 8388608000 | bytes 12779520 | tf_op jit(solution)/shard_map/queries/pallas_call | solution.py:200
  179.8 2.6 %collective-permute-done.36.refs_13_ = bf16[1,2,80,640]{3,2,1,0:T(8,128)(2,1)S(1)} collective-permute-done((bf16[1,2,80,640]{3,2,1,0:T(8,128)(2,1)S(1)}, bf16[1,2,80,640]{3,2,1,0:T(8,128)(2,1)S(1)}, u32[]{:S(2)}, u32[]{:S(2)}) %collective-permute-start.36) | collective-permute-done | bytes 204832 | tf_op jit(solution)/shard_map/ppermute | solution.py:247
  184.8 20.0 %queries.3 = bf16[1024,1280]{1,0:T(8,128)(2,1)} custom-call(s32[4]{0:T(128)} %pad_add_fusion.spot_ref, bf16[352,1280]{1,0:T(8,128)(2,1)} %collective-permute-done.2.refs_0_, bf16[336,1280]{1,0:T(8,128)(2,1)} %copy-done.18, bf16[352,1280]{1,0:T(8,128)(2,1)} %copy-done.17, bf16[4,2,160,640]{3,2,1,0:T(8,128)(2,1)} %bitcast.56, ...), custom_call_target="tpu_custom_call" | custom-call | flops 8388608000 | bytes 12779520 | tf_op jit(solution)/shard_map/queries/pallas_call | solution.py:200
  (165 shorter events, 47.3 us)
Async XLA Ops:
  11.9 31.6 %collective-permute-start.3 = (bf16[2,640,640]{2,1,0:T(8,128)(2,1)}, bf16[2,640,640]{2,1,0:T(8,128)(2,1)S(1)}, u32[]{:S(2)}, u32[]{:S(2)}) collective-permute-start(bf16[2,640,640]{2,1,0:T(8,128)(2,1)} %get-tuple-element.82), channel_id=1, source_target_pairs={{0,2},{2,0},{4,6},{6,4},{8,10},{10,8},{12,14},{14,12},{16,18},{18,... | collective-permute-start | bytes 4915208 | tf_op jit(solution)/shard_map/ppermute | solution.py:247
  14.5 25.6 %collective-permute-start.2 = (bf16[352,1280]{1,0:T(8,128)(2,1)}, bf16[352,1280]{1,0:T(8,128)(2,1)}, u32[]{:S(2)}, u32[]{:S(2)}) collective-permute-start(bf16[352,1280]{1,0:T(8,128)(2,1)} %slice.33), channel_id=1, source_target_pairs={{0,1},{1,0},{2,3},{3,2},{4,5},{5,4},{6,7},{7,6},{8,9},{9,8},{10,11... | collective-permute-start | bytes 2703368 | tf_op jit(solution)/shard_map/ppermute | solution.py:250
  17.0 23.0 %collective-permute-start.5 = (bf16[640,640]{1,0:T(8,128)(2,1)}, bf16[640,640]{1,0:T(8,128)(2,1)}, u32[]{:S(2)}, u32[]{:S(2)}) collective-permute-start(bf16[640,640]{1,0:T(8,128)(2,1)} %get-tuple-element.84), channel_id=1, source_target_pairs={{0,2},{2,0},{4,6},{6,4},{8,10},{10,8},{12,14},{14,12},{16,18},{18,... | collective-permute-start | bytes 2457608 | tf_op jit(solution)/shard_map/ppermute | solution.py:247
  17.2 20.5 %collective-permute-start = (bf16[320,640]{1,0:T(8,128)(2,1)S(1)}, bf16[320,640]{1,0:T(8,128)(2,1)}, u32[]{:S(2)}, u32[]{:S(2)}) collective-permute-start(bf16[320,640]{1,0:T(8,128)(2,1)S(1)} %bitcast.57), channel_id=1, source_target_pairs={{0,8},{2,10},{4,12},{6,14},{8,0},{10,2},{12,4},{14,6},{16,24},{18,... | collective-permute-start | bytes 1228808 | tf_op jit(solution)/shard_map/ppermute | solution.py:247
  18.9 21.1 %collective-permute-start.1 = (bf16[320,640]{1,0:T(8,128)(2,1)S(1)}, bf16[320,640]{1,0:T(8,128)(2,1)S(1)}, u32[]{:S(2)}, u32[]{:S(2)}) collective-permute-start(bf16[320,640]{1,0:T(8,128)(2,1)S(1)} %bitcast.58), channel_id=1, source_target_pairs={{0,16},{2,18},{4,20},{6,22},{8,24},{10,26},{12,28},{14,30},{16,0},... | collective-permute-start | bytes 1228808 | tf_op jit(solution)/shard_map/ppermute | solution.py:247
  43.0 23.0 %collective-permute-start.6 = (bf16[480,640]{1,0:T(8,128)(2,1)}, bf16[480,640]{1,0:T(8,128)(2,1)}, u32[]{:S(2)}, u32[]{:S(2)}) collective-permute-start(bf16[480,640]{1,0:T(8,128)(2,1)} %pad_maximum_fusion.9), channel_id=1, source_target_pairs={{0,8},{2,10},{4,12},{6,14},{8,0},{10,2},{12,4},{14,6},{16,24},{18,... | collective-permute-start | bytes 1843208 | tf_op jit(solution)/shard_map/ppermute | solution.py:247
  45.7 24.6 %collective-permute-start.4 = (bf16[640,640]{1,0:T(8,128)(2,1)}, bf16[640,640]{1,0:T(8,128)(2,1)}, u32[]{:S(2)}, u32[]{:S(2)}) collective-permute-start(bf16[640,640]{1,0:T(8,128)(2,1)} %bitcast.8), channel_id=1, source_target_pairs={{0,4},{2,6},{4,0},{6,2},{8,12},{10,14},{12,8},{14,10},{16,20},{18,... | collective-permute-start | bytes 2457608 | tf_op jit(solution)/shard_map/ppermute | solution.py:247
  47.3 19.9 %collective-permute-start.8 = (bf16[160,640]{1,0:T(8,128)(2,1)}, bf16[160,640]{1,0:T(8,128)(2,1)S(1)}, u32[]{:S(2)}, u32[]{:S(2)}) collective-permute-start(bf16[160,640]{1,0:T(8,128)(2,1)} %get-tuple-element.148), channel_id=1, source_target_pairs={{0,24},{2,26},{4,28},{6,30},{8,16},{10,18},{12,20},{14,22},{16,8},... | collective-permute-start | bytes 614408 | tf_op jit(solution)/shard_map/ppermute | solution.py:247
  49.3 17.8 %collective-permute-start.7 = (bf16[160,640]{1,0:T(8,128)(2,1)S(1)}, bf16[160,640]{1,0:T(8,128)(2,1)S(1)}, u32[]{:S(2)}, u32[]{:S(2)}) collective-permute-start(bf16[160,640]{1,0:T(8,128)(2,1)S(1)} %get-tuple-element.149), channel_id=1, source_target_pairs={{0,16},{2,18},{4,20},{6,22},{8,24},{10,26},{12,28},{14,30},{16,0},... | collective-permute-start | bytes 614408 | tf_op jit(solution)/shard_map/ppermute | solution.py:247
  50.3 23.2 %collective-permute-start.9 = (bf16[336,1280]{1,0:T(8,128)(2,1)}, bf16[336,1280]{1,0:T(8,128)(2,1)S(1)}, u32[]{:S(2)}, u32[]{:S(2)}) collective-permute-start(bf16[336,1280]{1,0:T(8,128)(2,1)} %get-tuple-element.89), channel_id=1, source_target_pairs={{0,1},{1,0},{2,3},{3,2},{4,5},{5,4},{6,7},{7,6},{8,9},{9,8},{10,11... | collective-permute-start | bytes 2580488 | tf_op jit(solution)/shard_map/ppermute | solution.py:250
  77.8 16.3 %collective-permute-start.10 = (bf16[160,640]{1,0:T(8,128)(2,1)}, bf16[160,640]{1,0:T(8,128)(2,1)}, u32[]{:S(2)}, u32[]{:S(2)}) collective-permute-start(bf16[160,640]{1,0:T(8,128)(2,1)} %bitcast.10), channel_id=1, source_target_pairs={{0,8},{2,10},{4,12},{6,14},{8,0},{10,2},{12,4},{14,6},{16,24},{18,... | collective-permute-start | bytes 614408 | tf_op jit(solution)/shard_map/ppermute | solution.py:247
  78.9 19.7 %collective-permute-start.13 = (bf16[720,640]{1,0:T(8,128)(2,1)S(1)}, bf16[720,640]{1,0:T(8,128)(2,1)S(1)}, u32[]{:S(2)}, u32[]{:S(2)}) collective-permute-start(bf16[720,640]{1,0:T(8,128)(2,1)S(1)} %pad_maximum_fusion.2), channel_id=1, source_target_pairs={{0,4},{2,6},{4,0},{6,2},{8,12},{10,14},{12,8},{14,10},{16,20},{18,... | collective-permute-start | bytes 2764808 | tf_op jit(solution)/shard_map/ppermute | solution.py:247
  80.6 20.2 %collective-permute-start.14 = (bf16[640,640]{1,0:T(8,128)(2,1)}, bf16[640,640]{1,0:T(8,128)(2,1)S(1)}, u32[]{:S(2)}, u32[]{:S(2)}) collective-permute-start(bf16[640,640]{1,0:T(8,128)(2,1)} %get-tuple-element.94), channel_id=1, source_target_pairs={{0,1},{1,0},{2,3},{3,2},{4,5},{5,4},{6,7},{7,6},{8,9},{9,8},{10,11... | collective-permute-start | bytes 2457608 | tf_op jit(solution)/shard_map/ppermute | solution.py:250
  100.9 21.4 %collective-permute-start.18 = (bf16[720,640]{1,0:T(8,128)(2,1)S(1)}, bf16[720,640]{1,0:T(8,128)(2,1)S(1)}, u32[]{:S(2)}, u32[]{:S(2)}) collective-permute-start(bf16[720,640]{1,0:T(8,128)(2,1)S(1)} %pad_maximum_fusion.3), channel_id=1, source_target_pairs={{0,4},{2,6},{4,0},{6,2},{8,12},{10,14},{12,8},{14,10},{16,20},{18,... | collective-permute-start | bytes 2764808 | tf_op jit(solution)/shard_map/ppermute | solution.py:247
  102.7 20.8 %collective-permute-start.19 = (bf16[352,1280]{1,0:T(8,128)(2,1)S(1)}, bf16[352,1280]{1,0:T(8,128)(2,1)S(1)}, u32[]{:S(2)}, u32[]{:S(2)}) collective-permute-start(bf16[352,1280]{1,0:T(8,128)(2,1)S(1)} %pad_maximum_fusion.5), channel_id=1, source_target_pairs={{0,1},{1,0},{2,3},{3,2},{4,5},{5,4},{6,7},{7,6},{8,9},{9,8},{10,11... | collective-permute-start | bytes 2703368 | tf_op jit(solution)/shard_map/ppermute | solution.py:250
  123.6 20.5 %collective-permute-start.21 = (bf16[720,640]{1,0:T(8,128)(2,1)S(1)}, bf16[720,640]{1,0:T(8,128)(2,1)S(1)}, u32[]{:S(2)}, u32[]{:S(2)}) collective-permute-start(bf16[720,640]{1,0:T(8,128)(2,1)S(1)} %pad_maximum_fusion.4), channel_id=1, source_target_pairs={{0,4},{2,6},{4,0},{6,2},{8,12},{10,14},{12,8},{14,10},{16,20},{18,... | collective-permute-start | bytes 2764808 | tf_op jit(solution)/shard_map/ppermute | solution.py:247
  124.0 20.3 %collective-permute-start.25 = (bf16[4,2,80,640]{3,2,1,0:T(8,128)(2,1)S(1)}, bf16[4,2,80,640]{3,2,1,0:T(8,128)(2,1)}, u32[]{:S(2)}, u32[]{:S(2)}) collective-permute-start(bf16[4,2,80,640]{3,2,1,0:T(8,128)(2,1)S(1)} %pad_maximum_fusion.7), channel_id=1, source_target_pairs={{0,1},{1,0},{2,3},{3,2},{4,5},{5,4},{6,7},{7,6},{8,9},{9,8},{10,11... | collective-permute-start | bytes 2457608 | tf_op jit(solution)/shard_map/ppermute | solution.py:250
  125.7 18.5 %collective-permute-start.22 = (bf16[160,640]{1,0:T(8,128)(2,1)S(1)}, bf16[160,640]{1,0:T(8,128)(2,1)S(1)}, u32[]{:S(2)}, u32[]{:S(2)}) collective-permute-start(bf16[160,640]{1,0:T(8,128)(2,1)S(1)} %bitcast.62), channel_id=1, source_target_pairs={{0,8},{2,10},{4,12},{6,14},{8,0},{10,2},{12,4},{14,6},{16,24},{18,... | collective-permute-start | bytes 614408 | tf_op jit(solution)/shard_map/ppermute | solution.py:247
  127.7 16.5 %collective-permute-start.23 = (bf16[2,80,640]{2,1,0:T(8,128)(2,1)S(1)}, bf16[2,80,640]{2,1,0:T(8,128)(2,1)S(1)}, u32[]{:S(2)}, u32[]{:S(2)}) collective-permute-start(bf16[2,80,640]{2,1,0:T(8,128)(2,1)S(1)} %pad_maximum_fusion.10), channel_id=1, source_target_pairs={{0,16},{2,18},{4,20},{6,22},{8,24},{10,26},{12,28},{14,30},{16,0},... | collective-permute-start | bytes 614408 | tf_op jit(solution)/shard_map/ppermute | solution.py:247
  146.9 31.7 %collective-permute-start.33 = (bf16[1280,640]{1,0:T(8,128)(2,1)S(1)}, bf16[1280,640]{1,0:T(8,128)(2,1)}, u32[]{:S(2)}, u32[]{:S(2)}) collective-permute-start(bf16[1280,640]{1,0:T(8,128)(2,1)S(1)} %pad_maximum_fusion.1), channel_id=1, source_target_pairs={{0,2},{2,0},{4,6},{6,4},{8,10},{10,8},{12,14},{14,12},{16,18},{18,... | collective-permute-start | bytes 4915208 | tf_op jit(solution)/shard_map/ppermute | solution.py:247
  147.6 31.0 %collective-permute-start.26 = (bf16[640,640]{1,0:T(8,128)(2,1)}, bf16[640,640]{1,0:T(8,128)(2,1)S(1)}, u32[]{:S(2)}, u32[]{:S(2)}) collective-permute-start(bf16[640,640]{1,0:T(8,128)(2,1)} %bitcast.23), channel_id=1, source_target_pairs={{0,4},{2,6},{4,0},{6,2},{8,12},{10,14},{12,8},{14,10},{16,20},{18,... | collective-permute-start | bytes 2457608 | tf_op jit(solution)/shard_map/ppermute | solution.py:247
  154.4 24.2 %collective-permute-start.28 = (bf16[2,80,640]{2,1,0:T(8,128)(2,1)S(1)}, bf16[2,80,640]{2,1,0:T(8,128)(2,1)S(1)}, u32[]{:S(2)}, u32[]{:S(2)}) collective-permute-start(bf16[2,80,640]{2,1,0:T(8,128)(2,1)S(1)} %get-tuple-element.154), channel_id=1, source_target_pairs={{0,16},{2,18},{4,20},{6,22},{8,24},{10,26},{12,28},{14,30},{16,0},... | collective-permute-start | bytes 614408 | tf_op jit(solution)/shard_map/ppermute | solution.py:247
  155.4 23.2 %collective-permute-start.29 = (bf16[2,80,640]{2,1,0:T(8,128)(2,1)S(1)}, bf16[2,80,640]{2,1,0:T(8,128)(2,1)S(1)}, u32[]{:S(2)}, u32[]{:S(2)}) collective-permute-start(bf16[2,80,640]{2,1,0:T(8,128)(2,1)S(1)} %get-tuple-element.154), channel_id=1, source_target_pairs={{0,24},{2,26},{4,28},{6,30},{8,16},{10,18},{12,20},{14,22},{16,8},... | collective-permute-start | bytes 614408 | tf_op jit(solution)/shard_map/ppermute | solution.py:247
  157.7 20.8 %collective-permute-start.27 = (bf16[160,640]{1,0:T(8,128)(2,1)S(1)}, bf16[160,640]{1,0:T(8,128)(2,1)S(1)}, u32[]{:S(2)}, u32[]{:S(2)}) collective-permute-start(bf16[160,640]{1,0:T(8,128)(2,1)S(1)} %bitcast.75), channel_id=1, source_target_pairs={{0,8},{2,10},{4,12},{6,14},{8,0},{10,2},{12,4},{14,6},{16,24},{18,... | collective-permute-start | bytes 614408 | tf_op jit(solution)/shard_map/ppermute | solution.py:247
  (48 other events, 330.0 us)

commit v4 on v3

--- a/solution.py
+++ b/solution.py
@@ -143,26 +143,32 @@
                 for copy in copies[name]:
                     copy.wait()
 
-    arrived("q", 0)
+    arrived("q", 0, 1)
     if final:
         tail = tail_scratch[...].astype(F32)
         gains = tail[0:1] + tail[1:2] + tail[2:3]
     else:
         gains = extra_ref[...].reshape(1, lanes)
-    for j in range(2):
-        if j == 1:
-            arrived(1)
-        head = spot_ref[0] if j == 0 else 1 - spot_ref[0]
-        columns = pl.ds(pl.multiple_of(head * width, 128), width)
-        weights = pair_scratch[j]
-        both = dot_nt(q_scratch[lined(step * block, block), columns], weights.reshape(-1, width))
-        units = both.shape[1] // 2
-        q_in, q_gate = both[:, :units], both[:, units:]
-        hidden = (q_in * sigmoid(q_in) * q_gate).astype(BF16)
-        head_out = dot_nt(hidden, out_scratch[j])
-        inverse = lax.rsqrt(jnp.mean(head_out * head_out, axis=-1, keepdims=True) + EPS)
-        gain = jnp.where(head == 0, gains[:, :width], gains[:, width:])
-        normed_ref[:, columns] = (head_out * inverse * gain).astype(BF16)
+    units = out_scratch.shape[2]
+    count = block // 2
+    tasks = [(lo, j) for lo in range(0, block, count) for j in range(2)]
+    heads = (spot_ref[0], 1 - spot_ref[0])
+    columns = [pl.ds(pl.multiple_of(h * width, 128), width) for h in heads]
+    both, head_out = {}, {}
+    for i in range(len(tasks) + 2):
+        if i < len(tasks):
+            lo, j = tasks[i]
+            q = q_scratch[lined(step * block + lo, count), columns[j]]
+            both[i] = dot_nt(q, pair_scratch[j].reshape(-1, width))
+        if 0 <= i - 1 < len(tasks):
+            q_in, q_gate = both[i - 1][:, :units], both[i - 1][:, units:]
+            hidden = (q_in * sigmoid(q_in) * q_gate).astype(BF16)
+            head_out[i - 1] = dot_nt(hidden, out_scratch[tasks[i - 1][1]])
+        if i >= 2:
+            (lo, j), result = tasks[i - 2], head_out[i - 2]
+            inverse = lax.rsqrt(jnp.mean(result * result, axis=-1, keepdims=True) + EPS)
+            gain = jnp.where(heads[j] == 0, gains[:, :width], gains[:, width:])
+            normed_ref[lo : lo + count, columns[j]] = (result * inverse * gain).astype(BF16)
     arrived("proj")
     total = dot_nt(normed_ref[...], proj_scratch[...])
     if final:
@@ -347,13 +353,6 @@
     far_parts.append(over(jnp.concatenate([query_parts[2], gain_rows])))
     far_new = over(out_new)
     pair_held, out_held = jnp.stack([pair_new] + pair_got), jnp.stack([out_new, out_got])
-    pair_held, out_held, far_parts, far_new = tie((pair_held, out_held, far_parts, far_new))
-
-    def finish(pair, out, beside, rider=None):
-        (pair_got, rider), (out_got, _) = to_upper(lambda u: pair, rider), to_ranks(lambda r: out)
-        pair_got, out_got, rider, done = tie((pair_got, out_got, rider, beside()))
-        return ([pair[None], pair_got[None]], [a[None] for a in (out, *out_got)]), rider, done
-
     if stepwise:
         masks = [[0, 4, 2, 6], [1, 5, 3, 7]]
         own_proj = [jnp.concatenate([kept, kept_upper])]
@@ -361,6 +360,13 @@
     else:
         masks = [[0]]
         own_proj, far_proj = [part(proj, group, 1)], [part(proj, 1 - group, 1)]
+    pair_held, out_held, far_parts, far_new = tie((pair_held, out_held, far_parts, far_new))
+
+    def finish(pair, out, beside, rider=None):
+        (pair_got, rider), (out_got, _) = to_upper(lambda u: pair, rider), to_ranks(lambda r: out)
+        pair_got, out_got, rider, done = tie((pair_got, out_got, rider, beside()))
+        return ([pair[None], pair_got[None]], [a[None] for a in (out, *out_got)]), rider, done
+
     mine, rider, far_pair = finish(pair_held, out_held, lambda: over(pair_held), far_new)
     far_out = jnp.stack([far_new, rider])
     mine = tuple([jnp.concatenate(g)] for g in mine)
@@ -378,10 +384,10 @@
         return [across(a, 1) for a in arrays]
 
     theirs = tuple(swapped_cores(g) for g in mine)
+    mine, theirs, come, come_upper = tie((mine, theirs, come, come_upper))
     if stepwise:
         far_proj = [jnp.concatenate([come, come_upper])]
         far_proj.append(across(far_proj[0], 1))
-    mine, theirs = tie((mine, theirs))
 
     def blocks_of(arrays):
         return [a.reshape(-1, 2, rows, width) for a in arrays] if stepwise else arrays

time: 206 us -> 201 us (0.976)
  waiting for transfers between devices: 73.2 us -> 69.8 us
  Pallas kernels: 61.6 us -> 59.1 us
    ppermute x34, waiting for transfers between devices: 72 us -> 68.6 us  [across(): return lax.ppermute(array, 'ctx', [(j, j ^ mask) for j in range(n_ctx)])]
    pallas_call x2, Pallas kernels: 39.5 us -> 37 us  [query_heads(): pl.pallas_call(functools.partial(query_kernel, counts, masks, final), out...]
    unnamed x62 -> x67, local copies, waits for them, and re-layouts: 4.05 us -> 4.75 us
  transfers between devices with their start and end apart: 40 -> 40, of which waited for: 15 -> 15; matrix products, arithmetic and copies ran while one was open for 10% -> 11% of each run, Pallas kernels for 15% -> 15%
where the time goes in v4:
time: 201 us; the launch traced here: 200 us
  waiting for transfers between devices  69.8 us (35%)
  Pallas kernels  59.1 us (29%)
  starting transfers between devices  41.3 us (21%)
  other arithmetic  16.5 us (8%)
  local copies, waits for them, and re-layouts  11.9 us (6%)
    ppermute x34, waiting for transfers between devices, across(): return lax.ppermute(array, 'ctx', [(j, j ^ mask) for j in range(n_ctx)])  68.6 us
    pallas_call x2, Pallas kernels, query_heads(): pl.pallas_call(functools.partial(query_kernel, counts, masks, final), out...  37 us
    ppermute x34, starting transfers between devices, across(): return lax.ppermute(array, 'ctx', [(j, j ^ mask) for j in range(n_ctx)])  33.5 us
    pallas_call x2, Pallas kernels, grads_of(): pl.pallas_call(functools.partial(grad_kernel, far), out_shape=[jax.ShapeD...  22.1 us
    ppermute x6, starting transfers between devices, over(): return lax.ppermute(array, 'head', [(j, j ^ 1) for j in range(n_head)])  7.88 us
    unnamed x67, local copies, waits for them, and re-layouts  4.75 us
    convert_element_type x2, other arithmetic, on_device(): pair_sent, out_sent = (pair_total.astype(BF16), out_total.astype(BF16))  4.66 us
  transfers between devices with their start and end apart: 40, of which 15 were waited for; matrix products, arithmetic and copies ran while one was open for 11% of the time, Pallas kernels for 15%

profile of v4, /device:TPU:0, one launch (start us, length us, event | category | flops | bytes accessed | tf_op | source)
XLA Modules:
  0.0 200.0 jit_solution(1012890683190508504)
XLA Ops:
  1.3 10.6 %grads.2 = (bf16[2,640,640]{2,1,0:T(8,128)(2,1)}, bf16[640,640]{1,0:T(8,128)(2,1)}) custom-call(s32[4]{0:T(128)} %pad_add_fusion.spot_ref, bf16[1024,1280]{1,0:T(8,128)(2,1)} %k_ref.2, bf16[1024,1280]{1,0:T(8,128)(2,1)} %v_ref.2, f32[2,1024]{1,0:T(2,128)} %lr_ref.2, bf16[2,640,640]{2,1,0:T(8,128)(2,1)} %win_ref.2, bf16[2,640,640]{2,1,0:T(8,128)(2,1)} %wgate_ref.2, ...), custom_call_target="tpu_custom_call" | custom-call | flops 419430400 | bytes 2621440 | tf_op jit(solution)/shard_map/grads/pallas_call | solution.py:61
  12.4 2.1 %slice.33 = bf16[352,1280]{1,0:T(8,128)(2,1)} slice(bf16[1024,1280]{1,0:T(8,128)(2,1)} %refs_0_.1), slice={[0:352], [0:1280]} | slice | bytes 1802240 | tf_op jit(solution)/shard_map/slice | solution.py:291
  14.5 2.5 %collective-permute-start.2 = (bf16[352,1280]{1,0:T(8,128)(2,1)}, bf16[352,1280]{1,0:T(8,128)(2,1)}, u32[]{:S(2)}, u32[]{:S(2)}) collective-permute-start(bf16[352,1280]{1,0:T(8,128)(2,1)} %slice.33), channel_id=1, source_target_pairs={{0,1},{1,0},{2,3},{3,2},{4,5},{5,4},{6,7},{7,6},{8,9},{9,8},{10,11... | collective-permute-start | bytes 2703368 | tf_op jit(solution)/shard_map/ppermute | solution.py:256
  18.9 2.6 %collective-permute-start.1 = (bf16[320,640]{1,0:T(8,128)(2,1)S(1)}, bf16[320,640]{1,0:T(8,128)(2,1)S(1)}, u32[]{:S(2)}, u32[]{:S(2)}) collective-permute-start(bf16[320,640]{1,0:T(8,128)(2,1)S(1)} %bitcast.57), channel_id=1, source_target_pairs={{0,16},{2,18},{4,20},{6,22},{8,24},{10,26},{12,28},{14,30},{16,0},... | collective-permute-start | bytes 1228808 | tf_op jit(solution)/shard_map/ppermute | solution.py:253
  21.5 11.5 %grads.3 = (bf16[2,640,640]{2,1,0:T(8,128)(2,1)}, bf16[640,640]{1,0:T(8,128)(2,1)}, bf16[2,640,640]{2,1,0:T(8,128)(2,1)}, bf16[640,640]{1,0:T(8,128)(2,1)}) custom-call(s32[4]{0:T(128)} %pad_add_fusion.spot_ref, bf16[1024,1280]{1,0:T(8,128)(2,1)} %k_ref.2, bf16[1024,1280]{1,0:T(8,128)(2,1)} %v_ref.2, f32[2,1024]{1,0:T(2,128)} %lr_ref.2, ...), custom_call_target="tpu_custom_call" | custom-call | flops 419430400 | bytes 2621440 | tf_op jit(solution)/shard_map/grads/pallas_call | solution.py:61
  34.1 3.7 %collective-permute-done = bf16[320,640]{1,0:T(8,128)(2,1)} collective-permute-done((bf16[320,640]{1,0:T(8,128)(2,1)S(1)}, bf16[320,640]{1,0:T(8,128)(2,1)}, u32[]{:S(2)}, u32[]{:S(2)}) %collective-permute-start) | collective-permute-done | bytes 409632 | tf_op jit(solution)/shard_map/ppermute | solution.py:253
  37.8 2.3 %collective-permute-done.1 = bf16[320,640]{1,0:T(8,128)(2,1)S(1)} collective-permute-done((bf16[320,640]{1,0:T(8,128)(2,1)S(1)}, bf16[320,640]{1,0:T(8,128)(2,1)S(1)}, u32[]{:S(2)}, u32[]{:S(2)}) %collective-permute-start.1) | collective-permute-done | bytes 409632 | tf_op jit(solution)/shard_map/ppermute | solution.py:253
  40.1 2.1 %add_convert_fusion.3 = (bf16[160,640]{1,0:T(8,128)(2,1)S(1)}, bf16[160,640]{1,0:T(8,128)(2,1)}, bf16[160,640]{1,0:T(8,128)(2,1)S(1)}) fusion(bf16[640,640]{1,0:T(8,128)(2,1)} %collective-permute-done.5, s32[]{:T(128)S(6)} %select_n.95, bf16[640,640]{1,0:T(8,128)(2,1)S(1)} %copy-done.9, s32[]{:T(128)S(6)} %select_n.97, s32[]{:T(128)S(6)} %select_n.96), kind=kLoop, calls=%fused_computation.25 | loop fusion | flops 1228800 | bytes 1843212 | tf_op jit(solution)/shard_map/convert_element_type | solution.py:327
  43.6 2.2 %add_convert_fusion = bf16[2,320,640]{2,1,0:T(8,128)(2,1)} fusion(bf16[2,640,640]{2,1,0:T(8,128)(2,1)S(1)} %collective-permute-done.3, s32[]{:T(128)S(6)} %select_n.92, bf16[2,640,640]{2,1,0:T(8,128)(2,1)} %get-tuple-element.83), kind=kLoop, calls=%fused_computation.2 | loop fusion | flops 1638400 | bytes 2457604 | tf_op jit(solution)/shard_map/convert_element_type | solution.py:325
  52.1 14.1 %collective-permute-done.6 = bf16[480,640]{1,0:T(8,128)(2,1)} collective-permute-done((bf16[480,640]{1,0:T(8,128)(2,1)}, bf16[480,640]{1,0:T(8,128)(2,1)}, u32[]{:S(2)}, u32[]{:S(2)}) %collective-permute-start.6) | collective-permute-done | bytes 614432 | tf_op jit(solution)/shard_map/ppermute | solution.py:253
  71.0 2.6 %fusion.12 = (bf16[2,320,640]{2,1,0:T(8,128)(2,1)S(1)}, f32[2,320,640]{2,1,0:T(8,128)}) fusion(bf16[2,320,640]{2,1,0:T(8,128)(2,1)} %bitcast.45, bf16[2,640,640]{2,1,0:T(8,128)(2,1)S(1)} %collective-permute-done.3, s32[]{:T(128)S(6)} %select_n.91, bf16[2,640,640]{2,1,0:T(8,128)(2,1)S(1)} %copy-done.3), kind=kLoop, calls=%fused_computation.60 | loop fusion | flops 2457600 | bytes 4915204 | tf_op jit(solution)/shard_map/convert_element_type | solution.py:333
  74.5 3.4 %collective-permute-start.12 = (bf16[2,80,640]{2,1,0:T(8,128)(2,1)}, bf16[2,80,640]{2,1,0:T(8,128)(2,1)}, u32[]{:S(2)}, u32[]{:S(2)}) collective-permute-start(bf16[2,80,640]{2,1,0:T(8,128)(2,1)} %get-tuple-element.155), channel_id=1, source_target_pairs={{0,24},{2,26},{4,28},{6,30},{8,16},{10,18},{12,20},{14,22},{16,8},... | collective-permute-start | bytes 614408 | tf_op jit(solution)/shard_map/ppermute | solution.py:253
  81.7 2.9 %collective-permute-done.12 = bf16[2,80,640]{2,1,0:T(8,128)(2,1)} collective-permute-done((bf16[2,80,640]{2,1,0:T(8,128)(2,1)}, bf16[2,80,640]{2,1,0:T(8,128)(2,1)}, u32[]{:S(2)}, u32[]{:S(2)}) %collective-permute-start.12) | collective-permute-done | bytes 204832 | tf_op jit(solution)/shard_map/ppermute | solution.py:253
  84.7 9.5 %collective-permute-done.11 = bf16[2,80,640]{2,1,0:T(8,128)(2,1)} collective-permute-done((bf16[2,80,640]{2,1,0:T(8,128)(2,1)}, bf16[2,80,640]{2,1,0:T(8,128)(2,1)}, u32[]{:S(2)}, u32[]{:S(2)}) %collective-permute-start.11) | collective-permute-done | bytes 204832 | tf_op jit(solution)/shard_map/ppermute | solution.py:253
  95.9 2.8 %collective-permute-done.13 = bf16[720,640]{1,0:T(8,128)(2,1)S(1)} collective-permute-done((bf16[720,640]{1,0:T(8,128)(2,1)S(1)}, bf16[720,640]{1,0:T(8,128)(2,1)S(1)}, u32[]{:S(2)}, u32[]{:S(2)}) %collective-permute-start.13) | collective-permute-done | bytes 921632 | tf_op jit(solution)/shard_map/ppermute | solution.py:253
  104.5 3.5 %collective-permute-start.17 = (bf16[2,80,640]{2,1,0:T(8,128)(2,1)S(1)}, bf16[2,80,640]{2,1,0:T(8,128)(2,1)S(1)}, u32[]{:S(2)}, u32[]{:S(2)}) collective-permute-start(bf16[2,80,640]{2,1,0:T(8,128)(2,1)S(1)} %multiply_convert_fusion), channel_id=1, source_target_pairs={{0,24},{2,26},{4,28},{6,30},{8,16},{10,18},{12,20},{14,22},{16,8},... | collective-permute-start | bytes 614408 | tf_op jit(solution)/shard_map/ppermute | solution.py:253
  108.8 5.4 %collective-permute-done.17 = bf16[2,80,640]{2,1,0:T(8,128)(2,1)S(1)} collective-permute-done((bf16[2,80,640]{2,1,0:T(8,128)(2,1)S(1)}, bf16[2,80,640]{2,1,0:T(8,128)(2,1)S(1)}, u32[]{:S(2)}, u32[]{:S(2)}) %collective-permute-start.17) | collective-permute-done | bytes 204832 | tf_op jit(solution)/shard_map/ppermute | solution.py:253
  114.7 7.6 %collective-permute-done.16 = bf16[2,80,640]{2,1,0:T(8,128)(2,1)S(1)} collective-permute-done((bf16[2,80,640]{2,1,0:T(8,128)(2,1)S(1)}, bf16[2,80,640]{2,1,0:T(8,128)(2,1)S(1)}, u32[]{:S(2)}, u32[]{:S(2)}) %collective-permute-start.16) | collective-permute-done | bytes 204832 | tf_op jit(solution)/shard_map/ppermute | solution.py:253
  127.8 2.6 %collective-permute-start.23 = (bf16[2,80,640]{2,1,0:T(8,128)(2,1)S(1)}, bf16[2,80,640]{2,1,0:T(8,128)(2,1)S(1)}, u32[]{:S(2)}, u32[]{:S(2)}) collective-permute-start(bf16[2,80,640]{2,1,0:T(8,128)(2,1)S(1)} %pad_maximum_fusion.9), channel_id=1, source_target_pairs={{0,16},{2,18},{4,20},{6,22},{8,24},{10,26},{12,28},{14,30},{16,0},... | collective-permute-start | bytes 614408 | tf_op jit(solution)/shard_map/ppermute | solution.py:253
  130.4 13.8 %collective-permute-done.21 = bf16[720,640]{1,0:T(8,128)(2,1)S(1)} collective-permute-done((bf16[720,640]{1,0:T(8,128)(2,1)S(1)}, bf16[720,640]{1,0:T(8,128)(2,1)S(1)}, u32[]{:S(2)}, u32[]{:S(2)}) %collective-permute-start.21) | collective-permute-done | bytes 921632 | tf_op jit(solution)/shard_map/ppermute | solution.py:253
  147.3 2.5 %collective-permute-done.32.refs_6_ = bf16[4,2,80,640]{3,2,1,0:T(8,128)(2,1)S(1)} collective-permute-done((bf16[4,2,80,640]{3,2,1,0:T(8,128)(2,1)S(1)}, bf16[4,2,80,640]{3,2,1,0:T(8,128)(2,1)S(1)}, u32[]{:S(2)}, u32[]{:S(2)}) %collective-permute-start.32) | collective-permute-done | bytes 819232 | tf_op jit(solution)/shard_map/ppermute | solution.py:253
  156.5 18.3 %queries.2 = (f32[1024,1280]{1,0:T(8,128)}, bf16[2,640,640]{2,1,0:T(8,128)(2,1)}, bf16[2,640,640]{2,1,0:T(8,128)(2,1)}, bf16[2,640,640]{2,1,0:T(8,128)(2,1)}) custom-call(s32[4]{0:T(128)} %pad_add_fusion.spot_ref, bf16[1024,1280]{1,0:T(8,128)(2,1)} %refs_0_.1, bf16[4,2,160,640]{3,2,1,0:T(8,128)(2,1)} %bitcast.66, bf16[4,2,160,640]{3,2,1,0:T(8,128)(2,1)} %bitcast.77, ...), custom_call_target="tpu_custom_call" | custom-call | flops 8388608000 | bytes 12779520 | tf_op jit(solution)/shard_map/queries/pallas_call | solution.py:206
  176.2 2.6 %collective-permute-done.36.refs_13_ = bf16[1,2,80,640]{3,2,1,0:T(8,128)(2,1)S(1)} collective-permute-done((bf16[1,2,80,640]{3,2,1,0:T(8,128)(2,1)S(1)}, bf16[1,2,80,640]{3,2,1,0:T(8,128)(2,1)S(1)}, u32[]{:S(2)}, u32[]{:S(2)}) %collective-permute-start.36) | collective-permute-done | bytes 204832 | tf_op jit(solution)/shard_map/ppermute | solution.py:253
  181.1 18.7 %queries.3 = bf16[1024,1280]{1,0:T(8,128)(2,1)} custom-call(s32[4]{0:T(128)} %pad_add_fusion.spot_ref, bf16[352,1280]{1,0:T(8,128)(2,1)} %collective-permute-done.2.refs_0_, bf16[336,1280]{1,0:T(8,128)(2,1)} %copy-done.20, bf16[352,1280]{1,0:T(8,128)(2,1)} %copy-done.19, bf16[4,2,160,640]{3,2,1,0:T(8,128)(2,1)} %bitcast.67, ...), custom_call_target="tpu_custom_call" | custom-call | flops 8388608000 | bytes 12779520 | tf_op jit(solution)/shard_map/queries/pallas_call | solution.py:206
  (171 shorter events, 48.5 us)
Async XLA Ops:
  11.9 31.6 %collective-permute-start.3 = (bf16[2,640,640]{2,1,0:T(8,128)(2,1)}, bf16[2,640,640]{2,1,0:T(8,128)(2,1)S(1)}, u32[]{:S(2)}, u32[]{:S(2)}) collective-permute-start(bf16[2,640,640]{2,1,0:T(8,128)(2,1)} %get-tuple-element.84), channel_id=1, source_target_pairs={{0,2},{2,0},{4,6},{6,4},{8,10},{10,8},{12,14},{14,12},{16,18},{18,... | collective-permute-start | bytes 4915208 | tf_op jit(solution)/shard_map/ppermute | solution.py:253
  14.5 25.6 %collective-permute-start.2 = (bf16[352,1280]{1,0:T(8,128)(2,1)}, bf16[352,1280]{1,0:T(8,128)(2,1)}, u32[]{:S(2)}, u32[]{:S(2)}) collective-permute-start(bf16[352,1280]{1,0:T(8,128)(2,1)} %slice.33), channel_id=1, source_target_pairs={{0,1},{1,0},{2,3},{3,2},{4,5},{5,4},{6,7},{7,6},{8,9},{9,8},{10,11... | collective-permute-start | bytes 2703368 | tf_op jit(solution)/shard_map/ppermute | solution.py:256
  17.1 23.0 %collective-permute-start.5 = (bf16[640,640]{1,0:T(8,128)(2,1)}, bf16[640,640]{1,0:T(8,128)(2,1)}, u32[]{:S(2)}, u32[]{:S(2)}) collective-permute-start(bf16[640,640]{1,0:T(8,128)(2,1)} %get-tuple-element.86), channel_id=1, source_target_pairs={{0,2},{2,0},{4,6},{6,4},{8,10},{10,8},{12,14},{14,12},{16,18},{18,... | collective-permute-start | bytes 2457608 | tf_op jit(solution)/shard_map/ppermute | solution.py:253
  17.3 20.5 %collective-permute-start = (bf16[320,640]{1,0:T(8,128)(2,1)S(1)}, bf16[320,640]{1,0:T(8,128)(2,1)}, u32[]{:S(2)}, u32[]{:S(2)}) collective-permute-start(bf16[320,640]{1,0:T(8,128)(2,1)S(1)} %bitcast.56), channel_id=1, source_target_pairs={{0,8},{2,10},{4,12},{6,14},{8,0},{10,2},{12,4},{14,6},{16,24},{18,... | collective-permute-start | bytes 1228808 | tf_op jit(solution)/shard_map/ppermute | solution.py:253
  18.9 21.2 %collective-permute-start.1 = (bf16[320,640]{1,0:T(8,128)(2,1)S(1)}, bf16[320,640]{1,0:T(8,128)(2,1)S(1)}, u32[]{:S(2)}, u32[]{:S(2)}) collective-permute-start(bf16[320,640]{1,0:T(8,128)(2,1)S(1)} %bitcast.57), channel_id=1, source_target_pairs={{0,16},{2,18},{4,20},{6,22},{8,24},{10,26},{12,28},{14,30},{16,0},... | collective-permute-start | bytes 1228808 | tf_op jit(solution)/shard_map/ppermute | solution.py:253
  43.1 23.0 %collective-permute-start.6 = (bf16[480,640]{1,0:T(8,128)(2,1)}, bf16[480,640]{1,0:T(8,128)(2,1)}, u32[]{:S(2)}, u32[]{:S(2)}) collective-permute-start(bf16[480,640]{1,0:T(8,128)(2,1)} %pad_maximum_fusion.8), channel_id=1, source_target_pairs={{0,8},{2,10},{4,12},{6,14},{8,0},{10,2},{12,4},{14,6},{16,24},{18,... | collective-permute-start | bytes 1843208 | tf_op jit(solution)/shard_map/ppermute | solution.py:253
  45.8 24.7 %collective-permute-start.4 = (bf16[640,640]{1,0:T(8,128)(2,1)}, bf16[640,640]{1,0:T(8,128)(2,1)}, u32[]{:S(2)}, u32[]{:S(2)}) collective-permute-start(bf16[640,640]{1,0:T(8,128)(2,1)} %bitcast.8), channel_id=1, source_target_pairs={{0,4},{2,6},{4,0},{6,2},{8,12},{10,14},{12,8},{14,10},{16,20},{18,... | collective-permute-start | bytes 2457608 | tf_op jit(solution)/shard_map/ppermute | solution.py:253
  47.3 19.9 %collective-permute-start.8 = (bf16[160,640]{1,0:T(8,128)(2,1)}, bf16[160,640]{1,0:T(8,128)(2,1)S(1)}, u32[]{:S(2)}, u32[]{:S(2)}) collective-permute-start(bf16[160,640]{1,0:T(8,128)(2,1)} %get-tuple-element.152), channel_id=1, source_target_pairs={{0,24},{2,26},{4,28},{6,30},{8,16},{10,18},{12,20},{14,22},{16,8},... | collective-permute-start | bytes 614408 | tf_op jit(solution)/shard_map/ppermute | solution.py:253
  49.3 17.8 %collective-permute-start.7 = (bf16[160,640]{1,0:T(8,128)(2,1)S(1)}, bf16[160,640]{1,0:T(8,128)(2,1)S(1)}, u32[]{:S(2)}, u32[]{:S(2)}) collective-permute-start(bf16[160,640]{1,0:T(8,128)(2,1)S(1)} %get-tuple-element.153), channel_id=1, source_target_pairs={{0,16},{2,18},{4,20},{6,22},{8,24},{10,26},{12,28},{14,30},{16,0},... | collective-permute-start | bytes 614408 | tf_op jit(solution)/shard_map/ppermute | solution.py:253
  50.4 23.2 %collective-permute-start.9 = (bf16[336,1280]{1,0:T(8,128)(2,1)}, bf16[336,1280]{1,0:T(8,128)(2,1)S(1)}, u32[]{:S(2)}, u32[]{:S(2)}) collective-permute-start(bf16[336,1280]{1,0:T(8,128)(2,1)} %get-tuple-element.91), channel_id=1, source_target_pairs={{0,1},{1,0},{2,3},{3,2},{4,5},{5,4},{6,7},{7,6},{8,9},{9,8},{10,11... | collective-permute-start | bytes 2580488 | tf_op jit(solution)/shard_map/ppermute | solution.py:256
  77.9 16.3 %collective-permute-start.11 = (bf16[2,80,640]{2,1,0:T(8,128)(2,1)}, bf16[2,80,640]{2,1,0:T(8,128)(2,1)}, u32[]{:S(2)}, u32[]{:S(2)}) collective-permute-start(bf16[2,80,640]{2,1,0:T(8,128)(2,1)} %get-tuple-element.156), channel_id=1, source_target_pairs={{0,16},{2,18},{4,20},{6,22},{8,24},{10,26},{12,28},{14,30},{16,0},... | collective-permute-start | bytes 614408 | tf_op jit(solution)/shard_map/ppermute | solution.py:253
  79.0 19.7 %collective-permute-start.13 = (bf16[720,640]{1,0:T(8,128)(2,1)S(1)}, bf16[720,640]{1,0:T(8,128)(2,1)S(1)}, u32[]{:S(2)}, u32[]{:S(2)}) collective-permute-start(bf16[720,640]{1,0:T(8,128)(2,1)S(1)} %pad_maximum_fusion.1), channel_id=1, source_target_pairs={{0,4},{2,6},{4,0},{6,2},{8,12},{10,14},{12,8},{14,10},{16,20},{18,... | collective-permute-start | bytes 2764808 | tf_op jit(solution)/shard_map/ppermute | solution.py:253
  80.7 20.2 %collective-permute-start.14 = (bf16[640,640]{1,0:T(8,128)(2,1)}, bf16[640,640]{1,0:T(8,128)(2,1)S(1)}, u32[]{:S(2)}, u32[]{:S(2)}) collective-permute-start(bf16[640,640]{1,0:T(8,128)(2,1)} %get-tuple-element.96), channel_id=1, source_target_pairs={{0,1},{1,0},{2,3},{3,2},{4,5},{5,4},{6,7},{7,6},{8,9},{9,8},{10,11... | collective-permute-start | bytes 2457608 | tf_op jit(solution)/shard_map/ppermute | solution.py:256
  101.0 21.4 %collective-permute-start.18 = (bf16[720,640]{1,0:T(8,128)(2,1)S(1)}, bf16[720,640]{1,0:T(8,128)(2,1)S(1)}, u32[]{:S(2)}, u32[]{:S(2)}) collective-permute-start(bf16[720,640]{1,0:T(8,128)(2,1)S(1)} %pad_maximum_fusion.2), channel_id=1, source_target_pairs={{0,4},{2,6},{4,0},{6,2},{8,12},{10,14},{12,8},{14,10},{16,20},{18,... | collective-permute-start | bytes 2764808 | tf_op jit(solution)/shard_map/ppermute | solution.py:253
  102.8 20.8 %collective-permute-start.19 = (bf16[352,1280]{1,0:T(8,128)(2,1)S(1)}, bf16[352,1280]{1,0:T(8,128)(2,1)S(1)}, u32[]{:S(2)}, u32[]{:S(2)}) collective-permute-start(bf16[352,1280]{1,0:T(8,128)(2,1)S(1)} %pad_maximum_fusion.4), channel_id=1, source_target_pairs={{0,1},{1,0},{2,3},{3,2},{4,5},{5,4},{6,7},{7,6},{8,9},{9,8},{10,11... | collective-permute-start | bytes 2703368 | tf_op jit(solution)/shard_map/ppermute | solution.py:256
  123.7 20.5 %collective-permute-start.21 = (bf16[720,640]{1,0:T(8,128)(2,1)S(1)}, bf16[720,640]{1,0:T(8,128)(2,1)S(1)}, u32[]{:S(2)}, u32[]{:S(2)}) collective-permute-start(bf16[720,640]{1,0:T(8,128)(2,1)S(1)} %pad_maximum_fusion.3), channel_id=1, source_target_pairs={{0,4},{2,6},{4,0},{6,2},{8,12},{10,14},{12,8},{14,10},{16,20},{18,... | collective-permute-start | bytes 2764808 | tf_op jit(solution)/shard_map/ppermute | solution.py:253
  124.1 20.3 %collective-permute-start.25 = (bf16[4,2,80,640]{3,2,1,0:T(8,128)(2,1)S(1)}, bf16[4,2,80,640]{3,2,1,0:T(8,128)(2,1)}, u32[]{:S(2)}, u32[]{:S(2)}) collective-permute-start(bf16[4,2,80,640]{3,2,1,0:T(8,128)(2,1)S(1)} %pad_maximum_fusion.6), channel_id=1, source_target_pairs={{0,1},{1,0},{2,3},{3,2},{4,5},{5,4},{6,7},{7,6},{8,9},{9,8},{10,11... | collective-permute-start | bytes 2457608 | tf_op jit(solution)/shard_map/ppermute | solution.py:256
  125.8 18.5 %collective-permute-start.22 = (bf16[160,640]{1,0:T(8,128)(2,1)S(1)}, bf16[160,640]{1,0:T(8,128)(2,1)S(1)}, u32[]{:S(2)}, u32[]{:S(2)}) collective-permute-start(bf16[160,640]{1,0:T(8,128)(2,1)S(1)} %bitcast.63), channel_id=1, source_target_pairs={{0,8},{2,10},{4,12},{6,14},{8,0},{10,2},{12,4},{14,6},{16,24},{18,... | collective-permute-start | bytes 614408 | tf_op jit(solution)/shard_map/ppermute | solution.py:253
  127.8 16.6 %collective-permute-start.23 = (bf16[2,80,640]{2,1,0:T(8,128)(2,1)S(1)}, bf16[2,80,640]{2,1,0:T(8,128)(2,1)S(1)}, u32[]{:S(2)}, u32[]{:S(2)}) collective-permute-start(bf16[2,80,640]{2,1,0:T(8,128)(2,1)S(1)} %pad_maximum_fusion.9), channel_id=1, source_target_pairs={{0,16},{2,18},{4,20},{6,22},{8,24},{10,26},{12,28},{14,30},{16,0},... | collective-permute-start | bytes 614408 | tf_op jit(solution)/shard_map/ppermute | solution.py:253
  150.1 24.9 %collective-permute-start.33 = (bf16[1280,640]{1,0:T(8,128)(2,1)S(1)}, bf16[1280,640]{1,0:T(8,128)(2,1)S(1)}, u32[]{:S(2)}, u32[]{:S(2)}) collective-permute-start(bf16[1280,640]{1,0:T(8,128)(2,1)S(1)} %constant_dynamic-update-slice_fusion.4), channel_id=1, source_target_pairs={{0,2},{2,0},{4,6},{6,4},{8,10},{10,8},{12,14},{14,12},{16,18},{18,... | collective-permute-start | bytes 4915208 | tf_op jit(solution)/shard_map/ppermute | solution.py:253
  151.3 23.7 %collective-permute-start.26 = (bf16[640,640]{1,0:T(8,128)(2,1)}, bf16[640,640]{1,0:T(8,128)(2,1)S(1)}, u32[]{:S(2)}, u32[]{:S(2)}) collective-permute-start(bf16[640,640]{1,0:T(8,128)(2,1)} %bitcast.23), channel_id=1, source_target_pairs={{0,4},{2,6},{4,0},{6,2},{8,12},{10,14},{12,8},{14,10},{16,20},{18,... | collective-permute-start | bytes 2457608 | tf_op jit(solution)/shard_map/ppermute | solution.py:253
  152.0 23.0 %collective-permute-start.28 = (bf16[2,80,640]{2,1,0:T(8,128)(2,1)S(1)}, bf16[2,80,640]{2,1,0:T(8,128)(2,1)S(1)}, u32[]{:S(2)}, u32[]{:S(2)}) collective-permute-start(bf16[2,80,640]{2,1,0:T(8,128)(2,1)S(1)} %get-tuple-element.158), channel_id=1, source_target_pairs={{0,16},{2,18},{4,20},{6,22},{8,24},{10,26},{12,28},{14,30},{16,0},... | collective-permute-start | bytes 614408 | tf_op jit(solution)/shard_map/ppermute | solution.py:253
  153.6 21.4 %collective-permute-start.29 = (bf16[2,80,640]{2,1,0:T(8,128)(2,1)S(1)}, bf16[2,80,640]{2,1,0:T(8,128)(2,1)S(1)}, u32[]{:S(2)}, u32[]{:S(2)}) collective-permute-start(bf16[2,80,640]{2,1,0:T(8,128)(2,1)S(1)} %get-tuple-element.158), channel_id=1, source_target_pairs={{0,24},{2,26},{4,28},{6,30},{8,16},{10,18},{12,20},{14,22},{16,8},... | collective-permute-start | bytes 614408 | tf_op jit(solution)/shard_map/ppermute | solution.py:253
  155.3 19.5 %collective-permute-start.27 = (bf16[160,640]{1,0:T(8,128)(2,1)S(1)}, bf16[160,640]{1,0:T(8,128)(2,1)S(1)}, u32[]{:S(2)}, u32[]{:S(2)}) collective-permute-start(bf16[160,640]{1,0:T(8,128)(2,1)S(1)} %bitcast.75), channel_id=1, source_target_pairs={{0,8},{2,10},{4,12},{6,14},{8,0},{10,2},{12,4},{14,6},{16,24},{18,... | collective-permute-start | bytes 614408 | tf_op jit(solution)/shard_map/ppermute | solution.py:253
  (51 other events, 341.4 us)

commit v5 on v4

--- a/solution.py
+++ b/solution.py
@@ -288,8 +288,7 @@
     tokens = query_rows.shape[0]
     third = tokens // 3 // 16 * 16
     cuts = (0, tokens - 2 * third, tokens - third, tokens)
-    query_parts = [query_rows[a:b] for a, b in zip(cuts, cuts[1:])]
-    far_parts = [over(query_parts[0])]
+    far_parts = [over(query_rows[cuts[0] : cuts[1]])]
     high = lax.reduce_precision(head_gain, 8, 7)
     middle = lax.reduce_precision(head_gain - high, 8, 7)
     gain_rows = jnp.stack([high, middle, head_gain - high - middle]).astype(BF16)
@@ -313,8 +312,7 @@
     other, inputs, spot = tie((other, inputs, spot))
     got_pair, got_out = (across(a, 1) for a in other)
     own_pair, own_out, pair_old, out_old = grads_of(spot, 0, *inputs)
-    own_pair, own_out, blocks, far_parts, query_parts = tie((own_pair, own_out, blocks, far_parts, query_parts))
-    far_parts.append(over(query_parts[1]))
+    own_pair, own_out, blocks, far_parts, late_rows = tie((own_pair, own_out, blocks, far_parts, query_rows))
 
     def pair_sum(start, count):
         return part(own_pair, start, count, 1).astype(F32) + part(got_pair, start, count, 1).astype(F32)
@@ -322,7 +320,9 @@
     def out_sum(start, count):
         return part(own_out, start, count).astype(F32) + part(got_out, start, count).astype(F32)
 
-    pair_got, _ = to_upper(lambda u: pair_sum(u * half, half).astype(BF16))
+    pair_sent, late_rows = tie((pair_sum((1 - upper) * half, half).astype(BF16), late_rows))
+    pair_got, _ = to_upper(lambda u: pair_sent)
+    far_parts.append(over(late_rows[cuts[1] : cuts[2]]))
     out_got, rider = to_ranks(
         lambda r: out_sum(r * 2 * piece, 2 * piece).astype(BF16), blocks[2] if stepwise else None
     )
@@ -335,9 +335,11 @@
     if stepwise:
         near, away = jnp.concatenate(blocks[:2]), jnp.concatenate([blocks[2], rider])
         kept, given = jnp.where(here, near, away), jnp.where(here, away, near)
-    pair_sent, out_sent, kept, given, far_parts = tie((pair_sent, out_sent, kept, given, far_parts))
+    out_sent = part(out_sent, (1 - upper) * piece, piece)
+    out_joined = joined(out_sent, kept)
+    pair_sent, out_joined, given, far_parts = tie((pair_sent, out_joined, given, far_parts))
     pair_got, _ = to_ranks(lambda r: part(pair_sent, r * piece, piece, 1))
-    out_got, kept_upper = to_upper(lambda u: part(out_sent, u * piece, piece), kept)
+    out_got, kept_upper = parted(across(out_joined, 2), out_sent, kept)
     come = over(given) if stepwise else None
     pair_grad = part(pair_total, rank * piece, piece, 1)
     for a in pair_got:
@@ -346,11 +348,11 @@
     pair_wide = part(pair_old, upper * half + rank * piece, piece, 1).astype(F32)
     out_wide = part(out_old, rank * 2 * piece + upper * piece, piece).astype(F32)
     pair_new, out_new = renorm(pair_wide, pair_grad), renorm(out_wide, out_grad)
-    pair_new, out_new, come, query_parts, kept, kept_upper = tie((pair_new, out_new, come, query_parts, kept, kept_upper))
+    pair_new, out_new, come, late_rows, kept, kept_upper = tie((pair_new, out_new, come, late_rows, kept, kept_upper))
 
     pair_got, _ = to_ranks(lambda r: pair_new)
     out_got, come_upper = to_upper(lambda u: out_new, come)
-    far_parts.append(over(jnp.concatenate([query_parts[2], gain_rows])))
+    far_parts.append(over(jnp.concatenate([late_rows[cuts[2] :], gain_rows])))
     far_new = over(out_new)
     pair_held, out_held = jnp.stack([pair_new] + pair_got), jnp.stack([out_new, out_got])
     if stepwise:

time: 201 us -> 202 us (level)
    slice x2 -> x4, local copies, waits for them, and re-layouts: 3.2 us -> 1.04 us  [the longest x1 0.98 us: on_device(): far_parts = [over(query_rows[cuts[0]:cuts[1]])]]
    convert_element_type x2 -> x1, other arithmetic: 4.66 us -> 2.63 us  [on_device(): pair_sent, out_sent = (pair_total.astype(BF16), out_total.astype(BF16))]
    unnamed x67 -> x65, local copies, waits for them, and re-layouts: 4.75 us -> 4.39 us
  transfers between devices with their start and end apart: 40 -> 40, of which waited for: 15 -> 17; matrix products, arithmetic and copies ran while one was open for 11% -> 10% of each run, Pallas kernels for 15% -> 15%
where the time goes in v5:
time: 202 us; the launch traced here: 201 us
  waiting for transfers between devices  71 us (35%)
  Pallas kernels  59.1 us (29%)
  starting transfers between devices  42.9 us (21%)
  other arithmetic  16.3 us (8%)
  local copies, waits for them, and re-layouts  10.2 us (5%)
    ppermute x34, waiting for transfers between devices, across(): return lax.ppermute(array, 'ctx', [(j, j ^ mask) for j in range(n_ctx)])  68.9 us
    pallas_call x2, Pallas kernels, query_heads(): pl.pallas_call(functools.partial(query_kernel, counts, masks, final), out...  37 us
    ppermute x34, starting transfers between devices, across(): return lax.ppermute(array, 'ctx', [(j, j ^ mask) for j in range(n_ctx)])  34.8 us
    pallas_call x2, Pallas kernels, grads_of(): pl.pallas_call(functools.partial(grad_kernel, far), out_shape=[jax.ShapeD...  22.2 us
    ppermute x6, starting transfers between devices, over(): return lax.ppermute(array, 'head', [(j, j ^ 1) for j in range(n_head)])  8.14 us
    unnamed x65, local copies, waits for them, and re-layouts  4.39 us
  transfers between devices with their start and end apart: 40, of which 17 were waited for; matrix products, arithmetic and copies ran while one was open for 10% of the time, Pallas kernels for 15%

profile of v5, /device:TPU:0, one launch (start us, length us, event | category | flops | bytes accessed | tf_op | source)
XLA Modules:
  0.0 201.0 jit_solution(4021795977234246710)
XLA Ops:
  1.3 10.8 %grads.2 = (bf16[2,640,640]{2,1,0:T(8,128)(2,1)}, bf16[640,640]{1,0:T(8,128)(2,1)}) custom-call(s32[4]{0:T(128)} %pad_add_fusion.spot_ref, bf16[1024,1280]{1,0:T(8,128)(2,1)} %k_ref.2, bf16[1024,1280]{1,0:T(8,128)(2,1)} %v_ref.2, f32[2,1024]{1,0:T(2,128)} %lr_ref.2, bf16[2,640,640]{2,1,0:T(8,128)(2,1)} %win_ref.2, bf16[2,640,640]{2,1,0:T(8,128)(2,1)} %wgate_ref.2, ...), custom_call_target="tpu_custom_call" | custom-call | flops 419430400 | bytes 2621440 | tf_op jit(solution)/shard_map/grads/pallas_call | solution.py:61
  13.5 2.5 %collective-permute-start.2 = (bf16[352,1280]{1,0:T(8,128)(2,1)}, bf16[352,1280]{1,0:T(8,128)(2,1)}, u32[]{:S(2)}, u32[]{:S(2)}) collective-permute-start(bf16[352,1280]{1,0:T(8,128)(2,1)} %slice.33), channel_id=1, source_target_pairs={{0,1},{1,0},{2,3},{3,2},{4,5},{5,4},{6,7},{7,6},{8,9},{9,8},{10,11... | collective-permute-start | bytes 2703368 | tf_op jit(solution)/shard_map/ppermute | solution.py:256
  17.9 2.6 %collective-permute-start.1 = (bf16[320,640]{1,0:T(8,128)(2,1)S(1)}, bf16[320,640]{1,0:T(8,128)(2,1)S(1)}, u32[]{:S(2)}, u32[]{:S(2)}) collective-permute-start(bf16[320,640]{1,0:T(8,128)(2,1)S(1)} %bitcast.57), channel_id=1, source_target_pairs={{0,16},{2,18},{4,20},{6,22},{8,24},{10,26},{12,28},{14,30},{16,0},... | collective-permute-start | bytes 1228808 | tf_op jit(solution)/shard_map/ppermute | solution.py:253
  20.5 11.4 %grads.3 = (bf16[2,640,640]{2,1,0:T(8,128)(2,1)}, bf16[640,640]{1,0:T(8,128)(2,1)}, bf16[2,640,640]{2,1,0:T(8,128)(2,1)}, bf16[640,640]{1,0:T(8,128)(2,1)}) custom-call(s32[4]{0:T(128)} %pad_add_fusion.spot_ref, bf16[1024,1280]{1,0:T(8,128)(2,1)} %k_ref.2, bf16[1024,1280]{1,0:T(8,128)(2,1)} %v_ref.2, f32[2,1024]{1,0:T(2,128)} %lr_ref.2, ...), custom_call_target="tpu_custom_call" | custom-call | flops 419430400 | bytes 2621440 | tf_op jit(solution)/shard_map/grads/pallas_call | solution.py:61
  31.9 4.8 %collective-permute-done = bf16[320,640]{1,0:T(8,128)(2,1)} collective-permute-done((bf16[320,640]{1,0:T(8,128)(2,1)S(1)}, bf16[320,640]{1,0:T(8,128)(2,1)}, u32[]{:S(2)}, u32[]{:S(2)}) %collective-permute-start) | collective-permute-done | bytes 409632 | tf_op jit(solution)/shard_map/ppermute | solution.py:253
  36.7 2.2 %collective-permute-done.1 = bf16[320,640]{1,0:T(8,128)(2,1)S(1)} collective-permute-done((bf16[320,640]{1,0:T(8,128)(2,1)S(1)}, bf16[320,640]{1,0:T(8,128)(2,1)S(1)}, u32[]{:S(2)}, u32[]{:S(2)}) %collective-permute-start.1) | collective-permute-done | bytes 409632 | tf_op jit(solution)/shard_map/ppermute | solution.py:253
  39.0 2.4 %add_convert_fusion.2 = (bf16[160,640]{1,0:T(8,128)(2,1)}, bf16[160,640]{1,0:T(8,128)(2,1)}, bf16[160,640]{1,0:T(8,128)(2,1)S(1)}) fusion(bf16[640,640]{1,0:T(8,128)(2,1)} %collective-permute-done.5, s32[]{:T(128)S(6)} %select_n.96, bf16[640,640]{1,0:T(8,128)(2,1)} %get-tuple-element.87, s32[]{:T(128)S(6)} %select_n.97, s32[]{:T(128)S(6)} %select_n.95), kind=kLoop, calls=%fused_computation.24 | loop fusion | flops 1228800 | bytes 1843212 | tf_op jit(solution)/shard_map/convert_element_type | solution.py:327
  42.7 2.0 %collective-permute-start.8 = (bf16[160,640]{1,0:T(8,128)(2,1)}, bf16[160,640]{1,0:T(8,128)(2,1)S(1)}, u32[]{:S(2)}, u32[]{:S(2)}) collective-permute-start(bf16[160,640]{1,0:T(8,128)(2,1)} %get-tuple-element.148), channel_id=1, source_target_pairs={{0,24},{2,26},{4,28},{6,30},{8,16},{10,18},{12,20},{14,22},{16,8},... | collective-permute-start | bytes 614408 | tf_op jit(solution)/shard_map/ppermute | solution.py:253
  50.8 13.4 %collective-permute-done.8 = bf16[160,640]{1,0:T(8,128)(2,1)S(1)} collective-permute-done((bf16[160,640]{1,0:T(8,128)(2,1)}, bf16[160,640]{1,0:T(8,128)(2,1)S(1)}, u32[]{:S(2)}, u32[]{:S(2)}) %collective-permute-start.8) | collective-permute-done | bytes 204832 | tf_op jit(solution)/shard_map/ppermute | solution.py:253
  70.8 2.6 %fusion.11 = (bf16[2,320,640]{2,1,0:T(8,128)(2,1)S(1)}, f32[2,320,640]{2,1,0:T(8,128)}) fusion(bf16[2,320,640]{2,1,0:T(8,128)(2,1)S(1)} %bitcast.61, bf16[2,640,640]{2,1,0:T(8,128)(2,1)} %collective-permute-done.3, s32[]{:T(128)S(6)} %select_n.91, bf16[2,640,640]{2,1,0:T(8,128)(2,1)S(1)} %copy-done.4), kind=kLoop, calls=%fused_computation.59 | loop fusion | flops 2457600 | bytes 4915204 | tf_op jit(solution)/shard_map/convert_element_type | solution.py:333
  74.3 3.5 %collective-permute-start.12 = (bf16[2,80,640]{2,1,0:T(8,128)(2,1)}, bf16[2,80,640]{2,1,0:T(8,128)(2,1)}, u32[]{:S(2)}, u32[]{:S(2)}) collective-permute-start(bf16[2,80,640]{2,1,0:T(8,128)(2,1)} %get-tuple-element.151), channel_id=1, source_target_pairs={{0,24},{2,26},{4,28},{6,30},{8,16},{10,18},{12,20},{14,22},{16,8},... | collective-permute-start | bytes 614408 | tf_op jit(solution)/shard_map/ppermute | solution.py:253
  81.5 2.9 %collective-permute-done.12 = bf16[2,80,640]{2,1,0:T(8,128)(2,1)} collective-permute-done((bf16[2,80,640]{2,1,0:T(8,128)(2,1)}, bf16[2,80,640]{2,1,0:T(8,128)(2,1)}, u32[]{:S(2)}, u32[]{:S(2)}) %collective-permute-start.12) | collective-permute-done | bytes 204832 | tf_op jit(solution)/shard_map/ppermute | solution.py:253
  84.4 10.3 %collective-permute-done.11 = bf16[2,80,640]{2,1,0:T(8,128)(2,1)} collective-permute-done((bf16[2,80,640]{2,1,0:T(8,128)(2,1)}, bf16[2,80,640]{2,1,0:T(8,128)(2,1)}, u32[]{:S(2)}, u32[]{:S(2)}) %collective-permute-start.11) | collective-permute-done | bytes 204832 | tf_op jit(solution)/shard_map/ppermute | solution.py:253
  96.5 2.2 %collective-permute-done.13 = bf16[720,640]{1,0:T(8,128)(2,1)} collective-permute-done((bf16[720,640]{1,0:T(8,128)(2,1)}, bf16[720,640]{1,0:T(8,128)(2,1)}, u32[]{:S(2)}, u32[]{:S(2)}) %collective-permute-start.13) | collective-permute-done | bytes 921632 | tf_op jit(solution)/shard_map/ppermute | solution.py:253
  105.8 3.5 %collective-permute-start.17 = (bf16[2,80,640]{2,1,0:T(8,128)(2,1)S(1)}, bf16[2,80,640]{2,1,0:T(8,128)(2,1)S(1)}, u32[]{:S(2)}, u32[]{:S(2)}) collective-permute-start(bf16[2,80,640]{2,1,0:T(8,128)(2,1)S(1)} %multiply_convert_fusion), channel_id=1, source_target_pairs={{0,24},{2,26},{4,28},{6,30},{8,16},{10,18},{12,20},{14,22},{16,8},... | collective-permute-start | bytes 614408 | tf_op jit(solution)/shard_map/ppermute | solution.py:253
  110.2 5.4 %collective-permute-done.17 = bf16[2,80,640]{2,1,0:T(8,128)(2,1)S(1)} collective-permute-done((bf16[2,80,640]{2,1,0:T(8,128)(2,1)S(1)}, bf16[2,80,640]{2,1,0:T(8,128)(2,1)S(1)}, u32[]{:S(2)}, u32[]{:S(2)}) %collective-permute-start.17) | collective-permute-done | bytes 204832 | tf_op jit(solution)/shard_map/ppermute | solution.py:253
  115.8 7.6 %collective-permute-done.16 = bf16[2,80,640]{2,1,0:T(8,128)(2,1)S(1)} collective-permute-done((bf16[2,80,640]{2,1,0:T(8,128)(2,1)S(1)}, bf16[2,80,640]{2,1,0:T(8,128)(2,1)S(1)}, u32[]{:S(2)}, u32[]{:S(2)}) %collective-permute-start.16) | collective-permute-done | bytes 204832 | tf_op jit(solution)/shard_map/ppermute | solution.py:253
  123.6 2.2 %collective-permute-done.20 = bf16[80,640]{1,0:T(8,128)(2,1)S(1)} collective-permute-done((bf16[80,640]{1,0:T(8,128)(2,1)S(1)}, bf16[80,640]{1,0:T(8,128)(2,1)S(1)}, u32[]{:S(2)}, u32[]{:S(2)}) %collective-permute-start.20) | collective-permute-done | bytes 102432 | tf_op jit(solution)/shard_map/ppermute | solution.py:256
  130.4 2.6 %collective-permute-start.23 = (bf16[2,80,640]{2,1,0:T(8,128)(2,1)S(1)}, bf16[2,80,640]{2,1,0:T(8,128)(2,1)S(1)}, u32[]{:S(2)}, u32[]{:S(2)}) collective-permute-start(bf16[2,80,640]{2,1,0:T(8,128)(2,1)S(1)} %pad_maximum_fusion.9), channel_id=1, source_target_pairs={{0,16},{2,18},{4,20},{6,22},{8,24},{10,26},{12,28},{14,30},{16,0},... | collective-permute-start | bytes 614408 | tf_op jit(solution)/shard_map/ppermute | solution.py:253
  133.3 11.8 %collective-permute-done.21 = bf16[720,640]{1,0:T(8,128)(2,1)S(1)} collective-permute-done((bf16[720,640]{1,0:T(8,128)(2,1)S(1)}, bf16[720,640]{1,0:T(8,128)(2,1)S(1)}, u32[]{:S(2)}, u32[]{:S(2)}) %collective-permute-start.21) | collective-permute-done | bytes 921632 | tf_op jit(solution)/shard_map/ppermute | solution.py:253
  147.5 3.1 %collective-permute-done.32.refs_6_ = bf16[4,2,80,640]{3,2,1,0:T(8,128)(2,1)S(1)} collective-permute-done((bf16[4,2,80,640]{3,2,1,0:T(8,128)(2,1)S(1)}, bf16[4,2,80,640]{3,2,1,0:T(8,128)(2,1)S(1)}, u32[]{:S(2)}, u32[]{:S(2)}) %collective-permute-start.32) | collective-permute-done | bytes 819232 | tf_op jit(solution)/shard_map/ppermute | solution.py:253
  157.6 18.3 %queries.2 = (f32[1024,1280]{1,0:T(8,128)}, bf16[2,640,640]{2,1,0:T(8,128)(2,1)}, bf16[2,640,640]{2,1,0:T(8,128)(2,1)}, bf16[2,640,640]{2,1,0:T(8,128)(2,1)}) custom-call(s32[4]{0:T(128)} %pad_add_fusion.spot_ref, bf16[1024,1280]{1,0:T(8,128)(2,1)} %refs_0_.1, bf16[4,2,160,640]{3,2,1,0:T(8,128)(2,1)} %bitcast.68, bf16[4,2,160,640]{3,2,1,0:T(8,128)(2,1)} %bitcast.79, ...), custom_call_target="tpu_custom_call" | custom-call | flops 8388608000 | bytes 12779520 | tf_op jit(solution)/shard_map/queries/pallas_call | solution.py:206
  177.2 2.6 %collective-permute-done.36.refs_13_ = bf16[1,2,80,640]{3,2,1,0:T(8,128)(2,1)S(1)} collective-permute-done((bf16[1,2,80,640]{3,2,1,0:T(8,128)(2,1)S(1)}, bf16[1,2,80,640]{3,2,1,0:T(8,128)(2,1)S(1)}, u32[]{:S(2)}, u32[]{:S(2)}) %collective-permute-start.36) | collective-permute-done | bytes 204832 | tf_op jit(solution)/shard_map/ppermute | solution.py:253
  182.2 18.7 %queries.3 = bf16[1024,1280]{1,0:T(8,128)(2,1)} custom-call(s32[4]{0:T(128)} %pad_add_fusion.spot_ref, bf16[352,1280]{1,0:T(8,128)(2,1)} %collective-permute-done.2.refs_0_, bf16[336,1280]{1,0:T(8,128)(2,1)} %copy-done.19, bf16[352,1280]{1,0:T(8,128)(2,1)} %copy-done.18, bf16[4,2,160,640]{3,2,1,0:T(8,128)(2,1)} %bitcast.69, ...), custom_call_target="tpu_custom_call" | custom-call | flops 8388608000 | bytes 12779520 | tf_op jit(solution)/shard_map/queries/pallas_call | solution.py:206
  (170 shorter events, 50.1 us)
Async XLA Ops:
  12.1 33.8 %collective-permute-start.3 = (bf16[2,640,640]{2,1,0:T(8,128)(2,1)}, bf16[2,640,640]{2,1,0:T(8,128)(2,1)}, u32[]{:S(2)}, u32[]{:S(2)}) collective-permute-start(bf16[2,640,640]{2,1,0:T(8,128)(2,1)} %get-tuple-element.84), channel_id=1, source_target_pairs={{0,2},{2,0},{4,6},{6,4},{8,10},{10,8},{12,14},{14,12},{16,18},{18,... | collective-permute-start | bytes 4915208 | tf_op jit(solution)/shard_map/ppermute | solution.py:253
  13.5 25.5 %collective-permute-start.2 = (bf16[352,1280]{1,0:T(8,128)(2,1)}, bf16[352,1280]{1,0:T(8,128)(2,1)}, u32[]{:S(2)}, u32[]{:S(2)}) collective-permute-start(bf16[352,1280]{1,0:T(8,128)(2,1)} %slice.33), channel_id=1, source_target_pairs={{0,1},{1,0},{2,3},{3,2},{4,5},{5,4},{6,7},{7,6},{8,9},{9,8},{10,11... | collective-permute-start | bytes 2703368 | tf_op jit(solution)/shard_map/ppermute | solution.py:256
  16.0 23.0 %collective-permute-start.5 = (bf16[640,640]{1,0:T(8,128)(2,1)}, bf16[640,640]{1,0:T(8,128)(2,1)}, u32[]{:S(2)}, u32[]{:S(2)}) collective-permute-start(bf16[640,640]{1,0:T(8,128)(2,1)} %get-tuple-element.88), channel_id=1, source_target_pairs={{0,2},{2,0},{4,6},{6,4},{8,10},{10,8},{12,14},{14,12},{16,18},{18,... | collective-permute-start | bytes 2457608 | tf_op jit(solution)/shard_map/ppermute | solution.py:253
  16.3 20.5 %collective-permute-start = (bf16[320,640]{1,0:T(8,128)(2,1)S(1)}, bf16[320,640]{1,0:T(8,128)(2,1)}, u32[]{:S(2)}, u32[]{:S(2)}) collective-permute-start(bf16[320,640]{1,0:T(8,128)(2,1)S(1)} %bitcast.56), channel_id=1, source_target_pairs={{0,8},{2,10},{4,12},{6,14},{8,0},{10,2},{12,4},{14,6},{16,24},{18,... | collective-permute-start | bytes 1228808 | tf_op jit(solution)/shard_map/ppermute | solution.py:253
  17.9 21.1 %collective-permute-start.1 = (bf16[320,640]{1,0:T(8,128)(2,1)S(1)}, bf16[320,640]{1,0:T(8,128)(2,1)S(1)}, u32[]{:S(2)}, u32[]{:S(2)}) collective-permute-start(bf16[320,640]{1,0:T(8,128)(2,1)S(1)} %bitcast.57), channel_id=1, source_target_pairs={{0,16},{2,18},{4,20},{6,22},{8,24},{10,26},{12,28},{14,30},{16,0},... | collective-permute-start | bytes 1228808 | tf_op jit(solution)/shard_map/ppermute | solution.py:253
  42.3 23.0 %collective-permute-start.6 = (bf16[480,640]{1,0:T(8,128)(2,1)}, bf16[480,640]{1,0:T(8,128)(2,1)}, u32[]{:S(2)}, u32[]{:S(2)}) collective-permute-start(bf16[480,640]{1,0:T(8,128)(2,1)} %pad_maximum_fusion.8), channel_id=1, source_target_pairs={{0,8},{2,10},{4,12},{6,14},{8,0},{10,2},{12,4},{14,6},{16,24},{18,... | collective-permute-start | bytes 1843208 | tf_op jit(solution)/shard_map/ppermute | solution.py:253
  42.7 21.4 %collective-permute-start.8 = (bf16[160,640]{1,0:T(8,128)(2,1)}, bf16[160,640]{1,0:T(8,128)(2,1)S(1)}, u32[]{:S(2)}, u32[]{:S(2)}) collective-permute-start(bf16[160,640]{1,0:T(8,128)(2,1)} %get-tuple-element.148), channel_id=1, source_target_pairs={{0,24},{2,26},{4,28},{6,30},{8,16},{10,18},{12,20},{14,22},{16,8},... | collective-permute-start | bytes 614408 | tf_op jit(solution)/shard_map/ppermute | solution.py:253
  44.8 19.8 %collective-permute-start.7 = (bf16[160,640]{1,0:T(8,128)(2,1)}, bf16[160,640]{1,0:T(8,128)(2,1)S(1)}, u32[]{:S(2)}, u32[]{:S(2)}) collective-permute-start(bf16[160,640]{1,0:T(8,128)(2,1)} %get-tuple-element.147), channel_id=1, source_target_pairs={{0,16},{2,18},{4,20},{6,22},{8,24},{10,26},{12,28},{14,30},{16,0},... | collective-permute-start | bytes 614408 | tf_op jit(solution)/shard_map/ppermute | solution.py:253
  47.4 22.6 %collective-permute-start.4 = (bf16[640,640]{1,0:T(8,128)(2,1)S(1)}, bf16[640,640]{1,0:T(8,128)(2,1)S(1)}, u32[]{:S(2)}, u32[]{:S(2)}) collective-permute-start(bf16[640,640]{1,0:T(8,128)(2,1)S(1)} %bitcast.66), channel_id=1, source_target_pairs={{0,4},{2,6},{4,0},{6,2},{8,12},{10,14},{12,8},{14,10},{16,20},{18,... | collective-permute-start | bytes 2457608 | tf_op jit(solution)/shard_map/ppermute | solution.py:253
  50.2 23.2 %collective-permute-start.9 = (bf16[336,1280]{1,0:T(8,128)(2,1)S(1)}, bf16[336,1280]{1,0:T(8,128)(2,1)S(1)}, u32[]{:S(2)}, u32[]{:S(2)}) collective-permute-start(bf16[336,1280]{1,0:T(8,128)(2,1)S(1)} %slice.36), channel_id=1, source_target_pairs={{0,1},{1,0},{2,3},{3,2},{4,5},{5,4},{6,7},{7,6},{8,9},{9,8},{10,11... | collective-permute-start | bytes 2580488 | tf_op jit(solution)/shard_map/ppermute | solution.py:256
  77.8 17.0 %collective-permute-start.11 = (bf16[2,80,640]{2,1,0:T(8,128)(2,1)}, bf16[2,80,640]{2,1,0:T(8,128)(2,1)}, u32[]{:S(2)}, u32[]{:S(2)}) collective-permute-start(bf16[2,80,640]{2,1,0:T(8,128)(2,1)} %get-tuple-element.152), channel_id=1, source_target_pairs={{0,16},{2,18},{4,20},{6,22},{8,24},{10,26},{12,28},{14,30},{16,0},... | collective-permute-start | bytes 614408 | tf_op jit(solution)/shard_map/ppermute | solution.py:253
  78.0 16.7 %collective-permute-start.10 = (bf16[160,640]{1,0:T(8,128)(2,1)}, bf16[160,640]{1,0:T(8,128)(2,1)}, u32[]{:S(2)}, u32[]{:S(2)}) collective-permute-start(bf16[160,640]{1,0:T(8,128)(2,1)} %bitcast.10), channel_id=1, source_target_pairs={{0,8},{2,10},{4,12},{6,14},{8,0},{10,2},{12,4},{14,6},{16,24},{18,... | collective-permute-start | bytes 614408 | tf_op jit(solution)/shard_map/ppermute | solution.py:253
  78.7 20.0 %collective-permute-start.13 = (bf16[720,640]{1,0:T(8,128)(2,1)}, bf16[720,640]{1,0:T(8,128)(2,1)}, u32[]{:S(2)}, u32[]{:S(2)}) collective-permute-start(bf16[720,640]{1,0:T(8,128)(2,1)} %pad_maximum_fusion.1), channel_id=1, source_target_pairs={{0,4},{2,6},{4,0},{6,2},{8,12},{10,14},{12,8},{14,10},{16,20},{18,... | collective-permute-start | bytes 2764808 | tf_op jit(solution)/shard_map/ppermute | solution.py:253
  80.3 21.8 %collective-permute-start.14 = (bf16[640,640]{1,0:T(8,128)(2,1)}, bf16[640,640]{1,0:T(8,128)(2,1)S(1)}, u32[]{:S(2)}, u32[]{:S(2)}) collective-permute-start(bf16[640,640]{1,0:T(8,128)(2,1)} %get-tuple-element.97), channel_id=1, source_target_pairs={{0,1},{1,0},{2,3},{3,2},{4,5},{5,4},{6,7},{7,6},{8,9},{9,8},{10,11... | collective-permute-start | bytes 2457608 | tf_op jit(solution)/shard_map/ppermute | solution.py:256
  102.2 21.3 %collective-permute-start.18 = (bf16[720,640]{1,0:T(8,128)(2,1)S(1)}, bf16[720,640]{1,0:T(8,128)(2,1)S(1)}, u32[]{:S(2)}, u32[]{:S(2)}) collective-permute-start(bf16[720,640]{1,0:T(8,128)(2,1)S(1)} %pad_maximum_fusion.2), channel_id=1, source_target_pairs={{0,4},{2,6},{4,0},{6,2},{8,12},{10,14},{12,8},{14,10},{16,20},{18,... | collective-permute-start | bytes 2764808 | tf_op jit(solution)/shard_map/ppermute | solution.py:253
  103.9 21.9 %collective-permute-start.19 = (bf16[352,1280]{1,0:T(8,128)(2,1)S(1)}, bf16[352,1280]{1,0:T(8,128)(2,1)S(1)}, u32[]{:S(2)}, u32[]{:S(2)}) collective-permute-start(bf16[352,1280]{1,0:T(8,128)(2,1)S(1)} %pad_maximum_fusion.4), channel_id=1, source_target_pairs={{0,1},{1,0},{2,3},{3,2},{4,5},{5,4},{6,7},{7,6},{8,9},{9,8},{10,11... | collective-permute-start | bytes 2703368 | tf_op jit(solution)/shard_map/ppermute | solution.py:256
  125.9 19.2 %collective-permute-start.21 = (bf16[720,640]{1,0:T(8,128)(2,1)S(1)}, bf16[720,640]{1,0:T(8,128)(2,1)S(1)}, u32[]{:S(2)}, u32[]{:S(2)}) collective-permute-start(bf16[720,640]{1,0:T(8,128)(2,1)S(1)} %pad_maximum_fusion.3), channel_id=1, source_target_pairs={{0,4},{2,6},{4,0},{6,2},{8,12},{10,14},{12,8},{14,10},{16,20},{18,... | collective-permute-start | bytes 2764808 | tf_op jit(solution)/shard_map/ppermute | solution.py:253
  127.2 18.0 %collective-permute-start.25 = (bf16[4,2,80,640]{3,2,1,0:T(8,128)(2,1)S(1)}, bf16[4,2,80,640]{3,2,1,0:T(8,128)(2,1)}, u32[]{:S(2)}, u32[]{:S(2)}) collective-permute-start(bf16[4,2,80,640]{3,2,1,0:T(8,128)(2,1)S(1)} %pad_maximum_fusion.6), channel_id=1, source_target_pairs={{0,1},{1,0},{2,3},{3,2},{4,5},{5,4},{6,7},{7,6},{8,9},{9,8},{10,11... | collective-permute-start | bytes 2457608 | tf_op jit(solution)/shard_map/ppermute | solution.py:256
  128.9 16.2 %collective-permute-start.22 = (bf16[160,640]{1,0:T(8,128)(2,1)S(1)}, bf16[160,640]{1,0:T(8,128)(2,1)S(1)}, u32[]{:S(2)}, u32[]{:S(2)}) collective-permute-start(bf16[160,640]{1,0:T(8,128)(2,1)S(1)} %bitcast.64), channel_id=1, source_target_pairs={{0,8},{2,10},{4,12},{6,14},{8,0},{10,2},{12,4},{14,6},{16,24},{18,... | collective-permute-start | bytes 614408 | tf_op jit(solution)/shard_map/ppermute | solution.py:253
  150.9 25.1 %collective-permute-start.33 = (bf16[1280,640]{1,0:T(8,128)(2,1)S(1)}, bf16[1280,640]{1,0:T(8,128)(2,1)S(1)}, u32[]{:S(2)}, u32[]{:S(2)}) collective-permute-start(bf16[1280,640]{1,0:T(8,128)(2,1)S(1)} %constant_dynamic-update-slice_fusion.4), channel_id=1, source_target_pairs={{0,2},{2,0},{4,6},{6,4},{8,10},{10,8},{12,14},{14,12},{16,18},{18,... | collective-permute-start | bytes 4915208 | tf_op jit(solution)/shard_map/ppermute | solution.py:253
  152.1 23.9 %collective-permute-start.26 = (bf16[640,640]{1,0:T(8,128)(2,1)}, bf16[640,640]{1,0:T(8,128)(2,1)S(1)}, u32[]{:S(2)}, u32[]{:S(2)}) collective-permute-start(bf16[640,640]{1,0:T(8,128)(2,1)} %bitcast.23), channel_id=1, source_target_pairs={{0,4},{2,6},{4,0},{6,2},{8,12},{10,14},{12,8},{14,10},{16,20},{18,... | collective-permute-start | bytes 2457608 | tf_op jit(solution)/shard_map/ppermute | solution.py:253
  153.7 22.3 %collective-permute-start.28 = (bf16[2,80,640]{2,1,0:T(8,128)(2,1)S(1)}, bf16[2,80,640]{2,1,0:T(8,128)(2,1)S(1)}, u32[]{:S(2)}, u32[]{:S(2)}) collective-permute-start(bf16[2,80,640]{2,1,0:T(8,128)(2,1)S(1)} %get-tuple-element.154), channel_id=1, source_target_pairs={{0,16},{2,18},{4,20},{6,22},{8,24},{10,26},{12,28},{14,30},{16,0},... | collective-permute-start | bytes 614408 | tf_op jit(solution)/shard_map/ppermute | solution.py:253
  155.0 20.9 %collective-permute-start.29 = (bf16[2,80,640]{2,1,0:T(8,128)(2,1)S(1)}, bf16[2,80,640]{2,1,0:T(8,128)(2,1)S(1)}, u32[]{:S(2)}, u32[]{:S(2)}) collective-permute-start(bf16[2,80,640]{2,1,0:T(8,128)(2,1)S(1)} %get-tuple-element.154), channel_id=1, source_target_pairs={{0,24},{2,26},{4,28},{6,30},{8,16},{10,18},{12,20},{14,22},{16,8},... | collective-permute-start | bytes 614408 | tf_op jit(solution)/shard_map/ppermute | solution.py:253
  156.4 19.5 %collective-permute-start.27 = (bf16[160,640]{1,0:T(8,128)(2,1)S(1)}, bf16[160,640]{1,0:T(8,128)(2,1)S(1)}, u32[]{:S(2)}, u32[]{:S(2)}) collective-permute-start(bf16[160,640]{1,0:T(8,128)(2,1)S(1)} %bitcast.77), channel_id=1, source_target_pairs={{0,8},{2,10},{4,12},{6,14},{8,0},{10,2},{12,4},{14,6},{16,24},{18,... | collective-permute-start | bytes 614408 | tf_op jit(solution)/shard_map/ppermute | solution.py:253
  (50 other events, 333.8 us)

commit v6 on v5

--- a/solution.py
+++ b/solution.py
@@ -335,19 +335,19 @@
     if stepwise:
         near, away = jnp.concatenate(blocks[:2]), jnp.concatenate([blocks[2], rider])
         kept, given = jnp.where(here, near, away), jnp.where(here, away, near)
-    out_sent = part(out_sent, (1 - upper) * piece, piece)
-    out_joined = joined(out_sent, kept)
-    pair_sent, out_joined, given, far_parts = tie((pair_sent, out_joined, given, far_parts))
+    pair_sent, out_sent, kept, given, far_parts = tie((pair_sent, out_sent, kept, given, far_parts))
     pair_got, _ = to_ranks(lambda r: part(pair_sent, r * piece, piece, 1))
-    out_got, kept_upper = parted(across(out_joined, 2), out_sent, kept)
+    out_got, kept_upper = to_upper(lambda u: part(out_sent, u * piece, piece), kept)
     come = over(given) if stepwise else None
+    out_grad = part(out_total, upper * piece, piece) + out_got.astype(F32)
+    pair_wide = part(pair_old, upper * half + rank * piece, piece, 1).astype(F32)
+    out_wide = part(out_old, rank * 2 * piece + upper * piece, piece).astype(F32)
+    out_new = renorm(out_wide, out_grad)
+    out_new, pair_got = tie((out_new, pair_got))
     pair_grad = part(pair_total, rank * piece, piece, 1)
     for a in pair_got:
         pair_grad = pair_grad + a.astype(F32)
-    out_grad = part(out_total, upper * piece, piece) + out_got.astype(F32)
-    pair_wide = part(pair_old, upper * half + rank * piece, piece, 1).astype(F32)
-    out_wide = part(out_old, rank * 2 * piece + upper * piece, piece).astype(F32)
-    pair_new, out_new = renorm(pair_wide, pair_grad), renorm(out_wide, out_grad)
+    pair_new = renorm(pair_wide, pair_grad)
     pair_new, out_new, come, late_rows, kept, kept_upper = tie((pair_new, out_new, come, late_rows, kept, kept_upper))
 
     pair_got, _ = to_ranks(lambda r: pair_new)

time: 202 us -> 201 us (level)
  waiting for transfers between devices: 71 us -> 66.2 us
    ppermute x34, starting transfers between devices: 34.8 us -> 38.4 us  [across(): return lax.ppermute(array, 'ctx', [(j, j ^ mask) for j in range(n_ctx)])]
    ppermute x34, waiting for transfers between devices: 68.9 us -> 65.6 us  [across(): return lax.ppermute(array, 'ctx', [(j, j ^ mask) for j in range(n_ctx)])]
    convert_element_type x1 -> x2, other arithmetic: 2.63 us -> 5.15 us  [on_device(): pair_sent, out_sent = (pair_total.astype(BF16), out_total.astype(BF16))]
    unnamed x65 -> x63, local copies, waits for them, and re-layouts: 4.39 us -> 4.73 us
  transfers between devices with their start and end apart: 40 -> 40, of which waited for: 17 -> 13; matrix products, arithmetic and copies ran while one was open for 10% -> 11% of each run, Pallas kernels for 15% -> 15%
where the time goes in v6:
time: 201 us; the launch traced here: 200 us
  waiting for transfers between devices  66.2 us (33%)
  Pallas kernels  59.1 us (29%)
  starting transfers between devices  44.6 us (22%)
  other arithmetic  18.2 us (9%)
  local copies, waits for them, and re-layouts  10.7 us (5%)
    ppermute x34, waiting for transfers between devices, across(): return lax.ppermute(array, 'ctx', [(j, j ^ mask) for j in range(n_ctx)])  65.6 us
    ppermute x34, starting transfers between devices, across(): return lax.ppermute(array, 'ctx', [(j, j ^ mask) for j in range(n_ctx)])  38.4 us
    pallas_call x2, Pallas kernels, query_heads(): pl.pallas_call(functools.partial(query_kernel, counts, masks, final), out...  37 us
    pallas_call x2, Pallas kernels, grads_of(): pl.pallas_call(functools.partial(grad_kernel, far), out_shape=[jax.ShapeD...  22.2 us
    ppermute x6, starting transfers between devices, over(): return lax.ppermute(array, 'head', [(j, j ^ 1) for j in range(n_head)])  6.18 us
    convert_element_type x2, other arithmetic, on_device(): pair_sent, out_sent = (pair_total.astype(BF16), out_total.astype(BF16))  5.15 us
    unnamed x63, local copies, waits for them, and re-layouts  4.73 us
  transfers between devices with their start and end apart: 40, of which 13 were waited for; matrix products, arithmetic and copies ran while one was open for 11% of the time, Pallas kernels for 15%

profile of v6, /device:TPU:0, one launch (start us, length us, event | category | flops | bytes accessed | tf_op | source)
XLA Modules:
  0.0 200.4 jit_solution(3337894213417404677)
XLA Ops:
  1.3 10.8 %grads.2 = (bf16[2,640,640]{2,1,0:T(8,128)(2,1)}, bf16[640,640]{1,0:T(8,128)(2,1)}) custom-call(s32[4]{0:T(128)} %pad_add_fusion.spot_ref, bf16[1024,1280]{1,0:T(8,128)(2,1)} %k_ref.2, bf16[1024,1280]{1,0:T(8,128)(2,1)} %v_ref.2, f32[2,1024]{1,0:T(2,128)} %lr_ref.2, bf16[2,640,640]{2,1,0:T(8,128)(2,1)} %win_ref.2, bf16[2,640,640]{2,1,0:T(8,128)(2,1)} %wgate_ref.2, ...), custom_call_target="tpu_custom_call" | custom-call | flops 419430400 | bytes 2621440 | tf_op jit(solution)/shard_map/grads/pallas_call | solution.py:61
  13.5 2.5 %collective-permute-start.2 = (bf16[352,1280]{1,0:T(8,128)(2,1)}, bf16[352,1280]{1,0:T(8,128)(2,1)}, u32[]{:S(2)}, u32[]{:S(2)}) collective-permute-start(bf16[352,1280]{1,0:T(8,128)(2,1)} %slice.33), channel_id=1, source_target_pairs={{0,1},{1,0},{2,3},{3,2},{4,5},{5,4},{6,7},{7,6},{8,9},{9,8},{10,11... | collective-permute-start | bytes 2703368 | tf_op jit(solution)/shard_map/ppermute | solution.py:256
  17.9 2.6 %collective-permute-start.1 = (bf16[320,640]{1,0:T(8,128)(2,1)S(1)}, bf16[320,640]{1,0:T(8,128)(2,1)S(1)}, u32[]{:S(2)}, u32[]{:S(2)}) collective-permute-start(bf16[320,640]{1,0:T(8,128)(2,1)S(1)} %bitcast.56), channel_id=1, source_target_pairs={{0,16},{2,18},{4,20},{6,22},{8,24},{10,26},{12,28},{14,30},{16,0},... | collective-permute-start | bytes 1228808 | tf_op jit(solution)/shard_map/ppermute | solution.py:253
  20.5 11.4 %grads.3 = (bf16[2,640,640]{2,1,0:T(8,128)(2,1)}, bf16[640,640]{1,0:T(8,128)(2,1)}, bf16[2,640,640]{2,1,0:T(8,128)(2,1)}, bf16[640,640]{1,0:T(8,128)(2,1)}) custom-call(s32[4]{0:T(128)} %pad_add_fusion.spot_ref, bf16[1024,1280]{1,0:T(8,128)(2,1)} %k_ref.2, bf16[1024,1280]{1,0:T(8,128)(2,1)} %v_ref.2, f32[2,1024]{1,0:T(2,128)} %lr_ref.2, ...), custom_call_target="tpu_custom_call" | custom-call | flops 419430400 | bytes 2621440 | tf_op jit(solution)/shard_map/grads/pallas_call | solution.py:61
  31.9 4.8 %collective-permute-done = bf16[320,640]{1,0:T(8,128)(2,1)} collective-permute-done((bf16[320,640]{1,0:T(8,128)(2,1)S(1)}, bf16[320,640]{1,0:T(8,128)(2,1)}, u32[]{:S(2)}, u32[]{:S(2)}) %collective-permute-start) | collective-permute-done | bytes 409632 | tf_op jit(solution)/shard_map/ppermute | solution.py:253
  36.7 2.2 %collective-permute-done.1 = bf16[320,640]{1,0:T(8,128)(2,1)S(1)} collective-permute-done((bf16[320,640]{1,0:T(8,128)(2,1)S(1)}, bf16[320,640]{1,0:T(8,128)(2,1)S(1)}, u32[]{:S(2)}, u32[]{:S(2)}) %collective-permute-start.1) | collective-permute-done | bytes 409632 | tf_op jit(solution)/shard_map/ppermute | solution.py:253
  39.0 2.4 %add_convert_fusion.3 = (bf16[160,640]{1,0:T(8,128)(2,1)S(1)}, bf16[160,640]{1,0:T(8,128)(2,1)}, bf16[160,640]{1,0:T(8,128)(2,1)}) fusion(bf16[640,640]{1,0:T(8,128)(2,1)} %collective-permute-done.5, s32[]{:T(128)S(6)} %select_n.96, bf16[640,640]{1,0:T(8,128)(2,1)} %get-tuple-element.93, s32[]{:T(128)S(6)} %select_n.98, s32[]{:T(128)S(6)} %select_n.97), kind=kLoop, calls=%fused_computation.22 | loop fusion | flops 1228800 | bytes 1843212 | tf_op jit(solution)/shard_map/convert_element_type | solution.py:327
  42.7 2.5 %add_convert_fusion = bf16[2,320,640]{2,1,0:T(8,128)(2,1)} fusion(bf16[2,640,640]{2,1,0:T(8,128)(2,1)} %collective-permute-done.3, s32[]{:T(128)S(6)} %select_n.92, bf16[2,640,640]{2,1,0:T(8,128)(2,1)} %get-tuple-element.88), kind=kLoop, calls=%fused_computation.2 | loop fusion | flops 1638400 | bytes 2457604 | tf_op jit(solution)/shard_map/convert_element_type | solution.py:323
  46.7 2.0 %collective-permute-start.8 = (bf16[160,640]{1,0:T(8,128)(2,1)}, bf16[160,640]{1,0:T(8,128)(2,1)S(1)}, u32[]{:S(2)}, u32[]{:S(2)}) collective-permute-start(bf16[160,640]{1,0:T(8,128)(2,1)} %get-tuple-element.160), channel_id=1, source_target_pairs={{0,24},{2,26},{4,28},{6,30},{8,16},{10,18},{12,20},{14,22},{16,8},... | collective-permute-start | bytes 614408 | tf_op jit(solution)/shard_map/ppermute | solution.py:253
  51.5 13.7 %collective-permute-done.6 = bf16[480,640]{1,0:T(8,128)(2,1)} collective-permute-done((bf16[480,640]{1,0:T(8,128)(2,1)}, bf16[480,640]{1,0:T(8,128)(2,1)}, u32[]{:S(2)}, u32[]{:S(2)}) %collective-permute-start.6) | collective-permute-done | bytes 614432 | tf_op jit(solution)/shard_map/ppermute | solution.py:253
  70.1 3.1 %fusion.10 = (bf16[2,320,640]{2,1,0:T(8,128)(2,1)}, f32[2,320,640]{2,1,0:T(8,128)}) fusion(bf16[2,320,640]{2,1,0:T(8,128)(2,1)} %bitcast.45, bf16[2,640,640]{2,1,0:T(8,128)(2,1)} %collective-permute-done.3, s32[]{:T(128)S(6)} %select_n.91, bf16[2,640,640]{2,1,0:T(8,128)(2,1)S(1)} %copy-done.2), kind=kLoop, calls=%fused_computation.57 | loop fusion | flops 2457600 | bytes 4915204 | tf_op jit(solution)/shard_map/convert_element_type | solution.py:333
  78.5 2.9 %collective-permute-start.12 = (bf16[2,80,640]{2,1,0:T(8,128)(2,1)S(1)}, bf16[2,80,640]{2,1,0:T(8,128)(2,1)S(1)}, u32[]{:S(2)}, u32[]{:S(2)}) collective-permute-start(bf16[2,80,640]{2,1,0:T(8,128)(2,1)S(1)} %get-tuple-element.163), channel_id=1, source_target_pairs={{0,16},{2,18},{4,20},{6,22},{8,24},{10,26},{12,28},{14,30},{16,0},... | collective-permute-start | bytes 614408 | tf_op jit(solution)/shard_map/ppermute | solution.py:253
  82.9 10.9 %collective-permute-done.10 = bf16[720,640]{1,0:T(8,128)(2,1)} collective-permute-done((bf16[720,640]{1,0:T(8,128)(2,1)}, bf16[720,640]{1,0:T(8,128)(2,1)}, u32[]{:S(2)}, u32[]{:S(2)}) %collective-permute-start.10) | collective-permute-done | bytes 921632 | tf_op jit(solution)/shard_map/ppermute | solution.py:253
  102.0 5.6 %collective-permute-start.17 = (bf16[2,80,640]{2,1,0:T(8,128)(2,1)S(1)}, bf16[2,80,640]{2,1,0:T(8,128)(2,1)S(1)}, u32[]{:S(2)}, u32[]{:S(2)}) collective-permute-start(bf16[2,80,640]{2,1,0:T(8,128)(2,1)S(1)} %multiply_convert_fusion), channel_id=1, source_target_pairs={{0,24},{2,26},{4,28},{6,30},{8,16},{10,18},{12,20},{14,22},{16,8},... | collective-permute-start | bytes 614408 | tf_op jit(solution)/shard_map/ppermute | solution.py:253
  108.1 5.4 %collective-permute-done.17 = bf16[2,80,640]{2,1,0:T(8,128)(2,1)S(1)} collective-permute-done((bf16[2,80,640]{2,1,0:T(8,128)(2,1)S(1)}, bf16[2,80,640]{2,1,0:T(8,128)(2,1)S(1)}, u32[]{:S(2)}, u32[]{:S(2)}) %collective-permute-start.17) | collective-permute-done | bytes 204832 | tf_op jit(solution)/shard_map/ppermute | solution.py:253
  113.7 8.6 %collective-permute-done.16 = bf16[2,80,640]{2,1,0:T(8,128)(2,1)S(1)} collective-permute-done((bf16[2,80,640]{2,1,0:T(8,128)(2,1)S(1)}, bf16[2,80,640]{2,1,0:T(8,128)(2,1)S(1)}, u32[]{:S(2)}, u32[]{:S(2)}) %collective-permute-start.16) | collective-permute-done | bytes 204832 | tf_op jit(solution)/shard_map/ppermute | solution.py:253
  124.3 4.2 %collective-permute-start.22 = (bf16[160,640]{1,0:T(8,128)(2,1)S(1)}, bf16[160,640]{1,0:T(8,128)(2,1)S(1)}, u32[]{:S(2)}, u32[]{:S(2)}) collective-permute-start(bf16[160,640]{1,0:T(8,128)(2,1)S(1)} %bitcast.60), channel_id=1, source_target_pairs={{0,8},{2,10},{4,12},{6,14},{8,0},{10,2},{12,4},{14,6},{16,24},{18,... | collective-permute-start | bytes 614408 | tf_op jit(solution)/shard_map/ppermute | solution.py:253
  128.5 2.7 %collective-permute-start.23 = (bf16[2,80,640]{2,1,0:T(8,128)(2,1)S(1)}, bf16[2,80,640]{2,1,0:T(8,128)(2,1)S(1)}, u32[]{:S(2)}, u32[]{:S(2)}) collective-permute-start(bf16[2,80,640]{2,1,0:T(8,128)(2,1)S(1)} %pad_maximum_fusion.9), channel_id=1, source_target_pairs={{0,16},{2,18},{4,20},{6,22},{8,24},{10,26},{12,28},{14,30},{16,0},... | collective-permute-start | bytes 614408 | tf_op jit(solution)/shard_map/ppermute | solution.py:253
  131.2 12.8 %collective-permute-done.21 = bf16[720,640]{1,0:T(8,128)(2,1)S(1)} collective-permute-done((bf16[720,640]{1,0:T(8,128)(2,1)S(1)}, bf16[720,640]{1,0:T(8,128)(2,1)S(1)}, u32[]{:S(2)}, u32[]{:S(2)}) %collective-permute-start.21) | collective-permute-done | bytes 921632 | tf_op jit(solution)/shard_map/ppermute | solution.py:253
  146.4 3.1 %collective-permute-done.32.refs_6_ = bf16[4,2,80,640]{3,2,1,0:T(8,128)(2,1)S(1)} collective-permute-done((bf16[4,2,80,640]{3,2,1,0:T(8,128)(2,1)S(1)}, bf16[4,2,80,640]{3,2,1,0:T(8,128)(2,1)S(1)}, u32[]{:S(2)}, u32[]{:S(2)}) %collective-permute-start.32) | collective-permute-done | bytes 819232 | tf_op jit(solution)/shard_map/ppermute | solution.py:253
  152.3 2.1 %collective-permute-start.28 = (bf16[2,80,640]{2,1,0:T(8,128)(2,1)S(1)}, bf16[2,80,640]{2,1,0:T(8,128)(2,1)S(1)}, u32[]{:S(2)}, u32[]{:S(2)}) collective-permute-start(bf16[2,80,640]{2,1,0:T(8,128)(2,1)S(1)} %get-tuple-element.166), channel_id=1, source_target_pairs={{0,16},{2,18},{4,20},{6,22},{8,24},{10,26},{12,28},{14,30},{16,0},... | collective-permute-start | bytes 614408 | tf_op jit(solution)/shard_map/ppermute | solution.py:253
  156.9 18.3 %queries.2 = (f32[1024,1280]{1,0:T(8,128)}, bf16[2,640,640]{2,1,0:T(8,128)(2,1)}, bf16[2,640,640]{2,1,0:T(8,128)(2,1)}, bf16[2,640,640]{2,1,0:T(8,128)(2,1)}) custom-call(s32[4]{0:T(128)} %pad_add_fusion.spot_ref, bf16[1024,1280]{1,0:T(8,128)(2,1)} %refs_0_.1, bf16[4,2,160,640]{3,2,1,0:T(8,128)(2,1)} %bitcast.65, bf16[4,2,160,640]{3,2,1,0:T(8,128)(2,1)} %bitcast.78, ...), custom_call_target="tpu_custom_call" | custom-call | flops 8388608000 | bytes 12779520 | tf_op jit(solution)/shard_map/queries/pallas_call | solution.py:206
  176.5 2.6 %collective-permute-done.36.refs_13_ = bf16[1,2,80,640]{3,2,1,0:T(8,128)(2,1)S(1)} collective-permute-done((bf16[1,2,80,640]{3,2,1,0:T(8,128)(2,1)S(1)}, bf16[1,2,80,640]{3,2,1,0:T(8,128)(2,1)S(1)}, u32[]{:S(2)}, u32[]{:S(2)}) %collective-permute-start.36) | collective-permute-done | bytes 204832 | tf_op jit(solution)/shard_map/ppermute | solution.py:253
  181.5 18.7 %queries.3 = bf16[1024,1280]{1,0:T(8,128)(2,1)} custom-call(s32[4]{0:T(128)} %pad_add_fusion.spot_ref, bf16[352,1280]{1,0:T(8,128)(2,1)} %collective-permute-done.2.refs_0_, bf16[336,1280]{1,0:T(8,128)(2,1)} %copy-done.18, bf16[352,1280]{1,0:T(8,128)(2,1)} %copy-done.17, bf16[4,2,160,640]{3,2,1,0:T(8,128)(2,1)} %bitcast.66, ...), custom_call_target="tpu_custom_call" | custom-call | flops 8388608000 | bytes 12779520 | tf_op jit(solution)/shard_map/queries/pallas_call | solution.py:206
  (168 shorter events, 42.9 us)
Async XLA Ops:
  12.1 30.7 %collective-permute-start.3 = (bf16[2,640,640]{2,1,0:T(8,128)(2,1)}, bf16[2,640,640]{2,1,0:T(8,128)(2,1)}, u32[]{:S(2)}, u32[]{:S(2)}) collective-permute-start(bf16[2,640,640]{2,1,0:T(8,128)(2,1)} %get-tuple-element.89), channel_id=1, source_target_pairs={{0,2},{2,0},{4,6},{6,4},{8,10},{10,8},{12,14},{14,12},{16,18},{18,... | collective-permute-start | bytes 4915208 | tf_op jit(solution)/shard_map/ppermute | solution.py:253
  13.5 25.5 %collective-permute-start.2 = (bf16[352,1280]{1,0:T(8,128)(2,1)}, bf16[352,1280]{1,0:T(8,128)(2,1)}, u32[]{:S(2)}, u32[]{:S(2)}) collective-permute-start(bf16[352,1280]{1,0:T(8,128)(2,1)} %slice.33), channel_id=1, source_target_pairs={{0,1},{1,0},{2,3},{3,2},{4,5},{5,4},{6,7},{7,6},{8,9},{9,8},{10,11... | collective-permute-start | bytes 2703368 | tf_op jit(solution)/shard_map/ppermute | solution.py:256
  16.0 23.0 %collective-permute-start.5 = (bf16[640,640]{1,0:T(8,128)(2,1)}, bf16[640,640]{1,0:T(8,128)(2,1)}, u32[]{:S(2)}, u32[]{:S(2)}) collective-permute-start(bf16[640,640]{1,0:T(8,128)(2,1)} %get-tuple-element.94), channel_id=1, source_target_pairs={{0,2},{2,0},{4,6},{6,4},{8,10},{10,8},{12,14},{14,12},{16,18},{18,... | collective-permute-start | bytes 2457608 | tf_op jit(solution)/shard_map/ppermute | solution.py:253
  16.3 20.5 %collective-permute-start = (bf16[320,640]{1,0:T(8,128)(2,1)S(1)}, bf16[320,640]{1,0:T(8,128)(2,1)}, u32[]{:S(2)}, u32[]{:S(2)}) collective-permute-start(bf16[320,640]{1,0:T(8,128)(2,1)S(1)} %bitcast.55), channel_id=1, source_target_pairs={{0,8},{2,10},{4,12},{6,14},{8,0},{10,2},{12,4},{14,6},{16,24},{18,... | collective-permute-start | bytes 1228808 | tf_op jit(solution)/shard_map/ppermute | solution.py:253
  17.9 21.1 %collective-permute-start.1 = (bf16[320,640]{1,0:T(8,128)(2,1)S(1)}, bf16[320,640]{1,0:T(8,128)(2,1)S(1)}, u32[]{:S(2)}, u32[]{:S(2)}) collective-permute-start(bf16[320,640]{1,0:T(8,128)(2,1)S(1)} %bitcast.56), channel_id=1, source_target_pairs={{0,16},{2,18},{4,20},{6,22},{8,24},{10,26},{12,28},{14,30},{16,0},... | collective-permute-start | bytes 1228808 | tf_op jit(solution)/shard_map/ppermute | solution.py:253
  42.3 23.0 %collective-permute-start.6 = (bf16[480,640]{1,0:T(8,128)(2,1)}, bf16[480,640]{1,0:T(8,128)(2,1)}, u32[]{:S(2)}, u32[]{:S(2)}) collective-permute-start(bf16[480,640]{1,0:T(8,128)(2,1)} %pad_maximum_fusion.8), channel_id=1, source_target_pairs={{0,8},{2,10},{4,12},{6,14},{8,0},{10,2},{12,4},{14,6},{16,24},{18,... | collective-permute-start | bytes 1843208 | tf_op jit(solution)/shard_map/ppermute | solution.py:253
  45.2 24.3 %collective-permute-start.4 = (bf16[640,640]{1,0:T(8,128)(2,1)}, bf16[640,640]{1,0:T(8,128)(2,1)}, u32[]{:S(2)}, u32[]{:S(2)}) collective-permute-start(bf16[640,640]{1,0:T(8,128)(2,1)} %bitcast.8), channel_id=1, source_target_pairs={{0,4},{2,6},{4,0},{6,2},{8,12},{10,14},{12,8},{14,10},{16,20},{18,... | collective-permute-start | bytes 2457608 | tf_op jit(solution)/shard_map/ppermute | solution.py:253
  46.7 19.6 %collective-permute-start.8 = (bf16[160,640]{1,0:T(8,128)(2,1)}, bf16[160,640]{1,0:T(8,128)(2,1)S(1)}, u32[]{:S(2)}, u32[]{:S(2)}) collective-permute-start(bf16[160,640]{1,0:T(8,128)(2,1)} %get-tuple-element.160), channel_id=1, source_target_pairs={{0,24},{2,26},{4,28},{6,30},{8,16},{10,18},{12,20},{14,22},{16,8},... | collective-permute-start | bytes 614408 | tf_op jit(solution)/shard_map/ppermute | solution.py:253
  48.8 17.5 %collective-permute-start.7 = (bf16[160,640]{1,0:T(8,128)(2,1)}, bf16[160,640]{1,0:T(8,128)(2,1)S(1)}, u32[]{:S(2)}, u32[]{:S(2)}) collective-permute-start(bf16[160,640]{1,0:T(8,128)(2,1)} %get-tuple-element.161), channel_id=1, source_target_pairs={{0,16},{2,18},{4,20},{6,22},{8,24},{10,26},{12,28},{14,30},{16,0},... | collective-permute-start | bytes 614408 | tf_op jit(solution)/shard_map/ppermute | solution.py:253
  49.9 23.3 %collective-permute-start.9 = (bf16[336,1280]{1,0:T(8,128)(2,1)S(1)}, bf16[336,1280]{1,0:T(8,128)(2,1)S(1)}, u32[]{:S(2)}, u32[]{:S(2)}) collective-permute-start(bf16[336,1280]{1,0:T(8,128)(2,1)S(1)} %slice.36), channel_id=1, source_target_pairs={{0,1},{1,0},{2,3},{3,2},{4,5},{5,4},{6,7},{7,6},{8,9},{9,8},{10,11... | collective-permute-start | bytes 2580488 | tf_op jit(solution)/shard_map/ppermute | solution.py:256
  74.4 19.4 %collective-permute-start.10 = (bf16[720,640]{1,0:T(8,128)(2,1)}, bf16[720,640]{1,0:T(8,128)(2,1)}, u32[]{:S(2)}, u32[]{:S(2)}) collective-permute-start(bf16[720,640]{1,0:T(8,128)(2,1)} %pad_maximum_fusion.1), channel_id=1, source_target_pairs={{0,4},{2,6},{4,0},{6,2},{8,12},{10,14},{12,8},{14,10},{16,20},{18,... | collective-permute-start | bytes 2764808 | tf_op jit(solution)/shard_map/ppermute | solution.py:253
  77.3 18.8 %collective-permute-start.11 = (bf16[160,640]{1,0:T(8,128)(2,1)S(1)}, bf16[160,640]{1,0:T(8,128)(2,1)S(1)}, u32[]{:S(2)}, u32[]{:S(2)}) collective-permute-start(bf16[160,640]{1,0:T(8,128)(2,1)S(1)} %bitcast.76), channel_id=1, source_target_pairs={{0,8},{2,10},{4,12},{6,14},{8,0},{10,2},{12,4},{14,6},{16,24},{18,... | collective-permute-start | bytes 614408 | tf_op jit(solution)/shard_map/ppermute | solution.py:253
  78.5 17.6 %collective-permute-start.12 = (bf16[2,80,640]{2,1,0:T(8,128)(2,1)S(1)}, bf16[2,80,640]{2,1,0:T(8,128)(2,1)S(1)}, u32[]{:S(2)}, u32[]{:S(2)}) collective-permute-start(bf16[2,80,640]{2,1,0:T(8,128)(2,1)S(1)} %get-tuple-element.163), channel_id=1, source_target_pairs={{0,16},{2,18},{4,20},{6,22},{8,24},{10,26},{12,28},{14,30},{16,0},... | collective-permute-start | bytes 614408 | tf_op jit(solution)/shard_map/ppermute | solution.py:253
  81.8 17.7 %collective-permute-start.14 = (bf16[640,640]{1,0:T(8,128)(2,1)}, bf16[640,640]{1,0:T(8,128)(2,1)S(1)}, u32[]{:S(2)}, u32[]{:S(2)}) collective-permute-start(bf16[640,640]{1,0:T(8,128)(2,1)} %get-tuple-element.107), channel_id=1, source_target_pairs={{0,1},{1,0},{2,3},{3,2},{4,5},{5,4},{6,7},{7,6},{8,9},{9,8},{10,11... | collective-permute-start | bytes 2457608 | tf_op jit(solution)/shard_map/ppermute | solution.py:256
  99.5 22.9 %collective-permute-start.18 = (bf16[720,640]{1,0:T(8,128)(2,1)S(1)}, bf16[720,640]{1,0:T(8,128)(2,1)S(1)}, u32[]{:S(2)}, u32[]{:S(2)}) collective-permute-start(bf16[720,640]{1,0:T(8,128)(2,1)S(1)} %pad_maximum_fusion.2), channel_id=1, source_target_pairs={{0,4},{2,6},{4,0},{6,2},{8,12},{10,14},{12,8},{14,10},{16,20},{18,... | collective-permute-start | bytes 2764808 | tf_op jit(solution)/shard_map/ppermute | solution.py:253
  100.6 21.9 %collective-permute-start.19 = (bf16[352,1280]{1,0:T(8,128)(2,1)S(1)}, bf16[352,1280]{1,0:T(8,128)(2,1)S(1)}, u32[]{:S(2)}, u32[]{:S(2)}) collective-permute-start(bf16[352,1280]{1,0:T(8,128)(2,1)S(1)} %pad_maximum_fusion.4), channel_id=1, source_target_pairs={{0,1},{1,0},{2,3},{3,2},{4,5},{5,4},{6,7},{7,6},{8,9},{9,8},{10,11... | collective-permute-start | bytes 2703368 | tf_op jit(solution)/shard_map/ppermute | solution.py:256
  122.6 21.4 %collective-permute-start.21 = (bf16[720,640]{1,0:T(8,128)(2,1)S(1)}, bf16[720,640]{1,0:T(8,128)(2,1)S(1)}, u32[]{:S(2)}, u32[]{:S(2)}) collective-permute-start(bf16[720,640]{1,0:T(8,128)(2,1)S(1)} %pad_maximum_fusion.3), channel_id=1, source_target_pairs={{0,4},{2,6},{4,0},{6,2},{8,12},{10,14},{12,8},{14,10},{16,20},{18,... | collective-permute-start | bytes 2764808 | tf_op jit(solution)/shard_map/ppermute | solution.py:253
  123.9 20.2 %collective-permute-start.25 = (bf16[4,2,80,640]{3,2,1,0:T(8,128)(2,1)S(1)}, bf16[4,2,80,640]{3,2,1,0:T(8,128)(2,1)}, u32[]{:S(2)}, u32[]{:S(2)}) collective-permute-start(bf16[4,2,80,640]{3,2,1,0:T(8,128)(2,1)S(1)} %pad_maximum_fusion.6), channel_id=1, source_target_pairs={{0,1},{1,0},{2,3},{3,2},{4,5},{5,4},{6,7},{7,6},{8,9},{9,8},{10,11... | collective-permute-start | bytes 2457608 | tf_op jit(solution)/shard_map/ppermute | solution.py:256
  124.3 19.8 %collective-permute-start.22 = (bf16[160,640]{1,0:T(8,128)(2,1)S(1)}, bf16[160,640]{1,0:T(8,128)(2,1)S(1)}, u32[]{:S(2)}, u32[]{:S(2)}) collective-permute-start(bf16[160,640]{1,0:T(8,128)(2,1)S(1)} %bitcast.60), channel_id=1, source_target_pairs={{0,8},{2,10},{4,12},{6,14},{8,0},{10,2},{12,4},{14,6},{16,24},{18,... | collective-permute-start | bytes 614408 | tf_op jit(solution)/shard_map/ppermute | solution.py:253
  149.8 25.6 %collective-permute-start.33 = (bf16[1280,640]{1,0:T(8,128)(2,1)S(1)}, bf16[1280,640]{1,0:T(8,128)(2,1)S(1)}, u32[]{:S(2)}, u32[]{:S(2)}) collective-permute-start(bf16[1280,640]{1,0:T(8,128)(2,1)S(1)} %constant_dynamic-update-slice_fusion.4), channel_id=1, source_target_pairs={{0,2},{2,0},{4,6},{6,4},{8,10},{10,8},{12,14},{14,12},{16,18},{18,... | collective-permute-start | bytes 4915208 | tf_op jit(solution)/shard_map/ppermute | solution.py:253
  151.0 24.3 %collective-permute-start.26 = (bf16[640,640]{1,0:T(8,128)(2,1)}, bf16[640,640]{1,0:T(8,128)(2,1)S(1)}, u32[]{:S(2)}, u32[]{:S(2)}) collective-permute-start(bf16[640,640]{1,0:T(8,128)(2,1)} %bitcast.23), channel_id=1, source_target_pairs={{0,4},{2,6},{4,0},{6,2},{8,12},{10,14},{12,8},{14,10},{16,20},{18,... | collective-permute-start | bytes 2457608 | tf_op jit(solution)/shard_map/ppermute | solution.py:253
  152.3 23.0 %collective-permute-start.28 = (bf16[2,80,640]{2,1,0:T(8,128)(2,1)S(1)}, bf16[2,80,640]{2,1,0:T(8,128)(2,1)S(1)}, u32[]{:S(2)}, u32[]{:S(2)}) collective-permute-start(bf16[2,80,640]{2,1,0:T(8,128)(2,1)S(1)} %get-tuple-element.166), channel_id=1, source_target_pairs={{0,16},{2,18},{4,20},{6,22},{8,24},{10,26},{12,28},{14,30},{16,0},... | collective-permute-start | bytes 614408 | tf_op jit(solution)/shard_map/ppermute | solution.py:253
  154.3 21.0 %collective-permute-start.29 = (bf16[2,80,640]{2,1,0:T(8,128)(2,1)S(1)}, bf16[2,80,640]{2,1,0:T(8,128)(2,1)S(1)}, u32[]{:S(2)}, u32[]{:S(2)}) collective-permute-start(bf16[2,80,640]{2,1,0:T(8,128)(2,1)S(1)} %get-tuple-element.166), channel_id=1, source_target_pairs={{0,24},{2,26},{4,28},{6,30},{8,16},{10,18},{12,20},{14,22},{16,8},... | collective-permute-start | bytes 614408 | tf_op jit(solution)/shard_map/ppermute | solution.py:253
  155.7 19.5 %collective-permute-start.27 = (bf16[160,640]{1,0:T(8,128)(2,1)S(1)}, bf16[160,640]{1,0:T(8,128)(2,1)S(1)}, u32[]{:S(2)}, u32[]{:S(2)}) collective-permute-start(bf16[160,640]{1,0:T(8,128)(2,1)S(1)} %bitcast.74), channel_id=1, source_target_pairs={{0,8},{2,10},{4,12},{6,14},{8,0},{10,2},{12,4},{14,6},{16,24},{18,... | collective-permute-start | bytes 614408 | tf_op jit(solution)/shard_map/ppermute | solution.py:253
  (49 other events, 345.9 us)
